TPU v7x, 32 devices: a whole 2x2x4 slice. The times are simulated.
32 devices in a mesh: dp: 32 (over z, y, x, core).
Axes of the slice: x: 2, y: 2, z: 4, core: 2. Of those that a mesh axis runs over, the one named last changes fastest.
Arguments:
- visual: bfloat16 [32, 512, 768], P('dp'), may hold values from -40 to 40
- text: bfloat16 [32, 512, 768], P('dp'), may hold values from -6 to 6
- lengths: int32 [32], P('dp'), may hold values from 20 to 512, as said below
- text_boxes: int32 [32, 2, 512], P('dp'), may hold values from 0 to 127
- cot_visual: bfloat16 [32, 512, 768], P('dp'), may hold values from -6 to 6
- cot_text: bfloat16 [32, 512, 768], P('dp'), may hold values from -6 to 6
- attn_w: float32 [2, 4, 768, 768], P(None, None, 'dp'), may hold values from -4 to 4
- ffn_in: float32 [2, 768, 3072], P(None, 'dp'), may hold values from -0.21875 to 0.21875
- ffn_out: float32 [2, 3072, 768], P(None, 'dp'), may hold values from -0.109375 to 0.109375
- bias_in: float32 [2, 3072], P(None, 'dp'), may hold values from -4 to 4
- vectors: float32 [12, 768], P(None, 'dp'), may hold values from -2 to 2
- pos_tables: float32 [2, 3, 12, 128], P(None, None, None, 'dp'), may hold values from -3 to 3
- spatial: float32 [2, 128, 768], P(None, 'dp'), may hold values from -3 to 3
- attn_mom: float32 [2, 4, 768, 768], P(None, None, 'dp'), may hold values from -1 to 1
- attn_sec: float32 [2, 4, 768, 768], P(None, None, 'dp'), may hold values from 0 to 1, as said below
- in_mom: float32 [2, 768, 3072], P(None, 'dp'), may hold values from -1 to 1
- in_sec: float32 [2, 768, 3072], P(None, 'dp'), may hold values from 0 to 1, as said below
- out_mom: float32 [2, 3072, 768], P(None, 'dp'), may hold values from -1 to 1
- out_sec: float32 [2, 3072, 768], P(None, 'dp'), may hold values from 0 to 1, as said below
- bias_mom: float32 [2, 3072], P(None, 'dp'), may hold values from -1 to 1
- bias_sec: float32 [2, 3072], P(None, 'dp'), may hold values from 0 to 1, as said below
- vec_mom: float32 [12, 768], P(None, 'dp'), may hold values from -1 to 1
- vec_sec: float32 [12, 768], P(None, 'dp'), may hold values from 0 to 1, as said below
- pos_mom: float32 [2, 3, 12, 128], P(None, None, None, 'dp'), may hold values from -1 to 1
- pos_sec: float32 [2, 3, 12, 128], P(None, None, None, 'dp'), may hold values from 0 to 1, as said below
- spatial_mom: float32 [2, 128, 768], P(None, 'dp'), may hold values from -1 to 1
- spatial_sec: float32 [2, 128, 768], P(None, 'dp'), may hold values from 0 to 1, as said below
Outputs:
- out_visual: bfloat16 [32, 512, 768], P('dp')
- out_text: bfloat16 [32, 512, 768], P('dp')
- grad_visual: float32 [32, 512, 768], P('dp')
- grad_text: float32 [32, 512, 768], P('dp')
- grad_norm: float32 [], replicated
- attn_mom_new: float32 [2, 4, 768, 768], P(None, None, 'dp')
- attn_sec_new: float32 [2, 4, 768, 768], P(None, None, 'dp')
- attn_new: float32 [2, 4, 768, 768], P(None, None, 'dp')
- attn_copy: bfloat16 [2, 4, 768, 768], P(None, None, 'dp')
- in_mom_new: float32 [2, 768, 3072], P(None, 'dp')
- in_sec_new: float32 [2, 768, 3072], P(None, 'dp')
- in_new: float32 [2, 768, 3072], P(None, 'dp')
- in_copy: bfloat16 [2, 768, 3072], P(None, 'dp')
- out_mom_new: float32 [2, 3072, 768], P(None, 'dp')
- out_sec_new: float32 [2, 3072, 768], P(None, 'dp')
- out_new: float32 [2, 3072, 768], P(None, 'dp')
- out_copy: bfloat16 [2, 3072, 768], P(None, 'dp')
- bias_mom_new: float32 [2, 3072], P(None, 'dp')
- bias_sec_new: float32 [2, 3072], P(None, 'dp')
- bias_new: float32 [2, 3072], P(None, 'dp')
- vec_mom_new: float32 [12, 768], P(None, 'dp')
- vec_sec_new: float32 [12, 768], P(None, 'dp')
- vec_new: float32 [12, 768], P(None, 'dp')
- pos_mom_new: float32 [2, 3, 12, 128], P(None, None, None, 'dp')
- pos_sec_new: float32 [2, 3, 12, 128], P(None, None, None, 'dp')
- pos_new: float32 [2, 3, 12, 128], P(None, None, None, 'dp')
- spatial_mom_new: float32 [2, 128, 768], P(None, 'dp')
- spatial_sec_new: float32 [2, 128, 768], P(None, 'dp')
- spatial_new: float32 [2, 128, 768], P(None, 'dp')
Inputs may be any that keep to these rules, and one draw needn't show every extreme that they name: `lengths`: at least one page has 512 text tokens. `attn_sec`: positive. `in_sec`: positive. `out_sec`: positive. `bias_sec`: positive. `vec_sec`: positive. `pos_sec`: positive. `spatial_sec`: positive.
All inputs are finite; a program needn't handle non-finite values.
Results may differ from a plain program's by a relative error of at most 0.015.
The roundings to bfloat16 on the way count: a program that leaves them out, or rounds other values in their place, can miss the bound.
Values may be sent and summed in bfloat16 or wider, within the bound.
No kernel may reach another device: no remote copies, remote signals or barrier semaphores. Data moves between devices by JAX's collectives and lax.ppermute only.
A program may use at most 256 MiB of HBM per device.

v0:
```python
import jax
import jax.numpy as jnp
from jax import lax
from jax.sharding import PartitionSpec as P

H = 12
HD = 64
VROWS = 16
VCOLS = 32
NB = 128
NR = 128
STEP = 10


HIGH = lax.Precision.HIGHEST
EPSILON = 1e-05
NEGATIVE = -1000000000.0
CLIP = 1.0
BETA_ONE = 0.9
BETA_TWO = 0.95
ADAM_EPS = 1e-08
DECAY = 0.1
RATE_ATTN = 0.15
RATE_FEED = 0.04
RATE_OTHER = 0.2


def matmul(left, right):
    return jnp.dot(left, right, preferred_element_type=jnp.float32)


def layer_norm(rows, gain, shift):
    center = rows - jnp.mean(rows, axis=-1, keepdims=True)
    spread = jnp.mean(center * center, axis=-1, keepdims=True)
    return center * lax.rsqrt(spread + EPSILON) * gain + shift


def gelu_exact(values):
    return jax.nn.gelu(values, approximate=False)


def toeplitz(table, width):
    half = NR // 2
    heads = table.shape[0]
    before = max(0, width - 1 - half)
    after = max(0, width - half)
    begin = max(-half, 1 - width) + half
    finish = min(half - 1, width - 1) + half + 1
    pieces = [
        jnp.broadcast_to(table[:, :1], (heads, before)),
        table,
        jnp.broadcast_to(table[:, -1:], (heads, after)),
        jnp.zeros((heads, 1), table.dtype),
    ]
    padded = jnp.concatenate(pieces, axis=1)
    tiled = jnp.tile(padded, (1, width))[:, : width * (2 * width - 1)]
    return tiled.reshape(heads, width, 2 * width - 1)[:, :, width - 1 :]


def one_hot(index, dtype):
    return (index[..., None] == jnp.arange(NB)).astype(dtype)


def spatial_left(tables, onehot_x, onehot_y):
    block_x = toeplitz(tables[0], NB)
    block_y = toeplitz(tables[1], NB)
    left_x = jnp.einsum(
        "qia,hab->qhib", onehot_x, block_x, preferred_element_type=jnp.float32, precision=HIGH
    )
    left_y = jnp.einsum(
        "qia,hab->qhib", onehot_y, block_y, preferred_element_type=jnp.float32, precision=HIGH
    )
    return jnp.concatenate([left_x, left_y], axis=-1)


def make_bias(tables, onehot_x, onehot_y, count):
    line = toeplitz(tables[0], count).astype(jnp.float32)
    left = spatial_left(tables[1:], onehot_x, onehot_y).astype(jnp.bfloat16)
    both = jnp.concatenate([onehot_x, onehot_y], axis=-1)
    plane = jnp.einsum("qhik,qjk->qhij", left, both, preferred_element_type=jnp.float32)
    return line[None] + plane


def table_grads(tables, onehot_x, onehot_y, grad_scores, count):
    pages = grad_scores.shape[0]
    grad_line = jnp.sum(grad_scores.astype(jnp.float32), axis=0)
    both = jnp.concatenate([onehot_x, onehot_y], axis=-1)
    grad_left = jnp.einsum("phij,pjk->phik", grad_scores, both, preferred_element_type=jnp.float32)
    wide_x = onehot_x.astype(jnp.float32)
    wide_y = onehot_y.astype(jnp.float32)
    plane_back = jax.vjp(lambda part: spatial_left(part, wide_x, wide_y), tables[1:])[1]
    line_back = jax.vjp(lambda part: toeplitz(part, count), tables[0])[1]
    grad_plane = plane_back(grad_left)[0]
    grad_first = line_back(grad_line)[0]
    return jnp.concatenate([grad_first[None], grad_plane], axis=0)


def embed(onehot_x, onehot_y, table):
    both = jnp.concatenate([onehot_x, onehot_y], axis=-1)
    flat = matmul(both.reshape(-1, 2 * NB), table.reshape(2 * NB, table.shape[2]))
    return flat.reshape(both.shape[0], both.shape[1], table.shape[2])


def scores_of(queries, key_rows, bias, keep):
    scores = (
        jnp.einsum("pihd,pjhd->phij", queries, key_rows, preferred_element_type=jnp.float32)
        * HD ** (-0.5)
        + bias
    )
    return jnp.where(keep[:, None, None, :], scores, NEGATIVE)


def attend(inputs, place, weights, bias, keep):
    pages, count, width = inputs.shape
    joint = (inputs + place).astype(jnp.bfloat16).reshape(pages * count, width)
    plain = inputs.astype(jnp.bfloat16).reshape(pages * count, width)
    shaped = (pages, count, H, HD)
    queries = matmul(joint, weights[0]).astype(jnp.bfloat16).reshape(shaped)
    key_rows = matmul(joint, weights[1]).astype(jnp.bfloat16).reshape(shaped)
    values = matmul(plain, weights[2]).astype(jnp.bfloat16).reshape(shaped)
    scores = scores_of(queries, key_rows, bias, keep)
    highest = jnp.max(scores, axis=-1, keepdims=True)
    raised = jnp.exp(scores - highest)
    totals = jnp.sum(raised, axis=-1, keepdims=True)
    probs = (raised / totals).astype(jnp.bfloat16)
    log_total = highest + jnp.log(totals)
    mixed = jnp.einsum("phij,pjhd->pihd", probs, values, preferred_element_type=jnp.float32)
    mixed = mixed.reshape(pages * count, width).astype(jnp.bfloat16)
    output = matmul(mixed, weights[3]).reshape(pages, count, width)
    return (output, (joint, plain, queries, key_rows, values, log_total, mixed))


def attend_back(grad_output, weights, bias, keep, saved):
    joint, plain, queries, key_rows, values, log_total, mixed = saved
    pages, count, heads, size = queries.shape
    width = heads * size
    grad_rows = grad_output.reshape(pages * count, width)
    grad_last = matmul(mixed.T, grad_rows)
    grad_mixed = matmul(grad_rows, weights[3].T).astype(jnp.bfloat16).reshape(queries.shape)
    scores = scores_of(queries, key_rows, bias, keep)
    probs = jnp.exp(scores - log_total)
    grad_probs = jnp.einsum(
        "pihd,pjhd->phij", grad_mixed, values, preferred_element_type=jnp.float32
    )
    inner = jnp.sum(probs * grad_probs, axis=-1, keepdims=True)
    grad_scores = (probs * (grad_probs - inner)).astype(jnp.bfloat16)
    grad_values = jnp.einsum(
        "phij,pihd->pjhd",
        probs.astype(jnp.bfloat16),
        grad_mixed,
        preferred_element_type=jnp.float32,
    )
    grad_values = grad_values.astype(jnp.bfloat16).reshape(pages * count, width)
    grad_queries = jnp.einsum(
        "phij,pjhd->pihd", grad_scores, key_rows, preferred_element_type=jnp.float32
    ) * HD ** (-0.5)
    grad_queries = grad_queries.astype(jnp.bfloat16).reshape(pages * count, width)
    grad_keys = jnp.einsum(
        "phij,pihd->pjhd", grad_scores, queries, preferred_element_type=jnp.float32
    ) * HD ** (-0.5)
    grad_keys = grad_keys.astype(jnp.bfloat16).reshape(pages * count, width)
    grad_weights = jnp.stack(
        [
            matmul(joint.T, grad_queries),
            matmul(joint.T, grad_keys),
            matmul(plain.T, grad_values),
            grad_last,
        ]
    )
    grad_joint = (matmul(grad_queries, weights[0].T) + matmul(grad_keys, weights[1].T)).reshape(
        pages, count, width
    )
    grad_plain = matmul(grad_values, weights[2].T).reshape(pages, count, width)
    return (grad_weights, grad_joint, grad_plain, grad_scores)


def feed_forward(rows, first, first_bias, second, second_bias):
    hidden_in = rows.reshape(-1, rows.shape[2]).astype(jnp.bfloat16)
    before = matmul(hidden_in, first) + first_bias
    active, gelu_back = jax.vjp(gelu_exact, before)
    active_low = active.astype(jnp.bfloat16)
    output = (matmul(active_low, second) + second_bias).reshape(rows.shape)
    return (output, (hidden_in, gelu_back, active_low))


def feed_back(grad_rows, first, second, saved):
    hidden_in, gelu_back, active_low = saved
    grad_low = grad_rows.reshape(-1, grad_rows.shape[2]).astype(jnp.bfloat16)
    grad_second = matmul(active_low.T, grad_low)
    grad_second_bias = jnp.sum(grad_low.astype(jnp.float32), axis=0)
    grad_active = matmul(grad_low, second.T)
    grad_before = gelu_back(grad_active)[0].astype(jnp.bfloat16)
    grad_first = matmul(hidden_in.T, grad_before)
    grad_first_bias = jnp.sum(grad_before.astype(jnp.float32), axis=0)
    grad_in = matmul(grad_before, first.T).reshape(grad_rows.shape)
    return (grad_in, grad_first, grad_first_bias, grad_second, grad_second_bias)


def adam(weight, grad, first, second, rate, decay):
    first_new = BETA_ONE * first + (1 - BETA_ONE) * grad
    second_new = BETA_TWO * second + (1 - BETA_TWO) * grad * grad
    ratio = (
        first_new / (1 - BETA_ONE**STEP) / (jnp.sqrt(second_new / (1 - BETA_TWO**STEP)) + ADAM_EPS)
    )
    return (first_new, second_new, weight - rate * (ratio + decay * weight))


def body(
    visual,
    text,
    lengths,
    text_boxes,
    cot_visual,
    cot_text,
    attn_w,
    ffn_in,
    ffn_out,
    bias_in,
    vectors,
    pos_tables,
    spatial,
    attn_mom,
    attn_sec,
    in_mom,
    in_sec,
    out_mom,
    out_sec,
    bias_mom,
    bias_sec,
    vec_mom,
    vec_sec,
    pos_mom,
    pos_sec,
    spatial_mom,
    spatial_sec,
):
    wide_attn, wide_in, wide_out, wide_pos, wide_spatial = (
        lax.all_gather(attn_w.astype(jnp.bfloat16), "dp", axis=2, tiled=True),
        lax.all_gather(ffn_in.astype(jnp.bfloat16), "dp", axis=1, tiled=True),
        lax.all_gather(ffn_out.astype(jnp.bfloat16), "dp", axis=1, tiled=True),
        lax.all_gather(pos_tables.astype(jnp.bfloat16), "dp", axis=3, tiled=True),
        lax.all_gather(spatial.astype(jnp.bfloat16), "dp", axis=1, tiled=True),
    )
    wide_vec, wide_bias = (
        lax.all_gather(vectors, "dp", axis=1, tiled=True),
        lax.all_gather(bias_in, "dp", axis=1, tiled=True),
    )
    pages, count, width = visual.shape
    devices = lax.axis_size("dp")
    raw = visual.astype(jnp.float32)
    sums = lax.psum((jnp.sum(raw, axis=(0, 1)), jnp.sum(raw * raw, axis=(0, 1))), "dp")
    total = pages * count * devices
    mean = sums[0] / total
    variance = sums[1] / total - mean * mean
    inverse = lax.rsqrt(variance + EPSILON)
    normed = (raw - mean) * inverse
    visual_in = normed * wide_vec[0] + wide_vec[1]
    text_in = text.astype(jnp.float32)
    position = jnp.arange(count)
    keep_text = position[None, :] < lengths[:, None]
    keep_all = jnp.ones((pages, count), bool)
    text_mask = keep_text.astype(jnp.float32)[..., None]
    grid_x = position % VCOLS * (NB // VCOLS) + NB // VCOLS // 2
    grid_y = position // VCOLS * (NB // VROWS) + NB // VROWS // 2
    vis_x = one_hot(grid_x, jnp.bfloat16)[None]
    vis_y = one_hot(grid_y, jnp.bfloat16)[None]
    txt_x = one_hot(text_boxes[:, 0, :], jnp.bfloat16)
    txt_y = one_hot(text_boxes[:, 1, :], jnp.bfloat16)
    vis_place = embed(vis_x, vis_y, wide_spatial)
    txt_place = embed(txt_x, txt_y, wide_spatial)
    vis_bias = make_bias(wide_pos[0], vis_x, vis_y, count)
    txt_bias = make_bias(wide_pos[1], txt_x, txt_y, count)
    vis_att, vis_saved = attend(visual_in, vis_place, wide_attn[0], vis_bias, keep_all)
    txt_att, txt_saved = attend(text_in, txt_place, wide_attn[1], txt_bias, keep_text)
    merged = vis_att + text_mask * txt_att
    vis_u, vis_first_back = jax.vjp(layer_norm, visual_in + merged, wide_vec[2], wide_vec[3])
    txt_u, txt_first_back = jax.vjp(layer_norm, text_in + merged, wide_vec[4], wide_vec[5])
    vis_ff, vis_ff_saved = feed_forward(vis_u, wide_in[0], wide_bias[0], wide_out[0], wide_vec[10])
    txt_ff, txt_ff_saved = feed_forward(txt_u, wide_in[1], wide_bias[1], wide_out[1], wide_vec[11])
    vis_out, vis_second_back = jax.vjp(layer_norm, vis_u + vis_ff, wide_vec[6], wide_vec[7])
    txt_out, txt_second_back = jax.vjp(layer_norm, txt_u + txt_ff, wide_vec[8], wide_vec[9])
    out_visual = vis_out.astype(jnp.bfloat16)
    out_text = (txt_out * text_mask).astype(jnp.bfloat16)
    back_attn, back_in, back_out = (
        lax.all_gather(attn_w.astype(jnp.bfloat16), "dp", axis=2, tiled=True),
        lax.all_gather(ffn_in.astype(jnp.bfloat16), "dp", axis=1, tiled=True),
        lax.all_gather(ffn_out.astype(jnp.bfloat16), "dp", axis=1, tiled=True),
    )
    vis_pre_two, vis_gain_two, vis_shift_two = vis_second_back(cot_visual.astype(jnp.float32))
    txt_pre_two, txt_gain_two, txt_shift_two = txt_second_back(
        cot_text.astype(jnp.float32) * text_mask
    )
    vis_ff_in, vis_first, vis_first_bias, vis_second, vis_second_bias = feed_back(
        vis_pre_two, back_in[0], back_out[0], vis_ff_saved
    )
    txt_ff_in, txt_first, txt_first_bias, txt_second, txt_second_bias = feed_back(
        txt_pre_two, back_in[1], back_out[1], txt_ff_saved
    )
    grad_bias = jnp.stack([vis_first_bias, txt_first_bias])
    grad_in = jnp.stack([vis_first, txt_first])
    grad_out = jnp.stack([vis_second, txt_second])
    vis_pre_one, vis_gain_one, vis_shift_one = vis_first_back(vis_pre_two + vis_ff_in)
    txt_pre_one, txt_gain_one, txt_shift_one = txt_first_back(txt_pre_two + txt_ff_in)
    grad_merged = vis_pre_one + txt_pre_one
    vis_attn_grad, vis_joint, vis_plain, vis_scores = attend_back(
        grad_merged.astype(jnp.bfloat16), back_attn[0], vis_bias, keep_all, vis_saved
    )
    txt_attn_grad, txt_joint, txt_plain, txt_scores = attend_back(
        (grad_merged * text_mask).astype(jnp.bfloat16), back_attn[1], txt_bias, keep_text, txt_saved
    )
    vis_both = jnp.concatenate([vis_x, vis_y], axis=-1).reshape(-1, 2 * NB)
    txt_both = jnp.concatenate([txt_x, txt_y], axis=-1).reshape(-1, 2 * NB)
    grad_spatial = matmul(vis_both.T, vis_joint.astype(jnp.bfloat16).reshape(-1, width))
    grad_spatial = grad_spatial + matmul(
        txt_both.T, txt_joint.astype(jnp.bfloat16).reshape(-1, width)
    )
    grad_spatial = grad_spatial.reshape(2, NB, width)
    vis_tables = table_grads(wide_pos[0].astype(jnp.float32), vis_x, vis_y, vis_scores, count)
    txt_tables = table_grads(wide_pos[1].astype(jnp.float32), txt_x, txt_y, txt_scores, count)
    grad_pos = jnp.stack([vis_tables, txt_tables])
    grad_text = txt_pre_one + txt_joint + txt_plain
    vis_grad_in = vis_pre_one + vis_joint + vis_plain
    local_shift = jnp.sum(vis_grad_in, axis=(0, 1))
    local_gain = jnp.sum(vis_grad_in * normed, axis=(0, 1))
    grad_visual = vis_grad_in * wide_vec[0] * inverse
    grad_vec = jnp.stack(
        [
            local_gain,
            local_shift,
            vis_gain_one,
            vis_shift_one,
            txt_gain_one,
            txt_shift_one,
            vis_gain_two,
            vis_shift_two,
            txt_gain_two,
            txt_shift_two,
            vis_second_bias,
            txt_second_bias,
        ]
    )
    grad_attn = jnp.stack([vis_attn_grad, txt_attn_grad])
    reduced = (
        lax.psum_scatter(grad_attn, "dp", scatter_dimension=2, tiled=True),
        lax.psum_scatter(grad_in, "dp", scatter_dimension=1, tiled=True),
        lax.psum_scatter(grad_out, "dp", scatter_dimension=1, tiled=True),
        lax.psum_scatter(grad_bias, "dp", scatter_dimension=1, tiled=True),
        lax.psum_scatter(grad_vec, "dp", scatter_dimension=1, tiled=True),
        lax.psum_scatter(grad_pos, "dp", scatter_dimension=3, tiled=True),
        lax.psum_scatter(grad_spatial, "dp", scatter_dimension=1, tiled=True),
    )
    squares = jnp.float32(0.0)
    for grad in reduced:
        squares = squares + jnp.sum(grad * grad)
    grad_norm = jnp.sqrt(lax.psum(squares, "dp"))
    factor = CLIP / jnp.maximum(grad_norm, CLIP)
    params = (attn_w, ffn_in, ffn_out, bias_in, vectors, pos_tables, spatial)
    states = (
        (attn_mom, attn_sec),
        (in_mom, in_sec),
        (out_mom, out_sec),
        (bias_mom, bias_sec),
        (vec_mom, vec_sec),
        (pos_mom, pos_sec),
        (spatial_mom, spatial_sec),
    )
    rates = (RATE_ATTN, RATE_FEED, RATE_FEED, RATE_OTHER, RATE_OTHER, RATE_OTHER, RATE_OTHER)
    decays = (DECAY, DECAY, DECAY, 0.0, 0.0, 0.0, DECAY)
    results = []
    for weight, grad, state, rate, decay in zip(params, reduced, states, rates, decays):
        results.append(adam(weight, grad * factor, state[0], state[1], rate, decay))
    return (
        out_visual,
        out_text,
        grad_visual,
        grad_text,
        grad_norm,
        results[0][0],
        results[0][1],
        results[0][2],
        results[0][2].astype(jnp.bfloat16),
        results[1][0],
        results[1][1],
        results[1][2],
        results[1][2].astype(jnp.bfloat16),
        results[2][0],
        results[2][1],
        results[2][2],
        results[2][2].astype(jnp.bfloat16),
        results[3][0],
        results[3][1],
        results[3][2],
        results[4][0],
        results[4][1],
        results[4][2],
        results[5][0],
        results[5][1],
        results[5][2],
        results[6][0],
        results[6][1],
        results[6][2],
    )


def solution(mesh):
    in_specs = (
        P("dp", None, None),
        P("dp", None, None),
        P("dp"),
        P("dp", None, None),
        P("dp", None, None),
        P("dp", None, None),
        P(None, None, "dp", None),
        P(None, "dp", None),
        P(None, "dp", None),
        P(None, "dp"),
        P(None, "dp"),
        P(None, None, None, "dp"),
        P(None, "dp", None),
        P(None, None, "dp", None),
        P(None, None, "dp", None),
        P(None, "dp", None),
        P(None, "dp", None),
        P(None, "dp", None),
        P(None, "dp", None),
        P(None, "dp"),
        P(None, "dp"),
        P(None, "dp"),
        P(None, "dp"),
        P(None, None, None, "dp"),
        P(None, None, None, "dp"),
        P(None, "dp", None),
        P(None, "dp", None),
    )
    out_specs = (
        P("dp", None, None),
        P("dp", None, None),
        P("dp", None, None),
        P("dp", None, None),
        P(),
        P(None, None, "dp", None),
        P(None, None, "dp", None),
        P(None, None, "dp", None),
        P(None, None, "dp", None),
        P(None, "dp", None),
        P(None, "dp", None),
        P(None, "dp", None),
        P(None, "dp", None),
        P(None, "dp", None),
        P(None, "dp", None),
        P(None, "dp", None),
        P(None, "dp", None),
        P(None, "dp"),
        P(None, "dp"),
        P(None, "dp"),
        P(None, "dp"),
        P(None, "dp"),
        P(None, "dp"),
        P(None, None, None, "dp"),
        P(None, None, None, "dp"),
        P(None, None, None, "dp"),
        P(None, "dp", None),
        P(None, "dp", None),
        P(None, "dp", None),
    )
    return jax.shard_map(body, mesh=mesh, in_specs=in_specs, out_specs=out_specs, check_vma=False)
```

profile of v0, /device:TPU:0, one launch (start us, length us, event | category | flops | bytes accessed | tf_op | source)
XLA Modules:
  0.0 2044.1 jit_solution(1362478586895888588)
XLA Ops:
  13.0 44.5 %all-gather = f32[32,24,12]{1,2,0:T(8,128)S(1)} all-gather(f32[1,24,12]{1,2,0:T(8,128)} %bitcast.599), channel_id=1, replica_groups=mesh['dp'=32] {'dp'}, dimensions={0}, use_global_device_ids=true | all-gather | bytes 38016 | tf_op jit(solution)/shard_map/all_gather | solution.py:245
  58.5 37.2 %all-gather.1 = f32[32,96,2]{1,2,0:T(2,128)S(1)} all-gather(f32[1,96,2]{1,2,0:T(2,128)} %bitcast.606), channel_id=1, replica_groups=mesh['dp'=32] {'dp'}, dimensions={0}, use_global_device_ids=true | all-gather | bytes 25344 | tf_op jit(solution)/shard_map/all_gather | solution.py:246
  98.2 39.0 %all_gather.27 = bf16[2,3,12,128]{2,0,1,3:T(2,128)(2,1)S(1)} all-gather(bf16[2,3,12,4]{2,0,1,3:T(2,128)(2,1)S(1)} %copy.452), channel_id=1, replica_groups=mesh['dp'=32] {'dp'}, dimensions={3}, use_global_device_ids=true | all-gather | bytes 19008 | tf_op jit(solution)/shard_map/all_gather | solution.py:241
  159.9 29.2 %copy.437 = bf16[2,8,512,1024]{3,1,2,0:T(8,128)(2,1)S(1)} copy(bf16[2,8,512,1024]{3,2,1,0:T(8,128)(2,1)S(1)} %bitcast.520) | data formatting | bytes 33554432
  189.1 6.6 slice.293
  195.7 44.5 %reshape.1278 = bf16[12,512,1023]{2,1,0:T(8,128)(2,1)} reshape(bf16[12,523776]{1,0:T(8,128)(2,1)} %slice.293) | data formatting | bytes 25141248 | tf_op jit(solution)/shard_map/reshape | solution.py:57
  240.2 9.8 slice.294
  250.0 8.7 copy.420
  258.7 38.6 %all_gather.26 = bf16[2,128,768]{2,0,1:T(2,128)(2,1)S(1)} all-gather(bf16[2,4,768]{2,0,1:T(2,128)(2,1)S(1)} %copy.451), channel_id=1, replica_groups=mesh['dp'=32] {'dp'}, dimensions={1}, use_global_device_ids=true | all-gather | bytes 405504 | tf_op jit(solution)/shard_map/all_gather | solution.py:242
  318.2 29.2 %copy.440 = bf16[2,8,512,1024]{3,1,2,0:T(8,128)(2,1)S(1)} copy(bf16[2,8,512,1024]{3,2,1,0:T(8,128)(2,1)S(1)} %bitcast.521) | data formatting | bytes 33554432
  347.4 6.6 slice.312
  354.0 36.5 %reshape.1289 = bf16[12,512,1023]{2,1,0:T(8,128)(2,1)} reshape(bf16[12,523776]{1,0:T(8,128)(2,1)} %slice.312) | data formatting | bytes 25141248 | tf_op jit(solution)/shard_map/reshape | solution.py:57
  390.5 9.7 slice.313
  400.3 8.7 copy.426
  410.7 37.1 %all-reduce.32 = (f32[768]{0:T(1024)S(1)}, f32[768]{0:T(1024)S(1)}) all-reduce(f32[768]{0:T(1024)S(1)} %get-tuple-element.44, f32[768]{0:T(1024)S(1)} %get-tuple-element.43), channel_id=1, replica_groups=mesh['dp'=32] {'dp'}, use_global_device_ids=true, to_apply=%region_3.0 | all-reduce | flops 1536 | bytes 12288 | tf_op jit(solution)/shard_map/psum | solution.py:251
  497.2 9.5 fusion.201
  523.6 8.8 fusion.202
  544.2 19.9 multiply_convert_fusion.3
  572.3 18.8 multiply_convert_fusion.2
  601.4 9.5 convert_reduce_fusion.1
  617.0 9.3 convert_reduce_fusion
  635.6 7.7 fusion.63
  643.2 9.0 multiply_reduce_fusion.1
  652.3 6.9 multiply_convert_fusion.1
  669.4 10.5 multiply_reduce_fusion
  682.0 7.3 multiply_convert_fusion
  725.6 8.7 copy.434
  734.3 10.6 pad.102.clone
  744.8 34.5 %reshape.1319 = bf16[12,523776]{1,0:T(8,128)(2,1)} reshape(bf16[12,512,1023]{2,1,0:T(8,128)(2,1)} %pad.102.clone) | data formatting | bytes 25141248 | tf_op jit(solution)/shard_map/transpose(jvp())/reshape | solution.py:57
  779.4 8.8 pad_convert_fusion
  788.2 36.1 %copy.446 = f32[2,8,512,1024]{3,2,1,0:T(8,128)} copy(f32[2,8,512,1024]{3,1,2,0:T(8,128)S(1)} %bitcast.516) | data formatting | bytes 67108864
  824.3 9.0 slice_reduce_fusion
  856.9 8.7 copy.431
  865.6 10.6 pad.88.clone
  876.2 34.5 %reshape.1310 = bf16[12,523776]{1,0:T(8,128)(2,1)} reshape(bf16[12,512,1023]{2,1,0:T(8,128)(2,1)} %pad.88.clone) | data formatting | bytes 25141248 | tf_op jit(solution)/shard_map/transpose(jvp())/reshape | solution.py:57
  910.7 8.6 pad_convert_fusion.1
  919.3 36.1 %copy.443 = f32[2,8,512,1024]{3,2,1,0:T(8,128)} copy(f32[2,8,512,1024]{3,1,2,0:T(8,128)S(1)} %bitcast.517) | data formatting | bytes 67108864
  955.4 9.6 slice_reduce_fusion.1
  1009.2 6.8 pad_maximum_fusion
  1025.1 7.2 pad_maximum_fusion.1
  1040.9 6.6 pad_maximum_fusion.2
  1047.6 29.0 %reduce-scatter.16.cloned.1.call-done = f32[96,2]{1,0:T(8,128)} async-done(((f32[3072,2]{1,0:T(8,128)}), f32[96,2]{1,0:T(8,128)}) %reduce-scatter.16.cloned.1.call-update) | async-done | bytes 784
  1078.1 130.2 %all-reduce.38.cloned.1.call-done = (f32[12,768]{1,0:T(8,128)}, f32[2,3,12,128]{2,3,1,0:T(8,128)}) async-done(((f32[12,768]{1,0:T(8,128)}, f32[2,3,12,128]{2,3,1,0:T(8,128)}), (f32[12,768]{1,0:T(8,128)}, f32[2,3,12,128]{2,3,1,0:T(8,128)})) %all-reduce.38.cloned.1.call-update) | async-done | bytes 73744
  1210.9 133.2 %all-reduce.36.cloned.1.call-done = f32[2,128,768]{2,1,0:T(8,128)} async-done(((f32[2,128,768]{2,1,0:T(8,128)}), f32[2,128,768]{2,1,0:T(8,128)}) %all-reduce.36.cloned.1.call-update) | async-done | bytes 786448
  1345.6 209.0 %reduce-scatter.10.cloned.1.call-done = f32[2,4,24,768]{3,2,1,0:T(8,128)} async-done(((f32[2,4,768,768]{3,2,1,0:T(8,128)}), f32[2,4,24,768]{3,2,1,0:T(8,128)}) %reduce-scatter.10.cloned.1.call-update) | async-done | bytes 589840 | tf_op jit(solution)/shard_map/reduce_scatter | solution.py:344
  1556.4 208.6 %reduce-scatter.12.cloned.1.call-done = f32[2,24,3072]{2,1,0:T(8,128)} async-done(((f32[2,768,3072]{2,1,0:T(8,128)}), f32[2,24,3072]{2,1,0:T(8,128)}) %reduce-scatter.12.cloned.1.call-update) | async-done | bytes 589840 | tf_op jit(solution)/shard_map/reduce_scatter | solution.py:345
  1768.1 207.2 %reduce-scatter.14.cloned.1.call-done = f32[2,96,768]{2,1,0:T(8,128)} async-done(((f32[2,3072,768]{2,1,0:T(8,128)}), f32[2,96,768]{2,1,0:T(8,128)}) %reduce-scatter.14.cloned.1.call-update) | async-done | bytes 589840 | tf_op jit(solution)/shard_map/reduce_scatter | solution.py:346
  1984.1 39.1 %psum.23 = f32[]{:T(128)} all-reduce(f32[]{:T(128)S(6)} %add.537), channel_id=1, replica_groups=mesh['dp'=32] {'dp'}, use_global_device_ids=true, to_apply=%region_72.73 | all-reduce | flops 1 | bytes 8 | tf_op jit(solution)/shard_map/psum | solution.py:355
  (632 shorter events, 324.5 us)
Async XLA Ops:
  7.2 89.2 %copy-start.61 = (bf16[1,512,768]{2,1,0:T(8,128)(2,1)S(1)}, bf16[1,512,768]{2,1,0:T(8,128)(2,1)}, u32[]{:S(2)}) copy-start(bf16[1,512,768]{2,1,0:T(8,128)(2,1)} %param.27) | copy-start | bytes 2359300
  7.2 91.0 %copy-start.90 = (f32[2,3,12,4]{2,3,1,0:T(4,128)S(1)}, f32[2,3,12,4]{2,3,1,0:T(4,128)}, u32[]{:S(2)}) copy-start(f32[2,3,12,4]{2,3,1,0:T(4,128)} %param.38) | copy-start | bytes 3460
  7.2 454.6 %all-gather.6.cloned.1.call-start = ((), (), s32[]{:S(2)}) async-start(), calls=%async_computation.4 | async-start | bytes 9732096 | tf_op jit(solution)/shard_map/all_gather | solution.py:238
  9.2 535.0 %all-gather.8.cloned.1.call-start = ((), (), s32[]{:S(2)}) async-start(), calls=%async_computation.5 | async-start | bytes 9732096 | tf_op jit(solution)/shard_map/all_gather | solution.py:239
  11.1 553.0 %all-gather.10.cloned.1.call-start = ((), (), s32[]{:S(2)}) async-start(), calls=%async_computation.6 | async-start | bytes 9732096 | tf_op jit(solution)/shard_map/all_gather | solution.py:240
  12.9 1063.6 %reduce-scatter.16.cloned.1.call-start = ((), (), s32[]{:S(2)}) async-start(), calls=%async_computation.10 | async-start | bytes 1622016
  13.0 437.6 %copy-start.94 = (s32[512]{0:T(512)}, s32[512]{0:T(512)S(1)}, u32[]{:S(2)}) copy-start(s32[512]{0:T(512)S(1)} %fusion.157) | copy-start | bytes 6148
  13.0 439.8 %copy-start.96 = (s32[512]{0:T(512)}, s32[512]{0:T(512)S(1)}, u32[]{:S(2)}) copy-start(s32[512]{0:T(512)S(1)} %fusion.154) | copy-start | bytes 6148
  250.0 47.3 %copy-start.137 = (s32[1,2,512]{2,1,0:T(2,128)S(1)}, s32[1,2,512]{2,1,0:T(2,128)}, u32[]{:S(2)}) copy-start(s32[1,2,512]{2,1,0:T(2,128)} %param.30) | copy-start | bytes 12292
  297.4 158.9 %copy-start.98 = (s32[1,1,512]{2,1,0:T(1,128)}, s32[1,1,512]{2,1,0:T(1,128)S(1)}, u32[]{:S(2)}) copy-start(s32[1,1,512]{2,1,0:T(1,128)S(1)} %get-tuple-element.135) | copy-start | bytes 6148
  297.4 162.2 %copy-start.100 = (s32[1,1,512]{2,1,0:T(1,128)}, s32[1,1,512]{2,1,0:T(1,128)S(1)}, u32[]{:S(2)}) copy-start(s32[1,1,512]{2,1,0:T(1,128)S(1)} %get-tuple-element.134) | copy-start | bytes 6148
  297.5 150.3 %copy-start.49 = (pred[1,512,128]{2,1,0:T(32,128)(4,1)}, pred[1,512,128]{2,1,0:T(32,128)(4,1)S(1)}, u32[]{:S(2)}) copy-start(pred[1,512,128]{2,1,0:T(32,128)(4,1)S(1)} %iota_compare_fusion.6) | copy-start | bytes 196612
  297.7 150.2 %copy-start.53 = (pred[1,512,128]{2,1,0:T(32,128)(4,1)}, pred[1,512,128]{2,1,0:T(32,128)(4,1)S(1)}, u32[]{:S(2)}) copy-start(pred[1,512,128]{2,1,0:T(32,128)(4,1)S(1)} %iota_compare_fusion.7) | copy-start | bytes 196612
  400.3 47.6 %copy-start.38 = (bf16[1,512,768]{2,1,0:T(8,128)(2,1)S(1)}, bf16[1,512,768]{2,1,0:T(8,128)(2,1)}, u32[]{:S(2)}) copy-start(bf16[1,512,768]{2,1,0:T(8,128)(2,1)} %param.28) | copy-start | bytes 2359300
  448.2 37.8 %copy-start.14 = (bf16[512,768]{1,0:T(8,128)(2,1)}, bf16[512,768]{1,0:T(8,128)(2,1)S(1)}, u32[]{:S(2)}) copy-start(bf16[512,768]{1,0:T(8,128)(2,1)S(1)} %fusion.72) | copy-start | bytes 2359300
  450.6 21.0 %copy-start.41 = (bf16[512,768]{1,0:T(8,128)(2,1)}, bf16[512,768]{1,0:T(8,128)(2,1)S(1)}, u32[]{:S(2)}) copy-start(bf16[512,768]{1,0:T(8,128)(2,1)S(1)} %fusion.71) | copy-start | bytes 2359300
  471.6 19.1 copy-start.18
  476.2 14.5 copy-start.8
  486.1 31.1 %copy-start.16 = (bf16[512,768]{0,1:T(8,128)(2,1)}, bf16[512,768]{0,1:T(8,128)(2,1)S(1)}, u32[]{:S(2)}) copy-start(bf16[512,768]{0,1:T(8,128)(2,1)S(1)} %copy.348) | copy-start | bytes 2359300
  490.7 26.4 %copy-start.6 = (bf16[512,768]{0,1:T(8,128)(2,1)}, bf16[512,768]{0,1:T(8,128)(2,1)S(1)}, u32[]{:S(2)}) copy-start(bf16[512,768]{0,1:T(8,128)(2,1)S(1)} %copy.349) | copy-start | bytes 2359300
  542.9 87.1 %copy-start.27 = (f32[1,512,768]{2,1,0:T(8,128)}, f32[1,512,768]{2,1,0:T(8,128)S(1)}, u32[]{:S(2)}) copy-start(f32[1,512,768]{2,1,0:T(8,128)S(1)} %get-tuple-element.121) | copy-start | bytes 4718596
  542.9 87.1 %copy-start.29 = (f32[1,512,768]{2,1,0:T(8,128)}, f32[1,512,768]{2,1,0:T(8,128)S(1)}, u32[]{:S(2)}) copy-start(f32[1,512,768]{2,1,0:T(8,128)S(1)} %get-tuple-element.112) | copy-start | bytes 4718596
  542.9 87.1 %copy-start.107 = (f32[512]{0:T(512)}, f32[512]{0:T(512)S(1)}, u32[]{:S(2)}) copy-start(f32[512]{0:T(512)S(1)} %broadcast_multiply_fusion.4) | copy-start | bytes 6148
  543.2 86.7 %copy-start.127 = (f32[512]{0:T(512)}, f32[512]{0:T(512)S(1)}, u32[]{:S(2)}) copy-start(f32[512]{0:T(512)S(1)} %fusion.162) | copy-start | bytes 6148
  544.2 19.9 copy-start.153
  571.9 58.1 %copy-start.109 = (f32[512]{0:T(512)}, f32[512]{0:T(512)S(1)}, u32[]{:S(2)}) copy-start(f32[512]{0:T(512)S(1)} %broadcast_multiply_fusion.2) | copy-start | bytes 6148
  572.2 57.8 %copy-start.129 = (f32[512]{0:T(512)}, f32[512]{0:T(512)S(1)}, u32[]{:S(2)}) copy-start(f32[512]{0:T(512)S(1)} %fusion.164) | copy-start | bytes 6148
  572.2 18.8 copy-start.152
  635.5 16.7 slice-start
  635.6 16.7 slice-start.1
  779.4 54.3 %slice-start.6 = ((s8[6291456]{0:T(1024)(128)(4,1)}), s8[4194304]{0:T(1024)(128)(4,1)S(1)}, s32[]{:S(2)}) async-start(s8[6291456]{0:T(1024)(128)(4,1)} %bitcast.514), calls=%async_computation.19 | async-start | bytes 8388608
  788.2 45.5 %slice-start.7 = ((s8[6291456]{0:T(1024)(128)(4,1)}), s8[2097152]{0:T(1024)(128)(4,1)S(1)}, s32[]{:S(2)}) async-start(s8[6291456]{0:T(1024)(128)(4,1)} %bitcast.514), calls=%async_computation.20 | async-start | bytes 4194304
  978.6 229.6 %all-reduce.38.cloned.1.call-start = ((), (), s32[]{:S(2)}) async-start(), calls=%async_computation.12 | async-start | bytes 884736
  999.1 345.1 %all-reduce.36.cloned.1.call-start = ((), (), s32[]{:S(2)}) async-start(), calls=%async_computation.11 | async-start | bytes 1572864
  1001.5 553.1 %reduce-scatter.10.cloned.1.call-start = ((), (), s32[]{:S(2)}) async-start(), calls=%async_computation.7 | async-start | bytes 19464192 | tf_op jit(solution)/shard_map/reduce_scatter | solution.py:344
  1016.1 748.9 %reduce-scatter.12.cloned.1.call-start = ((), (), s32[]{:S(2)}) async-start(), calls=%async_computation.8 | async-start | bytes 19464192 | tf_op jit(solution)/shard_map/reduce_scatter | solution.py:345
  1032.3 943.1 %reduce-scatter.14.cloned.1.call-start = ((), (), s32[]{:S(2)}) async-start(), calls=%async_computation.9 | async-start | bytes 19464192 | tf_op jit(solution)/shard_map/reduce_scatter | solution.py:346
  1047.5 932.9 %copy-start.5 = (f32[1,512,768]{2,1,0:T(8,128)S(1)}, f32[1,512,768]{2,1,0:T(8,128)}, u32[]{:S(2)}) copy-start(f32[1,512,768]{2,1,0:T(8,128)} %copy-done.4) | copy-start | bytes 4718596
  1047.5 932.9 %copy-start.106 = (f32[512]{0:T(512)S(1)}, f32[512]{0:T(512)}, u32[]{:S(2)}) copy-start(f32[512]{0:T(512)} %copy-done.105) | copy-start | bytes 6148
  1047.5 976.4 %copy-start.131 = (f32[2,96]{1,0:T(2,128)S(1)}, f32[2,96]{1,0:T(2,128)}, u32[]{:S(2)}) copy-start(f32[2,96]{1,0:T(2,128)} %param.36) | copy-start | bytes 2308
  1047.6 979.3 %copy-start.91 = (f32[2,3,12,4]{2,3,1,0:T(4,128)S(1)}, f32[2,3,12,4]{2,3,1,0:T(4,128)}, u32[]{:S(2)}) copy-start(f32[2,3,12,4]{2,3,1,0:T(4,128)} %param.38) | copy-start | bytes 3460
  1077.4 903.0 %copy-start.132 = (f32[2,96]{1,0:T(2,128)}, f32[2,96]{1,0:T(2,128)S(1)}, u32[]{:S(2)}) copy-start(f32[2,96]{1,0:T(2,128)S(1)} %copy.412) | copy-start | bytes 2308
  1984.0 47.4 %copy-start.44 = (f32[2,24,3072]{2,1,0:T(8,128)S(1)}, f32[2,24,3072]{2,1,0:T(8,128)}, u32[]{:S(2)}) copy-start(f32[2,24,3072]{2,1,0:T(8,128)} %param.34) | copy-start | bytes 1769476
  1984.0 47.4 %copy-start.46 = (f32[2,24,3072]{2,1,0:T(8,128)S(1)}, f32[2,24,3072]{2,1,0:T(8,128)}, u32[]{:S(2)}) copy-start(f32[2,24,3072]{2,1,0:T(8,128)} %reduce-scatter.12.cloned.1.call-done) | copy-start | bytes 1769476
  1984.0 47.4 %copy-start.78 = (f32[2,24,3072]{2,1,0:T(8,128)S(1)}, f32[2,24,3072]{2,1,0:T(8,128)}, u32[]{:S(2)}) copy-start(f32[2,24,3072]{2,1,0:T(8,128)} %param.43) | copy-start | bytes 1769476
  1984.0 47.4 %copy-start.79 = (f32[2,24,3072]{2,1,0:T(8,128)S(1)}, f32[2,24,3072]{2,1,0:T(8,128)}, u32[]{:S(2)}) copy-start(f32[2,24,3072]{2,1,0:T(8,128)} %param.42) | copy-start | bytes 1769476
  1984.1 49.0 %copy-start.45 = (f32[2,96,768]{2,1,0:T(8,128)S(1)}, f32[2,96,768]{2,1,0:T(8,128)}, u32[]{:S(2)}) copy-start(f32[2,96,768]{2,1,0:T(8,128)} %param.35) | copy-start | bytes 1769476
  1984.1 49.0 %copy-start.47 = (f32[2,96,768]{2,1,0:T(8,128)S(1)}, f32[2,96,768]{2,1,0:T(8,128)}, u32[]{:S(2)}) copy-start(f32[2,96,768]{2,1,0:T(8,128)} %reduce-scatter.14.cloned.1.call-done) | copy-start | bytes 1769476
  (133 other events, 715.6 us)
Sparse Core Ops, SparseCore 0:
  11.6 85.2 all-gather.5
  100.3 80.9 all-gather.7
  184.8 81.4 all-gather.9
  978.8 97.7 reduce-scatter.15
  1082.9 125.2 all-reduce.37
  1214.1 130.0 all-reduce.35
  1350.6 203.9 reduce-scatter.9
  1561.0 203.9 reduce-scatter.11
  1771.4 203.8 reduce-scatter.13
where the time goes:
time: 2050 us; the launch traced here: 2040 us
  waiting for transfers between devices  917 us (45%)
  local copies, waits for them, and re-layouts  472 us (23%)
  matrix products  268 us (13%)
  blocking collectives  236 us (12%)
  other arithmetic  127 us (6%)
  between operations  23.7 us (1%)
    unnamed x12, waiting for transfers between devices  292 us
    reduce_scatter x1, waiting for transfers between devices, body(): lax.psum_scatter(grad_attn, 'dp', scatter_dimension=2, tiled=True)  209 us
    reduce_scatter x1, waiting for transfers between devices, body(): lax.psum_scatter(grad_in, 'dp', scatter_dimension=1, tiled=True)  209 us
    reduce_scatter x1, waiting for transfers between devices, body(): lax.psum_scatter(grad_out, 'dp', scatter_dimension=1, tiled=True)  207 us
    unnamed x382, local copies, waits for them, and re-layouts  206 us
    reshape x12, local copies, waits for them, and re-layouts, toeplitz(): return tiled.reshape(heads, width, 2 * width - 1)[:, :, width - 1:]  173 us
    dot_general x40, matrix products, matmul(): return jnp.dot(left, right, preferred_element_type=jnp.float32)  161 us
    all_gather x1, blocking collectives, body(): lax.all_gather(vectors, 'dp', axis=1, tiled=True)  44.5 us
  transfers between devices with their start and end apart: 9, of which 6 were waited for; matrix products, arithmetic and copies ran while one was open for 21% of the time, Pallas kernels for 0%

commit v1 on v0

v1 whole, which is shorter than its diff:
```python
import functools

import jax
import jax.numpy as jnp
import numpy as np
from jax import lax
from jax.experimental import pallas as pl
from jax.experimental.pallas import tpu as pltpu
from jax.sharding import Mesh
from jax.sharding import PartitionSpec as P

H = 12
HD = 64
VROWS = 16
VCOLS = 32
NB = 128
NR = 128
STEP = 10

EPSILON = 1e-05
NEGATIVE = -1000000000.0
CLIP = 1.0
BETA_ONE = 0.9
BETA_TWO = 0.95
ADAM_EPS = 1e-08
DECAY = 0.1
RATE_ATTN = 0.15
RATE_FEED = 0.04
RATE_OTHER = 0.2

BF = jnp.bfloat16
F32 = jnp.float32
AXES = ("z", "y", "x", "c")
CHIP = ("z", "y", "x")
FEED_BLOCK = 512
VMEM_LIMIT = 56 * 1024 * 1024
NT = (((1,), (1,)), ((), ()))


def dot(left, right):
    return jnp.dot(left, right, preferred_element_type=F32)


def dot_nt(left, right):
    return lax.dot_general(left, right, NT, preferred_element_type=F32)


def swap(value):
    return lax.ppermute(value, "c", [(0, 1), (1, 0)])


def shift(value, axis, step):
    size = lax.axis_size(axis)
    return lax.ppermute(value, axis, [(i, (i + step) % size) for i in range(size)])


def diagonal(value, step_y, step_x):
    ny, nx = lax.axis_size("y"), lax.axis_size("x")
    pairs = [
        (y * nx + x, (y + step_y) % ny * nx + (x + step_x) % nx)
        for y in range(ny)
        for x in range(nx)
    ]
    return lax.ppermute(value, ("y", "x"), pairs)


def chip_of(dz, dy, dx):
    nz, ny, nx = (lax.axis_size(a) for a in CHIP)
    z = (lax.axis_index("z") - dz) % nz
    y = (lax.axis_index("y") - dy) % ny
    x = (lax.axis_index("x") - dx) % nx
    return (z * ny + y) * nx + x


def gather_pieces(piece, order):
    nz = lax.axis_size("z")
    stack = jnp.stack([piece] + [shift(piece, "z", k) for k in range(1, nz)])
    first, second = ("x", "y") if order == 0 else ("y", "x")
    found = []
    firsts = [stack] + [shift(stack, first, k) for k in range(1, lax.axis_size(first))]
    for one, part in enumerate(firsts):
        for two in range(lax.axis_size(second)):
            moved = part if two == 0 else shift(part, second, two)
            found.append((moved, (two, one) if order == 0 else (one, two)))
    return found


def place_kernel(parts, count, lead, *refs):
    where, sources, out = refs[0], refs[1 : 1 + parts], refs[1 + parts]
    size = sources[0].shape[1] if lead else sources[0].shape[-1]
    for part in range(parts):
        begin = 2 * part // parts * size
        for k in range(count):
            spot = where[part * count + k]
            if lead:
                for row in range(size):
                    out[begin + row, spot] = sources[part][k, row]
            else:
                out[spot, :, begin : begin + size] = sources[part][k]


def gather_matrix(halves, chips, lead):
    nz = lax.axis_size("z")
    found = gather_pieces(halves[0], 0) + gather_pieces(halves[1], 1)
    where = jnp.stack([chip_of(k, sy, sx) for _, (sy, sx) in found for k in range(nz)])
    parts = [part for part, _ in found]
    shape = halves[0].shape
    if lead:
        whole = (2 * shape[0], chips) + shape[1:]
    else:
        whole = (chips,) + shape[:-1] + (2 * shape[-1],)
    return pl.pallas_call(
        functools.partial(place_kernel, len(parts), nz, lead),
        out_shape=jax.ShapeDtypeStruct(whole, halves[0].dtype),
        in_specs=[pl.BlockSpec(memory_space=pltpu.SMEM)]
        + [pl.BlockSpec(memory_space=pltpu.VMEM)] * len(parts),
        out_specs=pl.BlockSpec(memory_space=pltpu.VMEM),
        compiler_params=pltpu.CompilerParams(vmem_limit_bytes=VMEM_LIMIT),
        name="place",
    )(where.astype(jnp.int32), *parts)


def slot_table(order):
    nz, ny, nx = (lax.axis_size(a) for a in CHIP)
    chips = jnp.arange(nz * ny * nx)
    zr = (chips // (ny * nx) - lax.axis_index("z")) % nz
    yr = (chips // nx % ny - lax.axis_index("y")) % ny
    xr = (chips % nx - lax.axis_index("x")) % nx
    if order == 0:
        return ((xr * ny + yr) * nz + zr).astype(jnp.int32)
    return ((yr * nx + xr) * nz + zr).astype(jnp.int32)


def scatter_plane(slots, order):
    first, second = ("x", "y") if order == 0 else ("y", "x")
    nz = lax.axis_size("z")
    for axis in (first, second):
        size = lax.axis_size(axis)
        parts = slots.reshape((size, -1) + slots.shape[1:])
        total = parts[0].astype(F32)
        for k in range(1, size):
            total = total + shift(parts[k], axis, k).astype(F32)
        slots = total.astype(BF)
    return slots.reshape((nz,) + slots.shape[1:])


def scatter_line(column):
    total = column[0].astype(F32)
    for k in range(1, lax.axis_size("z")):
        total = total + shift(column[k], "z", k).astype(F32)
    return total


def split_three(value):
    high = lax.reduce_precision(value, 8, 7)
    rest = value - high
    mid = lax.reduce_precision(rest, 8, 7)
    return [high.astype(BF), mid.astype(BF), (rest - mid).astype(BF)]


def join_three(parts):
    high, mid, small = (part.astype(F32) for part in parts)
    return high + (mid + small)


def base_rows(tables):
    half = NR // 2
    low, high = tables[:, :, :1], tables[:, :, -1:]
    one = tables.shape[:2]

    def many(edge, count):
        return jnp.broadcast_to(edge, one + (count,))

    line = jnp.concatenate(
        [many(high, NB - half + 1), tables[:, :, ::-1], many(low, 255 - half), many(high, 128)],
        axis=2,
    )[0]
    plane = jnp.concatenate(
        [tables[:, :, half:], many(high, NB - half), many(low, NB - half), tables[:, :, :half]], axis=2
    )
    pair = jnp.concatenate([plane[1], plane[2]], axis=1)
    rows = jnp.stack([line, pair], axis=1)
    return jnp.pad(rows, ((0, 0), (0, 6), (0, 0)))


def table_sums(sums):
    half = NR // 2
    line = jnp.concatenate([sums[:, 0, 384:], sums[:, 0, :384]], axis=1)[:, ::-1]
    far = jnp.sum(sums[:, 2, 256:], axis=1) + jnp.sum(line[:, : 256 - half], axis=1)
    near = jnp.sum(sums[:, 2, :256], axis=1) + jnp.sum(line[:, 254 + half :], axis=1)
    middle = line[:, 256 - half : 254 + half]
    first = jnp.concatenate([far[:, None], middle, near[:, None]], axis=1)

    def plane(part):
        ordered = jnp.concatenate([part[:, 128:], part[:, :128]], axis=1)[:, ::-1]
        low = jnp.sum(ordered[:, : 128 - half], axis=1)
        high = jnp.sum(ordered[:, 126 + half :], axis=1)
        return jnp.concatenate(
            [low[:, None], ordered[:, 128 - half : 126 + half], high[:, None]], axis=1
        )

    return jnp.stack([first, plane(sums[:, 1, :256]), plane(sums[:, 1, 256:])])


def build_tables(base, strip, planes, head):
    line = jnp.broadcast_to(base[head, 0:1, :], (128, 512))
    middle = pltpu.roll(line, 0, 1, stride=1, stride_axis=0)[:, :384]
    strip[head, :, 256:640] = middle
    strip[head, :, :256] = jnp.broadcast_to(base[head, 0:1, 0:1], (128, 256))
    strip[head, :, 640:] = jnp.broadcast_to(base[head, 0:1, 383:384], (128, 256))
    for k in range(2):
        row = jnp.broadcast_to(base[head, 1:2, 256 * k : 256 * k + 256], (128, 256))
        rolled = pltpu.roll(row, 0, 1, stride=1, stride_axis=0)
        planes[head, k] = rolled[:, :128].astype(BF)


def left_side(both, planes, head):
    return jnp.concatenate(
        [
            dot(both[:, :NB], planes[head, 0]).astype(BF),
            dot(both[:, NB:], planes[head, 1]).astype(BF),
        ],
        axis=1,
    )


def head_lanes(value, head):
    lanes = lax.broadcasted_iota(jnp.int32, value.shape, 1)
    return jnp.where((lanes >= HD) == (head == 1), value, jnp.zeros_like(value))


def scores_t(key_side, query_side, strip, head, valid):
    count = key_side.shape[0]
    raw = dot_nt(key_side, query_side)
    blocks = []
    for block in range(count // 128):
        start = 384 - 128 * block
        part = raw[128 * block : 128 * block + 128] + strip[head, :, start : start + count]
        rows = lax.broadcasted_iota(jnp.int32, (128, count), 0) + 128 * block
        blocks.append(jnp.where(rows < valid, part, NEGATIVE))
    return blocks


def attend_kernel(valid_ref, q_ref, k_ref, v_ref, both_ref, base_ref, mixed_ref, log_ref, strip, planes):
    page = pl.program_id(1)

    @pl.when(page == 0)
    def _():
        for head in range(2):
            build_tables(base_ref, strip, planes, head)

    valid = valid_ref[page]
    both = both_ref[...]
    key_side = jnp.concatenate([both, k_ref[...]], axis=1)
    values_t = v_ref[...].T
    mixed = []
    for head in range(2):
        query_side = jnp.concatenate(
            [left_side(both, planes, head), head_lanes(q_ref[...], head)], axis=1
        )
        blocks = scores_t(key_side, query_side, strip, head, valid)
        highest = functools.reduce(
            jnp.maximum, [jnp.max(block, axis=0, keepdims=True) for block in blocks]
        )
        raised = [jnp.exp(block - highest) for block in blocks]
        total = functools.reduce(
            jnp.add, [jnp.sum(part, axis=0, keepdims=True) for part in raised]
        )
        inverse = 1.0 / total
        probs = jnp.concatenate([(part * inverse).astype(BF) for part in raised], axis=0)
        mixed.append(dot(values_t[HD * head : HD * head + HD], probs))
        log_ref[0, 0, head : head + 1, :] = highest + jnp.log(total)
    mixed_ref[...] = jnp.concatenate(mixed, axis=0).T.astype(BF)


def attend_call(valid, queries, keys, values, both, base, count):
    pages = queries.shape[0] // count
    pairs = H // 2
    wide = pl.BlockSpec((count, 128), lambda pair, page: (page, pair))
    return pl.pallas_call(
        attend_kernel,
        grid=(pairs, pages),
        in_specs=[
            pl.BlockSpec(memory_space=pltpu.SMEM),
            wide,
            wide,
            wide,
            pl.BlockSpec((count, 2 * NB), lambda pair, page: (page, 0)),
            pl.BlockSpec((2, 8, 512), lambda pair, page: (pair, 0, 0)),
        ],
        out_specs=[
            wide,
            pl.BlockSpec((1, 1, 8, count), lambda pair, page: (page, pair, 0, 0)),
        ],
        out_shape=[
            jax.ShapeDtypeStruct(queries.shape, BF),
            jax.ShapeDtypeStruct((pages, pairs, 8, count), F32),
        ],
        scratch_shapes=[
            pltpu.VMEM((2, 128, count + 384), F32),
            pltpu.VMEM((2, 2, NB, NB), BF),
        ],
        compiler_params=pltpu.CompilerParams(vmem_limit_bytes=VMEM_LIMIT),
        name="attend",
    )(valid, queries, keys, values, both, base)


def fold_diagonals(value):
    rows, lanes = value.shape
    while rows > 1:
        rows //= 2
        value = value[:rows] + pltpu.roll(value[rows:], lanes - rows, 1)
    return value


def attend_back_kernel(
    valid_ref, q_ref, k_ref, v_ref, dm_ref, mixed_ref, log_ref, both_ref, both_t_ref, base_ref,
    dq_ref, dk_ref, dv_ref, sums_ref, strip, planes, d_strip, d_planes,
):
    page = pl.program_id(1)

    @pl.when(page == 0)
    def _():
        for head in range(2):
            build_tables(base_ref, strip, planes, head)
        d_strip[...] = jnp.zeros_like(d_strip)
        d_planes[...] = jnp.zeros_like(d_planes)

    valid = valid_ref[page]
    both = both_ref[...]
    both_t = both_t_ref[...]
    count = both.shape[0]
    key_side = jnp.concatenate([both, k_ref[...]], axis=1)
    values = v_ref[...]
    keys_t = k_ref[...].T
    d_mixed_t = dm_ref[...].T
    weighted = d_mixed_t.astype(F32) * mixed_ref[...].T.astype(F32)
    rows = lax.broadcasted_iota(jnp.int32, d_mixed_t.shape, 0)
    d_keys = d_values = None
    d_queries = []
    for head in range(2):
        masked_q = head_lanes(q_ref[...], head)
        query_side = jnp.concatenate([left_side(both, planes, head), masked_q], axis=1)
        blocks = scores_t(key_side, query_side, strip, head, valid)
        log_total = log_ref[0, 0, head : head + 1, :]
        inner = jnp.sum(weighted[HD * head : HD * head + HD], axis=0, keepdims=True)
        d_mixed_head = jnp.where(
            (rows >= HD) == (head == 1), d_mixed_t, jnp.zeros_like(d_mixed_t)
        )
        d_probs = dot(values, d_mixed_head)
        probs_low, scores_low = [], []
        for index, block in enumerate(blocks):
            probs = jnp.exp(block - log_total)
            d_scores = probs * (d_probs[128 * index : 128 * index + 128] - inner)
            start = 384 - 128 * index
            d_strip[head, :, start : start + count] += d_scores
            probs_low.append(probs.astype(BF))
            scores_low.append(d_scores.astype(BF))
        probs_low = jnp.concatenate(probs_low, axis=0)
        scores_low = jnp.concatenate(scores_low, axis=0)
        part_v = dot(probs_low, head_lanes(dm_ref[...], head))
        mixed_k = dot(scores_low, jnp.concatenate([both, masked_q], axis=1))
        part_k = mixed_k[:, 2 * NB :]
        d_values = part_v if d_values is None else d_values + part_v
        d_keys = part_k if d_keys is None else d_keys + part_k
        d_queries.append(dot(keys_t[HD * head : HD * head + HD], scores_low))
        for k in range(2):
            side = mixed_k[:, NB * k : NB * k + NB].astype(BF)
            d_planes[head, k] += dot(both_t[NB * k : NB * k + NB], side)
    dq_ref[...] = (jnp.concatenate(d_queries, axis=0).T * HD ** (-0.5)).astype(BF)
    dk_ref[...] = d_keys.astype(BF)
    dv_ref[...] = d_values.astype(BF)

    @pl.when(page == pl.num_programs(1) - 1)
    def _():
        blank = jnp.zeros((128, 128), F32)
        for head in range(2):
            middle = jnp.concatenate([d_strip[head, :, 256:640], blank], axis=1)
            sums_ref[head, 0:1, :] = fold_diagonals(middle)
            for k in range(2):
                padded = jnp.concatenate([d_planes[head, k], blank], axis=1)
                sums_ref[head, 1:2, 256 * k : 256 * k + 256] = fold_diagonals(padded)
            sums_ref[head, 2:3, :256] = jnp.sum(d_strip[head, :, :256], axis=0, keepdims=True)
            sums_ref[head, 2:3, 256:] = jnp.sum(d_strip[head, :, 640:], axis=0, keepdims=True)


def attend_back_call(valid, queries, keys, values, d_mixed, mixed, log_total, both, base, count):
    pages = queries.shape[0] // count
    pairs = H // 2
    both_t = both.T
    wide = pl.BlockSpec((count, 128), lambda pair, page: (page, pair))
    return pl.pallas_call(
        attend_back_kernel,
        grid=(pairs, pages),
        in_specs=[
            pl.BlockSpec(memory_space=pltpu.SMEM),
            wide,
            wide,
            wide,
            wide,
            wide,
            pl.BlockSpec((1, 1, 8, count), lambda pair, page: (page, pair, 0, 0)),
            pl.BlockSpec((count, 2 * NB), lambda pair, page: (page, 0)),
            pl.BlockSpec((2 * NB, count), lambda pair, page: (0, page)),
            pl.BlockSpec((2, 8, 512), lambda pair, page: (pair, 0, 0)),
        ],
        out_specs=[wide, wide, wide, pl.BlockSpec((2, 8, 512), lambda pair, page: (pair, 0, 0))],
        out_shape=[jax.ShapeDtypeStruct(queries.shape, BF)] * 3
        + [jax.ShapeDtypeStruct((H, 8, 512), F32)],
        scratch_shapes=[
            pltpu.VMEM((2, 128, count + 384), F32),
            pltpu.VMEM((2, 2, NB, NB), BF),
            pltpu.VMEM((2, 128, count + 384), F32),
            pltpu.VMEM((2, 2, NB, NB), F32),
        ],
        compiler_params=pltpu.CompilerParams(vmem_limit_bytes=VMEM_LIMIT),
        name="attend_back",
    )(valid, queries, keys, values, d_mixed, mixed, log_total, both, both_t, base)


def gelu_parts(before):
    size = jnp.abs(before) * (0.5**0.5)
    denominator = 1.0 + 0.3275911 * size
    t = pl.reciprocal(denominator, approx=True)
    t = t * (2.0 - denominator * t)
    bell = jnp.exp(-0.5 * before * before)
    tail = t * (
        0.5 * 0.254829592
        + t
        * (
            0.5 * -0.284496736
            + t * (0.5 * 1.421413741 + t * (0.5 * -1.453152027 + t * (0.5 * 1.061405429)))
        )
    )
    tail = tail * bell
    below = jnp.where(before >= 0.0, 1.0 - tail, tail)
    return before * below, below + before * (bell * 0.3989422804014327)


def feed_kernel(rows_ref, first_ref, bias_ref, active_ref, slope_ref):
    before = dot(rows_ref[...], first_ref[...]) + bias_ref[...]
    active, slope = gelu_parts(before)
    active_ref[...] = active.astype(BF)
    slope_ref[...] = slope.astype(BF)


def feed_call(rows, first, bias, block):
    tokens, width = rows.shape
    hidden = first.shape[1]
    out = pl.BlockSpec((tokens, block), lambda i: (0, i))
    return pl.pallas_call(
        feed_kernel,
        grid=(hidden // block,),
        in_specs=[
            pl.BlockSpec((tokens, width), lambda i: (0, 0)),
            pl.BlockSpec((width, block), lambda i: (0, i)),
            pl.BlockSpec((1, block), lambda i: (0, i)),
        ],
        out_specs=[out, out],
        out_shape=[jax.ShapeDtypeStruct((tokens, hidden), BF)] * 2,
        compiler_params=pltpu.CompilerParams(vmem_limit_bytes=VMEM_LIMIT),
        name="feed",
    )(rows, first, bias)


def store_slots(slots_ref, out_ref, total, half):
    chips = out_ref.shape[1]
    rows = total.shape[0] // chips
    for chip in range(chips):
        part = total[chip * rows : chip * rows + rows].astype(BF)
        out_ref[0, slots_ref[0, chip]] = part[:, :half]
        out_ref[1, slots_ref[1, chip]] = part[:, half:]


def feed_back_kernel(slots_ref, rows_t_ref, low_ref, second_ref, first_ref, slope_ref, rest_ref, du_ref, dfirst_ref, dbias_ref):
    step = pl.program_id(0)
    d_active = dot_nt(low_ref[...], second_ref[...])
    d_before = (slope_ref[...].astype(F32) * d_active).astype(BF)
    dbias_ref[...] = jnp.sum(d_before.astype(F32), axis=0, keepdims=True)
    part = dot_nt(d_before, first_ref[...])

    @pl.when(step == 0)
    def _():
        du_ref[...] = rest_ref[...] + part

    @pl.when(step > 0)
    def _():
        du_ref[...] += part

    total = dot(rows_t_ref[...], d_before)
    store_slots(slots_ref, dfirst_ref, total, total.shape[1] // 2)


def feed_back_call(slots, rows, low, second, first, slope, rest, chips, block):
    tokens, width = rows.shape
    hidden = second.shape[0]
    piece = width // chips
    whole = pl.BlockSpec((tokens, width), lambda i: (0, 0))
    return pl.pallas_call(
        feed_back_kernel,
        grid=(hidden // block,),
        in_specs=[
            pl.BlockSpec(memory_space=pltpu.SMEM),
            pl.BlockSpec((width, tokens), lambda i: (0, 0)),
            whole,
            pl.BlockSpec((block, width), lambda i: (i, 0)),
            pl.BlockSpec((width, block), lambda i: (0, i)),
            pl.BlockSpec((tokens, block), lambda i: (0, i)),
            whole,
        ],
        out_specs=[
            whole,
            pl.BlockSpec((2, chips, piece, block // 2), lambda i: (0, 0, 0, i)),
            pl.BlockSpec((1, block), lambda i: (0, i)),
        ],
        out_shape=[
            jax.ShapeDtypeStruct((tokens, width), F32),
            jax.ShapeDtypeStruct((2, chips, piece, hidden // 2), BF),
            jax.ShapeDtypeStruct((1, hidden), F32),
        ],
        compiler_params=pltpu.CompilerParams(vmem_limit_bytes=VMEM_LIMIT),
        name="feed_back",
    )(slots, rows.T, low, second, first, slope, rest)


def outer_kernel(slots_ref, left_ref, right_ref, out_ref):
    chips = out_ref.shape[1]
    step = pl.program_id(0)
    total = dot(left_ref[...], right_ref[...])
    rows = out_ref.shape[2]
    count = total.shape[0] // rows
    half = total.shape[1] // 2
    for index in range(count):
        part = total[index * rows : index * rows + rows].astype(BF)
        chip = step * count + index
        out_ref[0, slots_ref[0, chip]] = part[:, :half]
        out_ref[1, slots_ref[1, chip]] = part[:, half:]


def outer_call(slots, left_t, right, chips, steps):
    height, tokens = left_t.shape
    width = right.shape[1]
    block = height // steps
    return pl.pallas_call(
        outer_kernel,
        grid=(steps,),
        in_specs=[
            pl.BlockSpec(memory_space=pltpu.SMEM),
            pl.BlockSpec((block, tokens), lambda i: (i, 0)),
            pl.BlockSpec((tokens, width), lambda i: (0, 0)),
        ],
        out_specs=pl.BlockSpec((2, chips, height // chips, width // 2), lambda i: (0, 0, 0, 0)),
        out_shape=jax.ShapeDtypeStruct((2, chips, height // chips, width // 2), BF),
        compiler_params=pltpu.CompilerParams(vmem_limit_bytes=VMEM_LIMIT),
        name="outer",
    )(slots, left_t, right)


def layer_norm(rows, gain, shift_row):
    center = rows - jnp.mean(rows, axis=-1, keepdims=True)
    spread = jnp.mean(center * center, axis=-1, keepdims=True)
    scale = lax.rsqrt(spread + EPSILON)
    hat = center * scale
    return hat * gain + shift_row, hat, scale


def layer_norm_back(grad, hat, scale, gain):
    scaled = grad * gain
    first = jnp.mean(scaled, axis=-1, keepdims=True)
    second = jnp.mean(scaled * hat, axis=-1, keepdims=True)
    d_rows = scale * (scaled - first - hat * second)
    return d_rows, jnp.sum(grad * hat, axis=0), jnp.sum(grad, axis=0)


def adam(weight, grad, first, second, rate, decay):
    first_new = BETA_ONE * first + (1 - BETA_ONE) * grad
    second_new = BETA_TWO * second + (1 - BETA_TWO) * grad * grad
    ratio = (
        first_new / (1 - BETA_ONE**STEP) / (jnp.sqrt(second_new / (1 - BETA_TWO**STEP)) + ADAM_EPS)
    )
    return (first_new, second_new, weight - rate * (ratio + decay * weight))


def body(
    visual, text, lengths, text_boxes, cot_visual, cot_text,
    attn_w, ffn_in, ffn_out, bias_in, vectors, pos_tables, spatial,
    attn_mom, attn_sec, in_mom, in_sec, out_mom, out_sec, bias_mom, bias_sec,
    vec_mom, vec_sec, pos_mom, pos_sec, spatial_mom, spatial_sec,
):
    core = lax.axis_index("c")
    seen = core == 0
    nz, ny, nx = (lax.axis_size(a) for a in CHIP)
    chips = nz * ny * nx
    devices = 2 * chips
    _, count, width = visual.shape
    tokens = 2 * count

    def mine_of(first, second):
        return jnp.where(seen, first, second)

    def trade(first, second):
        return mine_of(first, second), swap(mine_of(second, first))

    def by_core(own, other):
        return jnp.where(seen, jnp.stack([own, other]), jnp.stack([other, own]))

    attn_low = attn_w.astype(BF)
    in_low = ffn_in.astype(BF)
    out_low = ffn_out.astype(BF)
    attn_own, attn_other = trade(attn_low[0], attn_low[1])
    in_own, in_other = trade(in_low[0], in_low[1])
    out_own, out_other = trade(out_low[0], out_low[1])
    rows_a = attn_w.shape[2]
    rows_o = ffn_out.shape[1]
    hidden = ffn_in.shape[2]
    attn_piece = jnp.where(
        seen,
        jnp.concatenate([attn_own, attn_other], axis=1),
        jnp.concatenate([attn_other, attn_own], axis=1),
    )
    in_piece = by_core(in_own, in_other).reshape(2 * rows_a, hidden)
    out_piece = by_core(out_own, out_other).reshape(2 * rows_o, width)

    raw_own = visual[0].astype(F32)
    sums = jnp.stack([jnp.sum(raw_own, axis=0), jnp.sum(raw_own * raw_own, axis=0)])
    vec_rows = [
        jnp.stack([vectors[0], vectors[1]] + [vectors[k + 2 * s] for k in (2, 3, 6, 7)] + [vectors[10 + s]])
        for s in range(2)
    ]

    def packed(s):
        def row(values):
            flat = values.reshape(1, -1)
            return jnp.pad(flat, ((0, 0), (0, -flat.shape[1] % width))).reshape(-1, width)

        return jnp.concatenate(
            [row(pos_tables[s].astype(BF)), row(jnp.concatenate(
                [part.reshape(1, -1) for part in split_three(vec_rows[s]) + split_three(bias_in[s])], axis=1
            ))], axis=0
        )

    pack_zero, pack_one = packed(0), packed(1)
    small_rows = pack_zero.shape[0]
    space = spatial.astype(BF).reshape(-1, width)
    space_rows = space.shape[0]
    pack_own, pack_other = trade(pack_zero, pack_one)
    space_other, sums_other = swap((space, sums))
    pack_both = by_core(pack_own, pack_other).reshape(2 * small_rows, width)
    space_both = by_core(space, space_other).reshape(2 * space_rows, width)
    small = jnp.concatenate(
        [space_both, pack_both, jnp.concatenate(split_three(sums + sums_other), axis=0)], axis=0
    )
    small = jnp.pad(small, ((0, -small.shape[0] % 8), (0, 0)))
    column = jnp.stack([small] + [shift(small, "z", k) for k in range(1, nz)])
    plane = [
        (column if sy == 0 and sx == 0 else diagonal(column, sy, sx), sy, sx)
        for sy in range(ny)
        for sx in range(nx)
    ]
    nearby = jnp.concatenate([part for part, _, _ in plane], axis=0)
    source = jnp.stack([chip_of(k, sy, sx) for _, sy, sx in plane for k in range(nz)])
    place_of = jnp.zeros((chips,), jnp.int32).at[source].set(jnp.arange(chips, dtype=jnp.int32))
    gathered = jnp.take(nearby, place_of, axis=0)
    wide_spatial = gathered[:, : 2 * space_rows].reshape(chips, 2, 2, -1, width)
    wide_spatial = wide_spatial.transpose(2, 0, 1, 3, 4).reshape(2 * NB, width)
    packs = gathered[:, 2 * space_rows : 2 * space_rows + 2 * small_rows]
    packs = packs.reshape(devices, small_rows, width)
    pos_size = pos_tables[0].size
    pos_lines = -(-pos_size // width)
    tables = packs[:, :pos_lines].reshape(devices, -1)[:, :pos_size]
    tables = tables.reshape(devices, 3, H, -1).transpose(1, 2, 0, 3).reshape(3, H, NR).astype(F32)
    params = packs[:, pos_lines:].reshape(devices, -1)
    vec_size = vec_rows[0].size
    bias_size = bias_in[0].size
    wide_vec = join_three([params[:, vec_size * k : vec_size * (k + 1)] for k in range(3)])
    wide_vec = wide_vec.reshape(devices, 7, -1).transpose(1, 0, 2).reshape(7, width)
    wide_bias = join_three(
        [params[:, 3 * vec_size + bias_size * k : 3 * vec_size + bias_size * (k + 1)] for k in range(3)]
    ).reshape(1, hidden)
    parts = gathered[:, 2 * space_rows + 2 * small_rows :]
    sums = jnp.sum(join_three([parts[:, 2 * k : 2 * k + 2] for k in range(3)]), axis=0)

    data_own, data_other = trade(visual[0], text[0])
    cot_own, cot_other = trade(cot_visual[0], cot_text[0])
    length_other, boxes_other = swap((lengths, text_boxes))
    total = count * devices
    mean = sums[0] / total
    variance = sums[1] / total - mean * mean
    inverse = lax.rsqrt(variance + EPSILON)
    stream_mean = jnp.where(seen, mean, 0.0)
    stream_inverse = jnp.where(seen, inverse, 1.0)
    stream_gain = jnp.where(seen, wide_vec[0], 1.0)
    stream_shift = jnp.where(seen, wide_vec[1], 0.0)
    raw = jnp.concatenate([data_own, data_other], axis=0).astype(F32)
    normed = (raw - stream_mean) * stream_inverse
    inputs = normed * stream_gain + stream_shift
    position = jnp.arange(count, dtype=jnp.int32)
    lengths_both = jnp.concatenate([lengths, length_other])
    keep_pages = (position[None, :] < lengths_both[:, None]).astype(F32).reshape(tokens, 1)
    keep_rows = jnp.where(seen, 1.0, keep_pages)
    valid = jnp.where(seen, count, lengths_both).astype(jnp.int32)
    grid_x = position % VCOLS * (NB // VCOLS) + NB // VCOLS // 2
    grid_y = position // VCOLS * (NB // VROWS) + NB // VROWS // 2
    boxes = jnp.concatenate([text_boxes, boxes_other], axis=0)
    boxes = jnp.where(seen, jnp.stack([grid_x, grid_y])[None], boxes)
    both = jnp.concatenate(
        [
            (boxes[:, k, :].reshape(tokens, 1) == jnp.arange(NB)[None, :]).astype(BF)
            for k in range(2)
        ],
        axis=1,
    )
    place = dot(both, wide_spatial)
    joint = (inputs + place).astype(BF)
    plain = inputs.astype(BF)
    base = base_rows(tables)

    wide_attn = gather_matrix((attn_piece[:2], attn_piece[2:]), chips, True)
    wide_attn = wide_attn.reshape(4, width, width)
    half_in, half_out = hidden // 2, width // 2
    wide_in = gather_matrix((in_piece[:, :half_in], in_piece[:, half_in:]), chips, False)
    wide_in = wide_in.reshape(width, hidden)
    wide_out = gather_matrix((out_piece[:, :half_out], out_piece[:, half_out:]), chips, False)
    wide_out = wide_out.reshape(hidden, width)

    scale = HD ** (-0.5)
    queries = (dot(joint, wide_attn[0]).astype(BF) * scale).astype(BF)
    keys = dot(joint, wide_attn[1]).astype(BF)
    values = dot(plain, wide_attn[2]).astype(BF)
    mixed, log_total = attend_call(valid, queries, keys, values, both, base, count)
    att = dot(mixed, wide_attn[3])
    own_att = att * keep_rows
    other_att = swap(own_att)
    other_att = jnp.concatenate([other_att[count:], other_att[:count]], axis=0)
    merged = own_att + other_att

    u, hat_one, scale_one = layer_norm(inputs + merged, wide_vec[2], wide_vec[3])
    u_low = u.astype(BF)
    active, slope = feed_call(u_low, wide_in, wide_bias, FEED_BLOCK)
    ff = dot(active, wide_out) + wide_vec[6]
    y, hat_two, scale_two = layer_norm(u + ff, wide_vec[4], wide_vec[5])
    out = (y * keep_rows).astype(BF)

    cot = jnp.concatenate([cot_own, cot_other], axis=0).astype(F32) * keep_rows
    dy, gain_two, shift_two = layer_norm_back(cot, hat_two, scale_two, wide_vec[4])
    dff = dy.astype(BF)
    dff_sum = jnp.sum(dff.astype(F32), axis=0)
    slots = jnp.stack([slot_table(0), slot_table(1)])
    d_out = outer_call(slots, active.T, dff, chips, 4)
    du, d_in, d_bias = feed_back_call(slots, u_low, dff, wide_out, wide_in, slope, dy, chips, FEED_BLOCK)
    d_pre, gain_one, shift_one = layer_norm_back(du, hat_one, scale_one, wide_vec[2])

    other_pre = swap(d_pre)
    other_pre = jnp.concatenate([other_pre[count:], other_pre[:count]], axis=0)
    d_merged = d_pre + other_pre
    d_att = (d_merged * keep_rows).astype(BF)
    d_w3 = outer_call(slots, mixed.T, d_att, chips, 1)
    d_mixed = dot_nt(d_att, wide_attn[3]).astype(BF)
    dq, dk, dv, table_parts = attend_back_call(
        valid, queries, keys, values, d_mixed, mixed, log_total, both, base, count
    )
    joint_t = joint.T
    d_w0 = outer_call(slots, joint_t, dq, chips, 1)
    d_w1 = outer_call(slots, joint_t, dk, chips, 1)
    d_w2 = outer_call(slots, plain.T, dv, chips, 1)
    d_joint = dot_nt(dq, wide_attn[0]) + dot_nt(dk, wide_attn[1])
    dx = d_joint + dot_nt(dv, wide_attn[2]) + d_pre
    d_space = dot(both.T, d_joint.astype(BF))
    d_tables = table_sums(table_parts)
    norm_shift = jnp.sum(dx, axis=0)
    norm_gain = jnp.sum(dx * normed, axis=0)
    grad_rows = dx * stream_gain * stream_inverse

    def reduced(halves, blocks=1):
        sums = [scatter_line(scatter_plane(halves[k], k)) for k in range(2)]
        cut = jnp.stack([part.reshape(part.shape[0], blocks, -1) for part in sums], axis=2)
        return cut.reshape(cut.shape[0], -1)

    sum_out = reduced(d_out)
    sum_in = reduced(d_in, hidden // FEED_BLOCK)
    sum_attn = jnp.stack([reduced(part) for part in (d_w0, d_w1, d_w2, d_w3)])

    def own_rows(value, axis):
        first, second = jnp.split(value, 2, axis=axis)
        return trade(first, second)

    def by_stream(own, other):
        return jnp.where(seen, jnp.stack([own, other]), jnp.stack([other, own]))

    is_norm = jnp.where(seen, 1.0, 0.0)
    vec_grad = jnp.stack(
        [norm_gain * is_norm, norm_shift * is_norm, gain_one, shift_one, gain_two, shift_two, dff_sum]
    )

    def lines(values):
        flat = values.reshape(chips, -1)
        flat = jnp.pad(flat, ((0, 0), (0, -flat.shape[1] % width)))
        return flat.reshape(chips, -1, width)

    space_grad = d_space.reshape(2, chips, 2, -1, width).transpose(1, 2, 0, 3, 4)
    pos_grad = d_tables.reshape(3, H, chips, 2, -1).transpose(2, 3, 0, 1, 4)
    vecs = vec_grad.reshape(7, chips, 2, -1).transpose(1, 2, 0, 3)
    pieces = [
        space_grad.reshape(chips, -1, width),
        lines(pos_grad),
        lines(vecs),
        lines(d_bias),
    ]
    bounds = np.cumsum([0] + [part.shape[1] for part in pieces])
    small_grad = jnp.concatenate(pieces, axis=1)
    small_grad = jnp.pad(small_grad, ((0, 0), (0, -small_grad.shape[1] % 8), (0, 0)))
    order = jnp.zeros((chips,), jnp.int32).at[slots[0]].set(jnp.arange(chips, dtype=jnp.int32))
    small_slots = jnp.take(small_grad.astype(BF), order, axis=0)
    small_sum = scatter_line(scatter_plane(small_slots, 0))
    own_space, other_space = own_rows(small_sum[: bounds[1]], 0)
    grad_spatial = (own_space + other_space).reshape(spatial.shape)

    def unline(index, shape):
        size = int(np.prod(shape))
        flat = small_sum[bounds[index] : bounds[index + 1]].reshape(-1)[: 2 * size]
        return own_rows(flat.reshape((2,) + shape), 0)

    own_pos, other_pos = unline(1, pos_tables.shape[1:])
    grad_pos = by_stream(own_pos[0], other_pos[0])
    own_vec, other_vec = unline(2, (7, vectors.shape[1]))
    pair_vec = by_stream(own_vec[0], other_vec[0])
    grad_vec = jnp.stack(
        [pair_vec[0, 0], pair_vec[0, 1]]
        + [pair_vec[0, 2], pair_vec[0, 3], pair_vec[1, 2], pair_vec[1, 3]]
        + [pair_vec[0, 4], pair_vec[0, 5], pair_vec[1, 4], pair_vec[1, 5]]
        + [pair_vec[0, 6], pair_vec[1, 6]]
    )
    own_bias, other_bias = unline(3, bias_in.shape[1:])
    grad_bias = by_stream(own_bias[0], other_bias[0])

    squares = jnp.sum(sum_out * sum_out) + jnp.sum(sum_in * sum_in) + jnp.sum(sum_attn * sum_attn)
    for grad in (grad_spatial, grad_pos, grad_vec, grad_bias):
        squares = squares + jnp.sum(grad * grad)
    tile = jnp.full((8, 128), squares, F32)
    tile = tile + swap(tile)
    around = tile
    for sy in range(ny):
        for sx in range(nx):
            if sy or sx:
                around = around + diagonal(tile, sy, sx)
    norm = around
    for k in range(1, nz):
        norm = norm + shift(around, "z", k)
    grad_norm = jnp.sqrt(norm[0, 0])
    factor = CLIP / jnp.maximum(grad_norm, CLIP)

    grad_attn = by_stream(*own_rows(sum_attn, 1))
    grad_in = by_stream(*own_rows(sum_in, 0))
    grad_out = by_stream(*own_rows(sum_out, 0))

    out_own, out_other = out[:count], swap(out[count:])
    grad_own, grad_other = grad_rows[:count], swap(grad_rows[count:])
    out_visual = mine_of(out_own, out_other)[None]
    out_text = mine_of(out_other, out_own)[None]
    grad_visual = mine_of(grad_own, grad_other)[None]
    grad_text = mine_of(grad_other, grad_own)[None]

    params = (attn_w, ffn_in, ffn_out, bias_in, vectors, pos_tables, spatial)
    grads = (grad_attn, grad_in, grad_out, grad_bias, grad_vec, grad_pos, grad_spatial)
    states = (
        (attn_mom, attn_sec), (in_mom, in_sec), (out_mom, out_sec), (bias_mom, bias_sec),
        (vec_mom, vec_sec), (pos_mom, pos_sec), (spatial_mom, spatial_sec),
    )
    rates = (RATE_ATTN, RATE_FEED, RATE_FEED, RATE_OTHER, RATE_OTHER, RATE_OTHER, RATE_OTHER)
    decays = (DECAY, DECAY, DECAY, 0.0, 0.0, 0.0, DECAY)
    results = [out_visual, out_text, grad_visual, grad_text, grad_norm]
    for index, (weight, grad, state, rate, decay) in enumerate(
        zip(params, grads, states, rates, decays)
    ):
        new = adam(weight, grad * factor, state[0], state[1], rate, decay)
        results.extend(new)
        if index < 3:
            results.append(new[2].astype(BF))
    return tuple(results)


def solution(mesh):
    devices = mesh.devices.reshape(-1)
    chips = devices.size // 2
    deep = 4 if chips % 4 == 0 else 1
    side = int(round((chips // deep) ** 0.5))
    if deep * side * side != chips:
        deep, side = chips, 1
    fine = Mesh(devices.reshape(deep, side, side, 2), AXES)
    every = AXES
    data = P(every, None, None)
    in_specs = (
        data, data, P(every), data, data, data,
        P(None, None, every, None), P(None, every, None), P(None, every, None),
        P(None, every), P(None, every), P(None, None, None, every), P(None, every, None),
        P(None, None, every, None), P(None, None, every, None),
        P(None, every, None), P(None, every, None), P(None, every, None), P(None, every, None),
        P(None, every), P(None, every), P(None, every), P(None, every),
        P(None, None, None, every), P(None, None, None, every),
        P(None, every, None), P(None, every, None),
    )
    weights = P(None, None, every, None)
    rows = P(None, every, None)
    flat = P(None, every)
    last = P(None, None, None, every)
    out_specs = (
        (data, data, data, data, P())
        + (weights,) * 4 + (rows,) * 8 + (flat,) * 6 + (last,) * 3 + (rows,) * 3
    )
    return jax.shard_map(body, mesh=fine, in_specs=in_specs, out_specs=out_specs, check_vma=False)
```

time: 2050 us -> 746 us (0.36)
  waiting for transfers between devices: 917 us -> 162 us
  local copies, waits for them, and re-layouts: 472 us -> 92.6 us
  blocking collectives: 236 us -> 0 us
  matrix products: 268 us -> 38.7 us
  starting transfers between devices: 0.76 us -> 186 us
  Pallas kernels: 0 us -> 156 us
  other arithmetic: 127 us -> 93.1 us
    reduce_scatter x3 -> x0, waiting for transfers between devices: 625 us -> none  [the longest x1 209 us: body(): lax.psum_scatter(grad_attn, 'dp', scatter_dimension=2, tiled=True)]
    unnamed x12 -> x0, waiting for transfers between devices: 292 us -> none
    dot_general x64 -> x11, matrix products: 268 us -> 38.7 us  [the longest x7 25.9 us: dot(): return jnp.dot(left, right, preferred_element_type=F32)]
    unnamed x382 -> x198, local copies, waits for them, and re-layouts: 206 us -> 11.3 us
    ppermute x0 -> x135, starting transfers between devices: none -> 186 us  [the longest x107 175 us: shift(): lax.ppermute(value, axis, [(i, (i + step) % size) for i in range(size)])]
    reshape x12 -> x18, local copies, waits for them, and re-layouts: 173 us -> 5.89 us  [the longest x6 3.38 us: lines(): return flat.reshape(chips, -1, width)]
    ppermute x0 -> x135, waiting for transfers between devices: none -> 162 us  [the longest x107 161 us: shift(): lax.ppermute(value, axis, [(i, (i + step) % size) for i in range(size)])]
    all_gather x4 -> x0, blocking collectives: 159 us -> none  [the longest x1 44.5 us: body(): lax.all_gather(vectors, 'dp', axis=1, tiled=True)]
  transfers between devices with their start and end apart: 9 -> 135, of which waited for: 6 -> 40; matrix products, arithmetic and copies ran while one was open for 21% -> 21% of each run, Pallas kernels for 0% -> 12%
where the time goes in v1:
time: 746 us; the launch traced here: 739 us
  starting transfers between devices  186 us (25%)
  waiting for transfers between devices  162 us (22%)
  Pallas kernels  156 us (21%)
  other arithmetic  93.1 us (12%)
  local copies, waits for them, and re-layouts  92.6 us (12%)
  matrix products  38.7 us (5%)
  between operations  10.3 us (1%)
    ppermute x107, starting transfers between devices, shift(): lax.ppermute(value, axis, [(i, (i + step) % size) for i in range(size)])  175 us
    ppermute x107, waiting for transfers between devices, shift(): lax.ppermute(value, axis, [(i, (i + step) % size) for i in range(size)])  161 us
    pallas_call x1, Pallas kernels, attend_back_call(): pl.pallas_call(attend_back_kernel, grid=(pairs, pages), in_specs=[pl.Bloc...  41.5 us
    pallas_call x1, Pallas kernels, attend_call(): pl.pallas_call(attend_kernel, grid=(pairs, pages), in_specs=[pl.BlockSpec...  27.9 us
    pallas_call x5, Pallas kernels, outer_call(): pl.pallas_call(outer_kernel, grid=(steps,), in_specs=[pl.BlockSpec(memory...  27 us
    dot_general x7, matrix products, dot(): return jnp.dot(left, right, preferred_element_type=F32)  25.9 us
    pallas_call x1, Pallas kernels, feed_back_call(): pl.pallas_call(feed_back_kernel, grid=(hidden // block,), in_specs=[pl.Bl...  25.4 us
    pallas_call x1, Pallas kernels, feed_call(): pl.pallas_call(feed_kernel, grid=(hidden // block,), in_specs=[pl.BlockSp...  20 us
  transfers between devices with their start and end apart: 135, of which 40 were waited for; matrix products, arithmetic and copies ran while one was open for 21% of the time, Pallas kernels for 12%

profile of v1, /device:TPU:0, one launch (start us, length us, event | category | flops | bytes accessed | tf_op | source)
XLA Modules:
  0.0 739.5 jit_solution(1893731856143362619)
XLA Ops:
  54.1 5.7 collective-permute-done.20
  70.0 7.9 %collective-permute-done.23.refs_7_ = bf16[4,2,48,768]{3,2,1,0:T(8,128)(2,1)} collective-permute-done((bf16[4,2,48,768]{3,2,1,0:T(8,128)(2,1)S(1)}, bf16[4,2,48,768]{3,2,1,0:T(8,128)(2,1)}, u32[]{:S(2)}, u32[]{:S(2)}) %collective-permute-start.23) | collective-permute-done | bytes 589856 | tf_op jit(solution)/shard_map/ppermute | solution.py:54
  84.9 5.6 collective-permute-done.16.refs_2_
  90.6 11.6 %collective-permute-done.18.refs_4_ = bf16[4,2,48,768]{3,2,1,0:T(8,128)(2,1)} collective-permute-done((bf16[4,2,48,768]{3,2,1,0:T(8,128)(2,1)}, bf16[4,2,48,768]{3,2,1,0:T(8,128)(2,1)}, u32[]{:S(2)}, u32[]{:S(2)}) %collective-permute-start.18) | collective-permute-done | bytes 589856 | tf_op jit(solution)/shard_map/ppermute | solution.py:54
  102.1 4.8 place.3
  114.9 3.8 convolution_convert_fusion.1.v_ref
  118.7 27.9 %attend.1 = (bf16[1024,768]{1,0:T(8,128)(2,1)}, f32[2,6,8,512]{3,2,1,0:T(8,128)}) custom-call(s32[2]{0:T(128)} %get-tuple-element.196.valid_ref, bf16[1024,768]{1,0:T(8,128)(2,1)} %fusion.15.q_ref, bf16[1024,768]{1,0:T(8,128)(2,1)} %convolution_convert_fusion.2.k_ref, bf16[1024,768]{1,0:T(8,128)(2,1)} %convolution_convert_fusion.1.v_ref, ...), custom_call_target="tpu_custom_call" | custom-call | tf_op jit(solution)/shard_map/attend/pallas_call | solution.py:280
  146.7 4.6 convolution_multiply_fusion
  160.6 5.6 collective-permute-done.41
  166.2 4.8 collective-permute-start.48
  171.0 5.2 collective-permute-start.27
  176.2 3.4 collective-permute-start.28
  179.6 5.2 collective-permute-done.47
  184.8 3.7 collective-permute-start.33
  188.5 3.8 collective-permute-start.34
  192.3 5.2 collective-permute-done.28
  208.9 5.1 collective-permute-done.44.refs_3_
  215.4 11.5 %collective-permute-done.50.refs_7_ = bf16[4,192,384]{2,1,0:T(8,128)(2,1)} collective-permute-done((bf16[4,192,384]{2,1,0:T(8,128)(2,1)S(1)}, bf16[4,192,384]{2,1,0:T(8,128)(2,1)}, u32[]{:S(2)}, u32[]{:S(2)}) %collective-permute-start.50) | collective-permute-done | bytes 589856 | tf_op jit(solution)/shard_map/ppermute | solution.py:54
  232.6 6.8 collective-permute-done.31.refs_3_
  244.1 12.1 %collective-permute-done.45.refs_4_ = bf16[4,192,384]{2,1,0:T(8,128)(2,1)} collective-permute-done((bf16[4,192,384]{2,1,0:T(8,128)(2,1)S(1)}, bf16[4,192,384]{2,1,0:T(8,128)(2,1)}, u32[]{:S(2)}, u32[]{:S(2)}) %collective-permute-start.45) | collective-permute-done | bytes 589856 | tf_op jit(solution)/shard_map/ppermute | solution.py:54
  267.8 4.9 place.5
  272.7 6.5 collective-permute-done.32.refs_4_
  279.2 4.9 place.4
  286.3 3.5 fusion.139
  291.9 20.0 %feed.1 = (bf16[1024,3072]{1,0:T(8,128)(2,1)}, bf16[1024,3072]{1,0:T(8,128)(2,1)}) custom-call(bf16[1024,768]{1,0:T(8,128)(2,1)} %fusion.7.rows_ref, bf16[768,3072]{1,0:T(8,128)(2,1)} %bitcast.507, f32[1,3072]{1,0:T(1,128)} %reshape.2066.bias_ref), custom_call_target="tpu_custom_call" | custom-call | tf_op jit(solution)/shard_map/feed/pallas_call | solution.py:451
  312.0 8.7 %copy.252 = bf16[1024,3072]{0,1:T(8,128)(2,1)} copy(bf16[1024,3072]{1,0:T(8,128)(2,1)} %get-tuple-element.41) | data formatting | bytes 12582912 | tf_op jit(solution)/shard_map/feed/pallas_call | solution.py:451
  320.7 8.8 %fusion.152 = (f32[1024]{0:T(1024)S(1)}, f32[1024,768]{1,0:T(8,128)S(1)}) fusion(f32[768]{0:T(1024)S(1)} %add.1480, bf16[1024,3072]{1,0:T(8,128)(2,1)} %get-tuple-element.41, bf16[3072,768]{1,0:T(8,128)(2,1)} %bitcast.512, f32[768]{0:T(1024)S(1)} %add.1475, f32[768]{0:T(1024)S(1)} %mul.881, f32[1024]{0:T(1024)S(1)} %add_rsqrt_fusion.1, ...), kind=kOutput, calls=%fused_computation.573 | convolution fusion | flops 4837342208 | bytes 17323008 | tf_op jit(solution)/shard_map/dot_general | solution.py:41
  331.8 3.6 multiply_reduce_fusion
  338.0 5.0 fusion.138
  343.0 25.4 %feed_back.1 = (f32[1024,768]{1,0:T(8,128)}, bf16[2,16,48,1536]{3,2,1,0:T(8,128)(2,1)}, f32[1,3072]{1,0:T(1,128)}) custom-call(s32[2,16]{1,0:T(2,128)} %pad_add_fusion.2.slots_ref, bf16[768,1024]{1,0:T(8,128)(2,1)} %copy.250.rows_t_ref, bf16[1024,768]{1,0:T(8,128)(2,1)} %get-tuple-element.192.low_ref.right_ref, bf16[3072,768]{1,0:T(8,128)(2,1)} %bitcast.513, ...), custom_call_target="tpu_custom_call" | custom-call | tf_op jit(solution)/shard_map/feed_back/pallas_call | solution.py:499
  375.5 9.8 %outer.5 = bf16[2,16,192,384]{3,2,1,0:T(8,128)(2,1)} custom-call(s32[2,16]{1,0:T(2,128)} %pad_add_fusion.2.slots_ref, bf16[3072,1024]{1,0:T(8,128)(2,1)} %bitcast.509, bf16[1024,768]{1,0:T(8,128)(2,1)} %get-tuple-element.192.low_ref.right_ref), custom_call_target="tpu_custom_call" | custom-call | tf_op jit(solution)/shard_map/outer/pallas_call | solution.py:544
  385.3 3.5 slice_bitcast_fusion.2
  411.8 16.1 %collective-permute-done.56 = bf16[8,192,384]{2,1,0:T(8,128)(2,1)} collective-permute-done((bf16[8,192,384]{2,1,0:T(8,128)(2,1)}, bf16[8,192,384]{2,1,0:T(8,128)(2,1)}, u32[]{:S(2)}, u32[]{:S(2)}) %collective-permute-start.56) | collective-permute-done | bytes 1179680 | tf_op jit(solution)/shard_map/ppermute | solution.py:54
  434.0 6.4 collective-permute-done.72
  443.8 3.9 collective-permute-start.74
  453.4 6.3 collective-permute-start.69
  460.5 9.8 %collective-permute-start.58 = (bf16[192,384]{1,0:T(8,128)(2,1)S(1)}, bf16[192,384]{1,0:T(8,128)(2,1)S(1)}, u32[]{:S(2)}, u32[]{:S(2)}) collective-permute-start(bf16[192,384]{1,0:T(8,128)(2,1)S(1)} %get-tuple-element.253), channel_id=1, source_target_pairs={{0,8},{8,16},{16,24},{24,0},{1,9},{9,17},{17,25},{25,1},{2,10},{10... | collective-permute-start | bytes 442376 | tf_op jit(solution)/shard_map/ppermute | solution.py:54
  470.6 7.2 collective-permute-done.69
  477.8 5.6 collective-permute-start.63
  483.8 3.9 collective-permute-done.59
  490.1 4.6 collective-permute-done.64
  507.0 41.5 %attend_back.1 = (bf16[1024,768]{1,0:T(8,128)(2,1)}, bf16[1024,768]{1,0:T(8,128)(2,1)}, bf16[1024,768]{1,0:T(8,128)(2,1)}, f32[12,8,512]{2,1,0:T(8,128)}) custom-call(s32[2]{0:T(128)} %get-tuple-element.196.valid_ref, bf16[1024,768]{1,0:T(8,128)(2,1)} %fusion.15.q_ref, bf16[1024,768]{1,0:T(8,128)(2,1)} %convolution_convert_fusion.2.k_ref, ...), custom_call_target="tpu_custom_call" | custom-call | tf_op jit(solution)/shard_map/attend_back/pallas_call | solution.py:392
  574.9 5.3 fusion.127
  586.5 4.3 outer.9
  595.1 4.3 outer.8
  601.6 4.3 outer.7
  607.1 4.3 outer.6
  638.5 3.8 collective-permute-start.118
  (799 shorter events, 349.0 us)
Async XLA Ops:
  2.7 32.7 %collective-permute-start.39 = (bf16[96,768]{1,0:T(8,128)(2,1)}, bf16[96,768]{1,0:T(8,128)(2,1)}, u32[]{:S(2)}, u32[]{:S(2)}) collective-permute-start(bf16[96,768]{1,0:T(8,128)(2,1)} %get-tuple-element.264), channel_id=1, source_target_pairs={{0,1},{1,0},{2,3},{3,2},{4,5},{5,4},{6,7},{7,6},{8,9},{9,8},{10,11... | collective-permute-start | bytes 442376 | tf_op jit(solution)/shard_map/ppermute | solution.py:49
  43.3 16.5 %collective-permute-start.20 = (bf16[2,48,768]{2,1,0:T(8,128)(2,1)}, bf16[2,48,768]{2,1,0:T(8,128)(2,1)S(1)}, u32[]{:S(2)}, u32[]{:S(2)}) collective-permute-start(bf16[2,48,768]{2,1,0:T(8,128)(2,1)} %get-tuple-element.273), channel_id=1, source_target_pairs={{0,16},{8,24},{16,0},{24,8},{1,17},{9,25},{17,1},{25,9},{2,18},{10... | collective-permute-start | bytes 442376 | tf_op jit(solution)/shard_map/ppermute | solution.py:54
  51.4 31.3 %collective-permute-start = (bf16[512,768]{1,0:T(8,128)(2,1)}, bf16[512,768]{1,0:T(8,128)(2,1)}, u32[]{:S(2)}, u32[]{:S(2)}) collective-permute-start(bf16[512,768]{1,0:T(8,128)(2,1)} %get-tuple-element.224), channel_id=1, source_target_pairs={{0,1},{1,0},{2,3},{3,2},{4,5},{5,4},{6,7},{7,6},{8,9},{9,8},{10,11... | collective-permute-start | bytes 2359304 | tf_op jit(solution)/shard_map/ppermute | solution.py:49
  66.1 24.5 %collective-permute-start.16 = (bf16[4,2,48,768]{3,2,1,0:T(8,128)(2,1)S(1)}, bf16[4,2,48,768]{3,2,1,0:T(8,128)(2,1)}, u32[]{:S(2)}, u32[]{:S(2)}) collective-permute-start(bf16[4,2,48,768]{3,2,1,0:T(8,128)(2,1)S(1)} %pad_maximum_fusion.3.refs_1_), channel_id=1, source_target_pairs={{0,4},{4,0},{1,5},{5,1},{2,6},{6,2},{3,7},{7,3},{8,12},{12,8},{9,1... | collective-permute-start | bytes 1769480 | tf_op jit(solution)/shard_map/ppermute | solution.py:54
  66.7 23.9 %collective-permute-start.22 = (bf16[4,2,48,768]{3,2,1,0:T(8,128)(2,1)S(1)}, bf16[4,2,48,768]{3,2,1,0:T(8,128)(2,1)}, u32[]{:S(2)}, u32[]{:S(2)}) collective-permute-start(bf16[4,2,48,768]{3,2,1,0:T(8,128)(2,1)S(1)} %pad_maximum_fusion.4.refs_5_), channel_id=1, source_target_pairs={{0,2},{2,0},{1,3},{3,1},{4,6},{6,4},{5,7},{7,5},{8,10},{10,8},{9,1... | collective-permute-start | bytes 1769480 | tf_op jit(solution)/shard_map/ppermute | solution.py:54
  68.5 33.7 %collective-permute-start.18 = (bf16[4,2,48,768]{3,2,1,0:T(8,128)(2,1)}, bf16[4,2,48,768]{3,2,1,0:T(8,128)(2,1)}, u32[]{:S(2)}, u32[]{:S(2)}) collective-permute-start(bf16[4,2,48,768]{3,2,1,0:T(8,128)(2,1)} %collective-permute-done.17.refs_3_), channel_id=1, source_target_pairs={{0,4},{4,0},{1,5},{5,1},{2,6},{6,2},{3,7},{7,3},{8,12},{12,8},{9,1... | collective-permute-start | bytes 1769480 | tf_op jit(solution)/shard_map/ppermute | solution.py:54
  77.9 24.2 %collective-permute-start.24 = (bf16[4,2,48,768]{3,2,1,0:T(8,128)(2,1)}, bf16[4,2,48,768]{3,2,1,0:T(8,128)(2,1)}, u32[]{:S(2)}, u32[]{:S(2)}) collective-permute-start(bf16[4,2,48,768]{3,2,1,0:T(8,128)(2,1)} %collective-permute-done.23.refs_7_), channel_id=1, source_target_pairs={{0,2},{2,0},{1,3},{3,1},{4,6},{6,4},{5,7},{7,5},{8,10},{10,8},{9,1... | collective-permute-start | bytes 1769480 | tf_op jit(solution)/shard_map/ppermute | solution.py:54
  82.7 74.2 %collective-permute-start.26 = (bf16[24,3072]{1,0:T(8,128)(2,1)}, bf16[24,3072]{1,0:T(8,128)(2,1)S(1)}, u32[]{:S(2)}, u32[]{:S(2)}) collective-permute-start(bf16[24,3072]{1,0:T(8,128)(2,1)} %get-tuple-element.270), channel_id=1, source_target_pairs={{0,1},{1,0},{2,3},{3,2},{4,5},{5,4},{6,7},{7,6},{8,9},{9,8},{10,11... | collective-permute-start | bytes 442376 | tf_op jit(solution)/shard_map/ppermute | solution.py:49
  151.2 132.8 %collective-permute-start.25 = (f32[1024,768]{1,0:T(8,128)}, f32[1024,768]{1,0:T(8,128)}, u32[]{:S(2)}, u32[]{:S(2)}) collective-permute-start(f32[1024,768]{1,0:T(8,128)} %convolution_multiply_fusion), channel_id=1, source_target_pairs={{0,1},{1,0},{2,3},{3,2},{4,5},{5,4},{6,7},{7,6},{8,9},{9,8},{10,11... | collective-permute-start | bytes 9437192 | tf_op jit(solution)/shard_map/ppermute | solution.py:49
  154.5 16.5 %collective-permute-start.42 = (bf16[192,384]{1,0:T(8,128)(2,1)S(1)}, bf16[192,384]{1,0:T(8,128)(2,1)S(1)}, u32[]{:S(2)}, u32[]{:S(2)}) collective-permute-start(bf16[192,384]{1,0:T(8,128)(2,1)S(1)} %get-tuple-element.262), channel_id=1, source_target_pairs={{0,24},{8,0},{16,8},{24,16},{1,25},{9,1},{17,9},{25,17},{2,26},{10... | collective-permute-start | bytes 442376 | tf_op jit(solution)/shard_map/ppermute | solution.py:54
  156.9 19.3 %collective-permute-start.46 = (bf16[192,384]{1,0:T(8,128)(2,1)S(1)}, bf16[192,384]{1,0:T(8,128)(2,1)S(1)}, u32[]{:S(2)}, u32[]{:S(2)}) collective-permute-start(bf16[192,384]{1,0:T(8,128)(2,1)S(1)} %get-tuple-element.261), channel_id=1, source_target_pairs={{0,8},{8,16},{16,24},{24,0},{1,9},{9,17},{17,25},{25,1},{2,10},{10... | collective-permute-start | bytes 442376 | tf_op jit(solution)/shard_map/ppermute | solution.py:54
  159.9 24.9 %collective-permute-start.47 = (bf16[192,384]{1,0:T(8,128)(2,1)S(1)}, bf16[192,384]{1,0:T(8,128)(2,1)S(1)}, u32[]{:S(2)}, u32[]{:S(2)}) collective-permute-start(bf16[192,384]{1,0:T(8,128)(2,1)S(1)} %get-tuple-element.261), channel_id=1, source_target_pairs={{0,16},{8,24},{16,0},{24,8},{1,17},{9,25},{17,1},{25,9},{2,18},{10... | collective-permute-start | bytes 442376 | tf_op jit(solution)/shard_map/ppermute | solution.py:54
  166.2 18.6 %collective-permute-start.48 = (bf16[192,384]{1,0:T(8,128)(2,1)S(1)}, bf16[192,384]{1,0:T(8,128)(2,1)S(1)}, u32[]{:S(2)}, u32[]{:S(2)}) collective-permute-start(bf16[192,384]{1,0:T(8,128)(2,1)S(1)} %get-tuple-element.261), channel_id=1, source_target_pairs={{0,24},{8,0},{16,8},{24,16},{1,25},{9,1},{17,9},{25,17},{2,26},{10... | collective-permute-start | bytes 442376 | tf_op jit(solution)/shard_map/ppermute | solution.py:54
  171.0 17.5 %collective-permute-start.27 = (bf16[48,1536]{1,0:T(8,128)(2,1)S(1)}, bf16[48,1536]{1,0:T(8,128)(2,1)S(1)}, u32[]{:S(2)}, u32[]{:S(2)}) collective-permute-start(bf16[48,1536]{1,0:T(8,128)(2,1)S(1)} %get-tuple-element.268), channel_id=1, source_target_pairs={{0,8},{8,16},{16,24},{24,0},{1,9},{9,17},{17,25},{25,1},{2,10},{10... | collective-permute-start | bytes 442376 | tf_op jit(solution)/shard_map/ppermute | solution.py:54
  176.2 21.3 %collective-permute-start.28 = (bf16[48,1536]{1,0:T(8,128)(2,1)S(1)}, bf16[48,1536]{1,0:T(8,128)(2,1)S(1)}, u32[]{:S(2)}, u32[]{:S(2)}) collective-permute-start(bf16[48,1536]{1,0:T(8,128)(2,1)S(1)} %get-tuple-element.268), channel_id=1, source_target_pairs={{0,16},{8,24},{16,0},{24,8},{1,17},{9,25},{17,1},{25,9},{2,18},{10... | collective-permute-start | bytes 442376 | tf_op jit(solution)/shard_map/ppermute | solution.py:54
  199.2 29.2 %collective-permute-start.43 = (bf16[4,192,384]{2,1,0:T(8,128)(2,1)S(1)}, bf16[4,192,384]{2,1,0:T(8,128)(2,1)S(1)}, u32[]{:S(2)}, u32[]{:S(2)}) collective-permute-start(bf16[4,192,384]{2,1,0:T(8,128)(2,1)S(1)} %pad_maximum_fusion.7.refs_1_), channel_id=1, source_target_pairs={{0,4},{4,0},{1,5},{5,1},{2,6},{6,2},{3,7},{7,3},{8,12},{12,8},{9,1... | collective-permute-start | bytes 1769480 | tf_op jit(solution)/shard_map/ppermute | solution.py:54
  203.8 23.1 %collective-permute-start.50 = (bf16[4,192,384]{2,1,0:T(8,128)(2,1)S(1)}, bf16[4,192,384]{2,1,0:T(8,128)(2,1)}, u32[]{:S(2)}, u32[]{:S(2)}) collective-permute-start(bf16[4,192,384]{2,1,0:T(8,128)(2,1)S(1)} %pad_maximum_fusion.8.refs_5_), channel_id=1, source_target_pairs={{0,4},{4,0},{1,5},{5,1},{2,6},{6,2},{3,7},{7,3},{8,12},{12,8},{9,1... | collective-permute-start | bytes 1769480 | tf_op jit(solution)/shard_map/ppermute | solution.py:54
  206.3 22.6 %collective-permute-start.49 = (bf16[4,192,384]{2,1,0:T(8,128)(2,1)S(1)}, bf16[4,192,384]{2,1,0:T(8,128)(2,1)S(1)}, u32[]{:S(2)}, u32[]{:S(2)}) collective-permute-start(bf16[4,192,384]{2,1,0:T(8,128)(2,1)S(1)} %pad_maximum_fusion.8.refs_5_), channel_id=1, source_target_pairs={{0,2},{2,0},{1,3},{3,1},{4,6},{6,4},{5,7},{7,5},{8,10},{10,8},{9,1... | collective-permute-start | bytes 1769480 | tf_op jit(solution)/shard_map/ppermute | solution.py:54
  214.0 25.4 %collective-permute-start.31 = (bf16[4,48,1536]{2,1,0:T(8,128)(2,1)S(1)}, bf16[4,48,1536]{2,1,0:T(8,128)(2,1)}, u32[]{:S(2)}, u32[]{:S(2)}) collective-permute-start(bf16[4,48,1536]{2,1,0:T(8,128)(2,1)S(1)} %pad_maximum_fusion.5.refs_1_), channel_id=1, source_target_pairs={{0,2},{2,0},{1,3},{3,1},{4,6},{6,4},{5,7},{7,5},{8,10},{10,8},{9,1... | collective-permute-start | bytes 1769480 | tf_op jit(solution)/shard_map/ppermute | solution.py:54
  226.9 16.6 %collective-permute-start.37 = (bf16[4,48,1536]{2,1,0:T(8,128)(2,1)}, bf16[4,48,1536]{2,1,0:T(8,128)(2,1)}, u32[]{:S(2)}, u32[]{:S(2)}) collective-permute-start(bf16[4,48,1536]{2,1,0:T(8,128)(2,1)} %pad_maximum_fusion.6.refs_5_), channel_id=1, source_target_pairs={{0,4},{4,0},{1,5},{5,1},{2,6},{6,2},{3,7},{7,3},{8,12},{12,8},{9,1... | collective-permute-start | bytes 1769480 | tf_op jit(solution)/shard_map/ppermute | solution.py:54
  228.4 27.7 %collective-permute-start.45 = (bf16[4,192,384]{2,1,0:T(8,128)(2,1)S(1)}, bf16[4,192,384]{2,1,0:T(8,128)(2,1)}, u32[]{:S(2)}, u32[]{:S(2)}) collective-permute-start(bf16[4,192,384]{2,1,0:T(8,128)(2,1)S(1)} %collective-permute-done.44.refs_3_), channel_id=1, source_target_pairs={{0,4},{4,0},{1,5},{5,1},{2,6},{6,2},{3,7},{7,3},{8,12},{12,8},{9,1... | collective-permute-start | bytes 1769480 | tf_op jit(solution)/shard_map/ppermute | solution.py:54
  229.8 27.9 %collective-permute-start.51 = (bf16[4,192,384]{2,1,0:T(8,128)(2,1)}, bf16[4,192,384]{2,1,0:T(8,128)(2,1)}, u32[]{:S(2)}, u32[]{:S(2)}) collective-permute-start(bf16[4,192,384]{2,1,0:T(8,128)(2,1)} %collective-permute-done.50.refs_7_), channel_id=1, source_target_pairs={{0,2},{2,0},{1,3},{3,1},{4,6},{6,4},{5,7},{7,5},{8,10},{10,8},{9,1... | collective-permute-start | bytes 1769480 | tf_op jit(solution)/shard_map/ppermute | solution.py:54
  239.3 33.3 %collective-permute-start.30 = (bf16[4,48,1536]{2,1,0:T(8,128)(2,1)S(1)}, bf16[4,48,1536]{2,1,0:T(8,128)(2,1)}, u32[]{:S(2)}, u32[]{:S(2)}) collective-permute-start(bf16[4,48,1536]{2,1,0:T(8,128)(2,1)S(1)} %pad_maximum_fusion.5.refs_1_), channel_id=1, source_target_pairs={{0,4},{4,0},{1,5},{5,1},{2,6},{6,2},{3,7},{7,3},{8,12},{12,8},{9,1... | collective-permute-start | bytes 1769480 | tf_op jit(solution)/shard_map/ppermute | solution.py:54
  243.5 29.2 %collective-permute-start.36 = (bf16[4,48,1536]{2,1,0:T(8,128)(2,1)}, bf16[4,48,1536]{2,1,0:T(8,128)(2,1)}, u32[]{:S(2)}, u32[]{:S(2)}) collective-permute-start(bf16[4,48,1536]{2,1,0:T(8,128)(2,1)} %pad_maximum_fusion.6.refs_5_), channel_id=1, source_target_pairs={{0,2},{2,0},{1,3},{3,1},{4,6},{6,4},{5,7},{7,5},{8,10},{10,8},{9,1... | collective-permute-start | bytes 1769480 | tf_op jit(solution)/shard_map/ppermute | solution.py:54
  256.1 23.1 %collective-permute-start.32 = (bf16[4,48,1536]{2,1,0:T(8,128)(2,1)}, bf16[4,48,1536]{2,1,0:T(8,128)(2,1)}, u32[]{:S(2)}, u32[]{:S(2)}) collective-permute-start(bf16[4,48,1536]{2,1,0:T(8,128)(2,1)} %collective-permute-done.31.refs_3_), channel_id=1, source_target_pairs={{0,4},{4,0},{1,5},{5,1},{2,6},{6,2},{3,7},{7,3},{8,12},{12,8},{9,1... | collective-permute-start | bytes 1769480 | tf_op jit(solution)/shard_map/ppermute | solution.py:54
  257.7 21.5 %collective-permute-start.38 = (bf16[4,48,1536]{2,1,0:T(8,128)(2,1)}, bf16[4,48,1536]{2,1,0:T(8,128)(2,1)}, u32[]{:S(2)}, u32[]{:S(2)}) collective-permute-start(bf16[4,48,1536]{2,1,0:T(8,128)(2,1)} %collective-permute-done.37.refs_7_), channel_id=1, source_target_pairs={{0,2},{2,0},{1,3},{3,1},{4,6},{6,4},{5,7},{7,5},{8,10},{10,8},{9,1... | collective-permute-start | bytes 1769480 | tf_op jit(solution)/shard_map/ppermute | solution.py:54
  272.7 59.1 %collective-permute-start.53 = (bf16[512,768]{1,0:T(8,128)(2,1)}, bf16[512,768]{1,0:T(8,128)(2,1)}, u32[]{:S(2)}, u32[]{:S(2)}) collective-permute-start(bf16[512,768]{1,0:T(8,128)(2,1)} %get-tuple-element.222), channel_id=1, source_target_pairs={{0,1},{1,0},{2,3},{3,2},{4,5},{5,4},{6,7},{7,6},{8,9},{9,8},{10,11... | collective-permute-start | bytes 2359304 | tf_op jit(solution)/shard_map/ppermute | solution.py:49
  373.4 29.2 %collective-permute-start.66 = (bf16[8,48,1536]{2,1,0:T(8,128)(2,1)}, bf16[8,48,1536]{2,1,0:T(8,128)(2,1)}, u32[]{:S(2)}, u32[]{:S(2)}) collective-permute-start(bf16[8,48,1536]{2,1,0:T(8,128)(2,1)} %get-tuple-element.201), channel_id=1, source_target_pairs={{0,2},{2,0},{1,3},{3,1},{4,6},{6,4},{5,7},{7,5},{8,10},{10,8},{9,1... | collective-permute-start | bytes 3538952 | tf_op jit(solution)/shard_map/ppermute | solution.py:54
  374.0 29.2 %collective-permute-start.71 = (bf16[8,48,1536]{2,1,0:T(8,128)(2,1)}, bf16[8,48,1536]{2,1,0:T(8,128)(2,1)}, u32[]{:S(2)}, u32[]{:S(2)}) collective-permute-start(bf16[8,48,1536]{2,1,0:T(8,128)(2,1)} %get-tuple-element.200), channel_id=1, source_target_pairs={{0,4},{4,0},{1,5},{5,1},{2,6},{6,2},{3,7},{7,3},{8,12},{12,8},{9,1... | collective-permute-start | bytes 3538952 | tf_op jit(solution)/shard_map/ppermute | solution.py:54
  388.8 39.1 %collective-permute-start.56 = (bf16[8,192,384]{2,1,0:T(8,128)(2,1)}, bf16[8,192,384]{2,1,0:T(8,128)(2,1)}, u32[]{:S(2)}, u32[]{:S(2)}) collective-permute-start(bf16[8,192,384]{2,1,0:T(8,128)(2,1)} %get-tuple-element.204), channel_id=1, source_target_pairs={{0,2},{2,0},{1,3},{3,1},{4,6},{6,4},{5,7},{7,5},{8,10},{10,8},{9,1... | collective-permute-start | bytes 3538952 | tf_op jit(solution)/shard_map/ppermute | solution.py:54
  390.3 38.2 %collective-permute-start.61 = (bf16[8,192,384]{2,1,0:T(8,128)(2,1)}, bf16[8,192,384]{2,1,0:T(8,128)(2,1)}, u32[]{:S(2)}, u32[]{:S(2)}) collective-permute-start(bf16[8,192,384]{2,1,0:T(8,128)(2,1)} %get-tuple-element.205), channel_id=1, source_target_pairs={{0,4},{4,0},{1,5},{5,1},{2,6},{6,2},{3,7},{7,3},{8,12},{12,8},{9,1... | collective-permute-start | bytes 3538952 | tf_op jit(solution)/shard_map/ppermute | solution.py:54
  402.6 97.6 %collective-permute-start.54 = (f32[1024,768]{1,0:T(8,128)}, f32[1024,768]{1,0:T(8,128)}, u32[]{:S(2)}, u32[]{:S(2)}) collective-permute-start(f32[1024,768]{1,0:T(8,128)} %subtract_multiply_fusion), channel_id=1, source_target_pairs={{0,1},{1,0},{2,3},{3,2},{4,5},{5,4},{6,7},{7,6},{8,9},{9,8},{10,11... | collective-permute-start | bytes 9437192 | tf_op jit(solution)/shard_map/ppermute | solution.py:49
  406.3 34.2 %collective-permute-start.72 = (bf16[4,48,1536]{2,1,0:T(8,128)(2,1)S(1)}, bf16[4,48,1536]{2,1,0:T(8,128)(2,1)S(1)}, u32[]{:S(2)}, u32[]{:S(2)}) collective-permute-start(bf16[4,48,1536]{2,1,0:T(8,128)(2,1)S(1)} %slice.1094), channel_id=1, source_target_pairs={{0,2},{2,0},{1,3},{3,1},{4,6},{6,4},{5,7},{7,5},{8,10},{10,8},{9,1... | collective-permute-start | bytes 1769480 | tf_op jit(solution)/shard_map/ppermute | solution.py:54
  410.2 33.6 %collective-permute-start.67 = (bf16[4,48,1536]{2,1,0:T(8,128)(2,1)S(1)}, bf16[4,48,1536]{2,1,0:T(8,128)(2,1)S(1)}, u32[]{:S(2)}, u32[]{:S(2)}) collective-permute-start(bf16[4,48,1536]{2,1,0:T(8,128)(2,1)S(1)} %slice.1088), channel_id=1, source_target_pairs={{0,4},{4,0},{1,5},{5,1},{2,6},{6,2},{3,7},{7,3},{8,12},{12,8},{9,1... | collective-permute-start | bytes 1769480 | tf_op jit(solution)/shard_map/ppermute | solution.py:54
  430.8 19.4 %collective-permute-start.57 = (bf16[4,192,384]{2,1,0:T(8,128)(2,1)S(1)}, bf16[4,192,384]{2,1,0:T(8,128)(2,1)S(1)}, u32[]{:S(2)}, u32[]{:S(2)}) collective-permute-start(bf16[4,192,384]{2,1,0:T(8,128)(2,1)S(1)} %slice.1074), channel_id=1, source_target_pairs={{0,4},{4,0},{1,5},{5,1},{2,6},{6,2},{3,7},{7,3},{8,12},{12,8},{9,1... | collective-permute-start | bytes 1769480 | tf_op jit(solution)/shard_map/ppermute | solution.py:54
  432.5 19.0 %collective-permute-start.62 = (bf16[4,192,384]{2,1,0:T(8,128)(2,1)S(1)}, bf16[4,192,384]{2,1,0:T(8,128)(2,1)S(1)}, u32[]{:S(2)}, u32[]{:S(2)}) collective-permute-start(bf16[4,192,384]{2,1,0:T(8,128)(2,1)S(1)} %slice.1082), channel_id=1, source_target_pairs={{0,2},{2,0},{1,3},{3,1},{4,6},{6,4},{5,7},{7,5},{8,10},{10,8},{9,1... | collective-permute-start | bytes 1769480 | tf_op jit(solution)/shard_map/ppermute | solution.py:54
  451.5 18.9 %collective-permute-start.68 = (bf16[48,1536]{1,0:T(8,128)(2,1)S(1)}, bf16[48,1536]{1,0:T(8,128)(2,1)S(1)}, u32[]{:S(2)}, u32[]{:S(2)}) collective-permute-start(bf16[48,1536]{1,0:T(8,128)(2,1)S(1)} %get-tuple-element.250), channel_id=1, source_target_pairs={{0,8},{8,16},{16,24},{24,0},{1,9},{9,17},{17,25},{25,1},{2,10},{10... | collective-permute-start | bytes 442376 | tf_op jit(solution)/shard_map/ppermute | solution.py:54
  453.4 24.5 %collective-permute-start.69 = (bf16[48,1536]{1,0:T(8,128)(2,1)S(1)}, bf16[48,1536]{1,0:T(8,128)(2,1)S(1)}, u32[]{:S(2)}, u32[]{:S(2)}) collective-permute-start(bf16[48,1536]{1,0:T(8,128)(2,1)S(1)} %get-tuple-element.252), channel_id=1, source_target_pairs={{0,16},{8,24},{16,0},{24,8},{1,17},{9,25},{17,1},{25,9},{2,18},{10... | collective-permute-start | bytes 442376 | tf_op jit(solution)/shard_map/ppermute | solution.py:54
  459.6 18.2 %collective-permute-start.70 = (bf16[48,1536]{1,0:T(8,128)(2,1)S(1)}, bf16[48,1536]{1,0:T(8,128)(2,1)S(1)}, u32[]{:S(2)}, u32[]{:S(2)}) collective-permute-start(bf16[48,1536]{1,0:T(8,128)(2,1)S(1)} %get-tuple-element.251), channel_id=1, source_target_pairs={{0,24},{8,0},{16,8},{24,16},{1,25},{9,1},{17,9},{25,17},{2,26},{10... | collective-permute-start | bytes 442376 | tf_op jit(solution)/shard_map/ppermute | solution.py:54
  460.5 23.1 %collective-permute-start.58 = (bf16[192,384]{1,0:T(8,128)(2,1)S(1)}, bf16[192,384]{1,0:T(8,128)(2,1)S(1)}, u32[]{:S(2)}, u32[]{:S(2)}) collective-permute-start(bf16[192,384]{1,0:T(8,128)(2,1)S(1)} %get-tuple-element.253), channel_id=1, source_target_pairs={{0,8},{8,16},{16,24},{24,0},{1,9},{9,17},{17,25},{25,1},{2,10},{10... | collective-permute-start | bytes 442376 | tf_op jit(solution)/shard_map/ppermute | solution.py:54
  470.4 17.2 %collective-permute-start.59 = (bf16[192,384]{1,0:T(8,128)(2,1)S(1)}, bf16[192,384]{1,0:T(8,128)(2,1)S(1)}, u32[]{:S(2)}, u32[]{:S(2)}) collective-permute-start(bf16[192,384]{1,0:T(8,128)(2,1)S(1)} %get-tuple-element.255), channel_id=1, source_target_pairs={{0,16},{8,24},{16,0},{24,8},{1,17},{9,25},{17,1},{25,9},{2,18},{10... | collective-permute-start | bytes 442376 | tf_op jit(solution)/shard_map/ppermute | solution.py:54
  585.9 29.9 %collective-permute-start.116 = (bf16[8,24,768]{2,1,0:T(8,128)(2,1)S(1)}, bf16[8,24,768]{2,1,0:T(8,128)(2,1)S(1)}, u32[]{:S(2)}, u32[]{:S(2)}) collective-permute-start(bf16[8,24,768]{2,1,0:T(8,128)(2,1)S(1)} %slice.1174), channel_id=1, source_target_pairs={{0,2},{2,0},{1,3},{3,1},{4,6},{6,4},{5,7},{7,5},{8,10},{10,8},{9,1... | collective-permute-start | bytes 884744 | tf_op jit(solution)/shard_map/ppermute | solution.py:54
  592.0 20.6 %collective-permute-start.106 = (bf16[8,48,384]{2,1,0:T(8,128)(2,1)S(1)}, bf16[8,48,384]{2,1,0:T(8,128)(2,1)S(1)}, u32[]{:S(2)}, u32[]{:S(2)}) collective-permute-start(bf16[8,48,384]{2,1,0:T(8,128)(2,1)S(1)} %get-tuple-element.227), channel_id=1, source_target_pairs={{0,2},{2,0},{1,3},{3,1},{4,6},{6,4},{5,7},{7,5},{8,10},{10,8},{9,1... | collective-permute-start | bytes 884744 | tf_op jit(solution)/shard_map/ppermute | solution.py:54
  593.5 20.6 %collective-permute-start.111 = (bf16[8,48,384]{2,1,0:T(8,128)(2,1)S(1)}, bf16[8,48,384]{2,1,0:T(8,128)(2,1)S(1)}, u32[]{:S(2)}, u32[]{:S(2)}) collective-permute-start(bf16[8,48,384]{2,1,0:T(8,128)(2,1)S(1)} %get-tuple-element.228), channel_id=1, source_target_pairs={{0,4},{4,0},{1,5},{5,1},{2,6},{6,2},{3,7},{7,3},{8,12},{12,8},{9,1... | collective-permute-start | bytes 884744 | tf_op jit(solution)/shard_map/ppermute | solution.py:54
  692.9 17.0 %collective-permute-start.126 = (f32[8,128]{1,0:T(8,128)}, f32[8,128]{1,0:T(8,128)}, u32[]{:S(2)}, u32[]{:S(2)}) collective-permute-start(f32[8,128]{1,0:T(8,128)} %broadcast_add_fusion), channel_id=1, source_target_pairs={{0,2},{2,0},{4,6},{6,4},{1,3},{3,1},{5,7},{7,5},{8,10},{10,8},{12,... | collective-permute-start | bytes 12296 | tf_op jit(solution)/shard_map/ppermute | solution.py:64
  693.5 16.5 %collective-permute-start.127 = (f32[8,128]{1,0:T(8,128)}, f32[8,128]{1,0:T(8,128)}, u32[]{:S(2)}, u32[]{:S(2)}) collective-permute-start(f32[8,128]{1,0:T(8,128)} %broadcast_add_fusion), channel_id=1, source_target_pairs={{0,4},{2,6},{4,0},{6,2},{1,5},{3,7},{5,1},{7,3},{8,12},{10,14},{12... | collective-permute-start | bytes 12296 | tf_op jit(solution)/shard_map/ppermute | solution.py:64
  698.6 30.3 %collective-permute-start.134 = (f32[96,768]{1,0:T(8,128)}, f32[96,768]{1,0:T(8,128)}, u32[]{:S(2)}, u32[]{:S(2)}) collective-permute-start(f32[96,768]{1,0:T(8,128)} %bitcast.273), channel_id=1, source_target_pairs={{0,1},{1,0},{2,3},{3,2},{4,5},{5,4},{6,7},{7,6},{8,9},{9,8},{10,11... | collective-permute-start | bytes 884744 | tf_op jit(solution)/shard_map/ppermute | solution.py:49
  716.1 18.7 %collective-permute-start.55 = (f32[512,768]{1,0:T(8,128)}, f32[512,768]{1,0:T(8,128)}, u32[]{:S(2)}, u32[]{:S(2)}) collective-permute-start(f32[512,768]{1,0:T(8,128)} %slice.1070), channel_id=1, source_target_pairs={{0,1},{1,0},{2,3},{3,2},{4,5},{5,4},{6,7},{7,6},{8,9},{9,8},{10,11... | collective-permute-start | bytes 4718600 | tf_op jit(solution)/shard_map/ppermute | solution.py:49
  (171 other events, 2429.8 us)

commit v2 on v1

--- a/solution.py
+++ b/solution.py
@@ -32,9 +32,18 @@
 F32 = jnp.float32
 AXES = ("z", "y", "x", "c")
 CHIP = ("z", "y", "x")
-FEED_BLOCK = 512
 VMEM_LIMIT = 56 * 1024 * 1024
 NT = (((1,), (1,)), ((), ()))
+
+
+def cost(microseconds):
+    return pl.CostEstimate(
+        flops=int(microseconds * 1.1e9), bytes_accessed=int(microseconds * 3.5e6), transcendentals=0
+    )
+
+
+def params_of():
+    return pltpu.CompilerParams(vmem_limit_bytes=VMEM_LIMIT)
 
 
 def dot(left, right):
@@ -64,6 +73,10 @@
     return lax.ppermute(value, ("y", "x"), pairs)
 
 
+def after(value, others):
+    return lax.optimization_barrier((value, others))[0]
+
+
 def chip_of(dz, dy, dx):
     nz, ny, nx = (lax.axis_size(a) for a in CHIP)
     z = (lax.axis_index("z") - dz) % nz
@@ -72,76 +85,87 @@
     return (z * ny + y) * nx + x
 
 
-def gather_pieces(piece, order):
+def around(value):
+    steps = [(y, x) for y in range(lax.axis_size("y")) for x in range(lax.axis_size("x"))]
+    return [value] + [diagonal(value, sy, sx) for sy, sx in steps[1:]]
+
+
+def plane_steps():
+    return [(y, x) for y in range(lax.axis_size("y")) for x in range(lax.axis_size("x"))]
+
+
+def line_of(piece):
+    return [piece] + [shift(piece, "z", k) for k in range(1, lax.axis_size("z"))]
+
+
+def sources_of():
     nz = lax.axis_size("z")
-    stack = jnp.stack([piece] + [shift(piece, "z", k) for k in range(1, nz)])
-    first, second = ("x", "y") if order == 0 else ("y", "x")
-    found = []
-    firsts = [stack] + [shift(stack, first, k) for k in range(1, lax.axis_size(first))]
-    for one, part in enumerate(firsts):
-        for two in range(lax.axis_size(second)):
-            moved = part if two == 0 else shift(part, second, two)
-            found.append((moved, (two, one) if order == 0 else (one, two)))
-    return found
-
-
-def place_kernel(parts, count, lead, *refs):
-    where, sources, out = refs[0], refs[1 : 1 + parts], refs[1 + parts]
-    size = sources[0].shape[1] if lead else sources[0].shape[-1]
-    for part in range(parts):
-        begin = 2 * part // parts * size
+    return jnp.stack([chip_of(k, sy, sx) for sy, sx in plane_steps() for k in range(nz)]).astype(
+        jnp.int32
+    )
+
+
+def relay(piece):
+    line = jnp.stack(line_of(piece))
+    nz = line.shape[0]
+    sizes = {"x": lax.axis_size("x"), "y": lax.axis_size("y")}
+    half = line.shape[-1] // 2
+    halves, sources = [], []
+    for part, (first, second) in enumerate((("x", "y"), ("y", "x"))):
+        moved = line[..., half * part : half * part + half]
+        near = jnp.concatenate([moved] + [shift(moved, first, k) for k in range(1, sizes[first])], axis=0)
+        halves.append([near] + [shift(near, second, k) for k in range(1, sizes[second])])
+        sources.append(
+            [
+                chip_of(k, two, one) if first == "x" else chip_of(k, one, two)
+                for two in range(sizes[second])
+                for one in range(sizes[first])
+                for k in range(nz)
+            ]
+        )
+    return halves, [jnp.stack(source).astype(jnp.int32) for source in sources]
+
+
+def inverse_of(where):
+    return jnp.zeros_like(where).at[where].set(jnp.arange(where.shape[0], dtype=jnp.int32))
+
+
+def in_order(stacks, where, begin, end):
+    found = jnp.concatenate([part[:, begin:end] for part in stacks], axis=0)
+    return jnp.take(found, inverse_of(where), axis=0)
+
+
+def grouped(whole, rows, groups, lead=0):
+    width = whole.shape[2]
+    first = whole[:, :lead].reshape(-1, width)
+    others = whole[:, lead:].reshape(-1, groups, rows, width).transpose(1, 0, 2, 3).reshape(-1, width)
+    return jnp.concatenate([first, others], axis=0)[None], others.shape[0] // groups
+
+
+def place(where_ref, refs, target, begin=0):
+    count, _, width = refs[0].shape
+    for index, ref in enumerate(refs):
         for k in range(count):
-            spot = where[part * count + k]
-            if lead:
-                for row in range(size):
-                    out[begin + row, spot] = sources[part][k, row]
-            else:
-                out[spot, :, begin : begin + size] = sources[part][k]
-
-
-def gather_matrix(halves, chips, lead):
-    nz = lax.axis_size("z")
-    found = gather_pieces(halves[0], 0) + gather_pieces(halves[1], 1)
-    where = jnp.stack([chip_of(k, sy, sx) for _, (sy, sx) in found for k in range(nz)])
-    parts = [part for part, _ in found]
-    shape = halves[0].shape
-    if lead:
-        whole = (2 * shape[0], chips) + shape[1:]
-    else:
-        whole = (chips,) + shape[:-1] + (2 * shape[-1],)
-    return pl.pallas_call(
-        functools.partial(place_kernel, len(parts), nz, lead),
-        out_shape=jax.ShapeDtypeStruct(whole, halves[0].dtype),
-        in_specs=[pl.BlockSpec(memory_space=pltpu.SMEM)]
-        + [pl.BlockSpec(memory_space=pltpu.VMEM)] * len(parts),
-        out_specs=pl.BlockSpec(memory_space=pltpu.VMEM),
-        compiler_params=pltpu.CompilerParams(vmem_limit_bytes=VMEM_LIMIT),
-        name="place",
-    )(where.astype(jnp.int32), *parts)
-
-
-def slot_table(order):
+            target[where_ref[index * count + k], :, begin : begin + width] = ref[k]
+
+
+def slot_table():
     nz, ny, nx = (lax.axis_size(a) for a in CHIP)
     chips = jnp.arange(nz * ny * nx)
     zr = (chips // (ny * nx) - lax.axis_index("z")) % nz
     yr = (chips // nx % ny - lax.axis_index("y")) % ny
     xr = (chips % nx - lax.axis_index("x")) % nx
-    if order == 0:
-        return ((xr * ny + yr) * nz + zr).astype(jnp.int32)
     return ((yr * nx + xr) * nz + zr).astype(jnp.int32)
 
 
-def scatter_plane(slots, order):
-    first, second = ("x", "y") if order == 0 else ("y", "x")
+def scatter_plane(slots, others=()):
     nz = lax.axis_size("z")
-    for axis in (first, second):
-        size = lax.axis_size(axis)
-        parts = slots.reshape((size, -1) + slots.shape[1:])
-        total = parts[0].astype(F32)
-        for k in range(1, size):
-            total = total + shift(parts[k], axis, k).astype(F32)
-        slots = total.astype(BF)
-    return slots.reshape((nz,) + slots.shape[1:])
+    total = after(slots[:nz], others).astype(F32)
+    for index, (sy, sx) in enumerate(plane_steps()):
+        if index:
+            part = diagonal(slots[nz * index : nz * index + nz], sy, sx)
+            total = total + part.astype(F32)
+    return total.astype(BF)
 
 
 def scatter_line(column):
@@ -273,36 +297,40 @@
     mixed_ref[...] = jnp.concatenate(mixed, axis=0).T.astype(BF)
 
 
-def attend_call(valid, queries, keys, values, both, base, count):
-    pages = queries.shape[0] // count
+def attend_call(valid, projected, both, base, count):
+    pages = projected.shape[1] // count
     pairs = H // 2
-    wide = pl.BlockSpec((count, 128), lambda pair, page: (page, pair))
+
+    def part(index):
+        return pl.BlockSpec((None, count, 128), lambda pair, page: (index, page, pair))
+
     return pl.pallas_call(
         attend_kernel,
         grid=(pairs, pages),
         in_specs=[
             pl.BlockSpec(memory_space=pltpu.SMEM),
-            wide,
-            wide,
-            wide,
+            part(0),
+            part(1),
+            part(2),
             pl.BlockSpec((count, 2 * NB), lambda pair, page: (page, 0)),
             pl.BlockSpec((2, 8, 512), lambda pair, page: (pair, 0, 0)),
         ],
         out_specs=[
-            wide,
+            pl.BlockSpec((count, 128), lambda pair, page: (page, pair)),
             pl.BlockSpec((1, 1, 8, count), lambda pair, page: (page, pair, 0, 0)),
         ],
         out_shape=[
-            jax.ShapeDtypeStruct(queries.shape, BF),
+            jax.ShapeDtypeStruct(projected.shape[1:], BF),
             jax.ShapeDtypeStruct((pages, pairs, 8, count), F32),
         ],
         scratch_shapes=[
             pltpu.VMEM((2, 128, count + 384), F32),
             pltpu.VMEM((2, 2, NB, NB), BF),
         ],
-        compiler_params=pltpu.CompilerParams(vmem_limit_bytes=VMEM_LIMIT),
+        compiler_params=params_of(),
         name="attend",
-    )(valid, queries, keys, values, both, base)
+        cost_estimate=cost(28),
+    )(valid, projected, projected, projected, both, base)
 
 
 def fold_diagonals(value):
@@ -315,7 +343,7 @@
 
 def attend_back_kernel(
     valid_ref, q_ref, k_ref, v_ref, dm_ref, mixed_ref, log_ref, both_ref, both_t_ref, base_ref,
-    dq_ref, dk_ref, dv_ref, sums_ref, strip, planes, d_strip, d_planes,
+    grad_ref, sums_ref, strip, planes, d_strip, d_planes,
 ):
     page = pl.program_id(1)
 
@@ -367,9 +395,9 @@
         for k in range(2):
             side = mixed_k[:, NB * k : NB * k + NB].astype(BF)
             d_planes[head, k] += dot(both_t[NB * k : NB * k + NB], side)
-    dq_ref[...] = (jnp.concatenate(d_queries, axis=0).T * HD ** (-0.5)).astype(BF)
-    dk_ref[...] = d_keys.astype(BF)
-    dv_ref[...] = d_values.astype(BF)
+    grad_ref[0] = (jnp.concatenate(d_queries, axis=0).T * HD ** (-0.5)).astype(BF)
+    grad_ref[1] = d_keys.astype(BF)
+    grad_ref[2] = d_values.astype(BF)
 
     @pl.when(page == pl.num_programs(1) - 1)
     def _():
@@ -384,19 +412,23 @@
             sums_ref[head, 2:3, 256:] = jnp.sum(d_strip[head, :, 640:], axis=0, keepdims=True)
 
 
-def attend_back_call(valid, queries, keys, values, d_mixed, mixed, log_total, both, base, count):
-    pages = queries.shape[0] // count
+def attend_back_call(valid, projected, d_mixed, mixed, log_total, both, base, count):
+    pages = projected.shape[1] // count
     pairs = H // 2
     both_t = both.T
+
+    def part(index):
+        return pl.BlockSpec((None, count, 128), lambda pair, page: (index, page, pair))
+
     wide = pl.BlockSpec((count, 128), lambda pair, page: (page, pair))
     return pl.pallas_call(
         attend_back_kernel,
         grid=(pairs, pages),
         in_specs=[
             pl.BlockSpec(memory_space=pltpu.SMEM),
-            wide,
-            wide,
-            wide,
+            part(0),
+            part(1),
+            part(2),
             wide,
             wide,
             pl.BlockSpec((1, 1, 8, count), lambda pair, page: (page, pair, 0, 0)),
@@ -404,18 +436,24 @@
             pl.BlockSpec((2 * NB, count), lambda pair, page: (0, page)),
             pl.BlockSpec((2, 8, 512), lambda pair, page: (pair, 0, 0)),
         ],
-        out_specs=[wide, wide, wide, pl.BlockSpec((2, 8, 512), lambda pair, page: (pair, 0, 0))],
-        out_shape=[jax.ShapeDtypeStruct(queries.shape, BF)] * 3
-        + [jax.ShapeDtypeStruct((H, 8, 512), F32)],
+        out_specs=[
+            pl.BlockSpec((3, count, 128), lambda pair, page: (0, page, pair)),
+            pl.BlockSpec((2, 8, 512), lambda pair, page: (pair, 0, 0)),
+        ],
+        out_shape=[
+            jax.ShapeDtypeStruct(projected.shape, BF),
+            jax.ShapeDtypeStruct((H, 8, 512), F32),
+        ],
         scratch_shapes=[
             pltpu.VMEM((2, 128, count + 384), F32),
             pltpu.VMEM((2, 2, NB, NB), BF),
             pltpu.VMEM((2, 128, count + 384), F32),
             pltpu.VMEM((2, 2, NB, NB), F32),
         ],
-        compiler_params=pltpu.CompilerParams(vmem_limit_bytes=VMEM_LIMIT),
+        compiler_params=params_of(),
         name="attend_back",
-    )(valid, queries, keys, values, d_mixed, mixed, log_total, both, both_t, base)
+        cost_estimate=cost(41),
+    )(valid, projected, projected, projected, d_mixed, mixed, log_total, both, both_t, base)
 
 
 def gelu_parts(before):
@@ -437,139 +475,475 @@
     return before * below, below + before * (bell * 0.3989422804014327)
 
 
-def feed_kernel(rows_ref, first_ref, bias_ref, active_ref, slope_ref):
-    before = dot(rows_ref[...], first_ref[...]) + bias_ref[...]
+def normalize(rows):
+    center = rows - jnp.mean(rows, axis=-1, keepdims=True)
+    spread = jnp.mean(center * center, axis=-1, keepdims=True)
+    scale = lax.rsqrt(spread + EPSILON)
+    return center * scale, scale
+
+
+def normalize_back(grad, hat, scale, gain):
+    scaled = grad * gain
+    first = jnp.mean(scaled, axis=-1, keepdims=True)
+    second = jnp.mean(scaled * hat, axis=-1, keepdims=True)
+    return scale * (scaled - first - hat * second)
+
+
+def add_sums(ref, index, value, fresh):
+    total = jnp.sum(value, axis=0, keepdims=True)
+    ref[index : index + 1] = jnp.where(fresh, total, ref[index : index + 1] + total)
+
+
+def whole_spec(shape):
+    return pl.BlockSpec(shape, lambda *_: (0,) * len(shape))
+
+
+def smem():
+    return pl.BlockSpec(memory_space=pltpu.SMEM)
+
+
+def weight_specs(stacks, rows, first):
+    nz, _, width = stacks[0].shape
+    return [pl.BlockSpec((nz, rows, width), lambda i: (0, first + i, 0))] * len(stacks)
+
+
+def project_kernel(count, one_ref, two_ref, raw_ref, both_ref, space_ref, coef_ref, *refs):
+    stacks, (out_ref, wide_ref, normed_ref, inputs_ref, joint_ref, plain_ref) = refs[:count], refs[count:]
+    step = pl.program_id(0)
+
+    @pl.when(step == 0)
+    def _():
+        normed = (raw_ref[...].astype(F32) - coef_ref[0:1]) * coef_ref[1:2]
+        inputs = normed * coef_ref[2:3] + coef_ref[3:4]
+        normed_ref[...] = normed
+        inputs_ref[...] = inputs
+        plain_ref[...] = inputs.astype(BF)
+        joint_ref[...] = (inputs + dot(both_ref[...], space_ref[...])).astype(BF)
+
+    if two_ref.shape[0] == 1:
+        place(one_ref, stacks, wide_ref.at[0])
+    else:
+        place(one_ref, stacks[: count // 2], wide_ref.at[0])
+        place(two_ref, stacks[count // 2 :], wide_ref.at[0], wide_ref.shape[3] // 2)
+    width = raw_ref.shape[1]
+    weight = wide_ref[0].reshape(width, width)
+    rows = jnp.where(step == 2, plain_ref[...], joint_ref[...])
+    factor = jnp.where(step == 0, HD ** (-0.5), 1.0)
+    out_ref[0] = (dot(rows, weight) * factor).astype(BF)
+
+
+def project_call(sources, stacks, rows, raw, both, space, coefs):
+    tokens, width = raw.shape
+    chips = sources[0].shape[0]
+    whole = whole_spec((tokens, width))
+    return pl.pallas_call(
+        functools.partial(project_kernel, len(stacks)),
+        grid=(3,),
+        in_specs=[smem(), smem(), whole, whole_spec(both.shape), whole_spec(space.shape)]
+        + [whole_spec(coefs.shape)]
+        + weight_specs(stacks, rows, 0),
+        out_specs=[
+            pl.BlockSpec((1, tokens, width), lambda i: (i, 0, 0)),
+            pl.BlockSpec((1, chips, rows, width), lambda i: (i, 0, 0, 0)),
+            whole,
+            whole,
+            whole,
+            whole,
+        ],
+        out_shape=[
+            jax.ShapeDtypeStruct((3, tokens, width), BF),
+            jax.ShapeDtypeStruct((3, chips, rows, width), BF),
+            jax.ShapeDtypeStruct((tokens, width), F32),
+            jax.ShapeDtypeStruct((tokens, width), F32),
+            jax.ShapeDtypeStruct((tokens, width), BF),
+            jax.ShapeDtypeStruct((tokens, width), BF),
+        ],
+        compiler_params=params_of(),
+        name="project",
+        cost_estimate=cost(12),
+    )(*sources, raw, both, space, coefs, *stacks)
+
+
+def output_kernel(count, where_ref, mixed_ref, keep_ref, *refs):
+    stacks, (att_ref, low_ref, wide_ref) = refs[:count], refs[count:]
+    place(where_ref, stacks, wide_ref)
+    width = mixed_ref.shape[1]
+    att = dot(mixed_ref[...], wide_ref[...].reshape(width, width)) * keep_ref[...]
+    att_ref[...] = att
+    low_ref[...] = att.astype(BF)
+
+
+def output_call(where, stacks, rows, mixed, keep):
+    tokens, width = mixed.shape
+    nz = stacks[0].shape[0]
+    chips = len(stacks) * nz
+    return pl.pallas_call(
+        functools.partial(output_kernel, len(stacks)),
+        grid=(1,),
+        in_specs=[smem(), whole_spec((tokens, width)), whole_spec((tokens, 1))]
+        + weight_specs(stacks, rows, 8),
+        out_specs=[
+            whole_spec((tokens, width)),
+            whole_spec((tokens, width)),
+            whole_spec((chips, rows, width)),
+        ],
+        out_shape=[
+            jax.ShapeDtypeStruct((tokens, width), F32),
+            jax.ShapeDtypeStruct((tokens, width), BF),
+            jax.ShapeDtypeStruct((chips, rows, width), BF),
+        ],
+        compiler_params=params_of(),
+        name="output",
+        cost_estimate=cost(5),
+    )(where, mixed, keep, *stacks)
+
+
+def feed_kernel(count, where_ref, inputs_ref, own_ref, other_ref, vec_ref, bias_ref, *refs):
+    stacks = refs[:count]
+    u_ref, low_ref, hat_ref, scale_ref, active_ref, slope_ref, wide_ref = refs[count:]
+    half = inputs_ref.shape[0] // 2
+
+    @pl.when(pl.program_id(0) == 0)
+    def _():
+        for page in range(2):
+            here = pl.ds(half * page, half)
+            there = pl.ds(half * (1 - page), half)
+            rows = inputs_ref[here, :] + own_ref[here, :] + other_ref[there, :].astype(F32)
+            hat, scale = normalize(rows)
+            u = hat * vec_ref[2:3] + vec_ref[3:4]
+            u_ref[here, :] = u
+            low_ref[here, :] = u.astype(BF)
+            hat_ref[here, :] = hat
+            scale_ref[here, :] = scale
+
+    place(where_ref, stacks, wide_ref.at[0])
+    width = inputs_ref.shape[1]
+    weight = wide_ref[0].reshape(width, width)
+    before = dot(low_ref[...], weight) + bias_ref[...]
     active, slope = gelu_parts(before)
     active_ref[...] = active.astype(BF)
     slope_ref[...] = slope.astype(BF)
 
 
-def feed_call(rows, first, bias, block):
-    tokens, width = rows.shape
-    hidden = first.shape[1]
-    out = pl.BlockSpec((tokens, block), lambda i: (0, i))
+def feed_call(where, stacks, rows, inputs, own, other, vecs, bias):
+    tokens, width = inputs.shape
+    hidden = bias.shape[1]
+    nz = stacks[0].shape[0]
+    chips = len(stacks) * nz
+    whole = whole_spec((tokens, width))
+    block = pl.BlockSpec((tokens, width), lambda i: (0, i))
     return pl.pallas_call(
-        feed_kernel,
-        grid=(hidden // block,),
+        functools.partial(feed_kernel, len(stacks)),
+        grid=(hidden // width,),
+        in_specs=[smem(), whole, whole, whole, whole_spec(vecs.shape)]
+        + [pl.BlockSpec((1, width), lambda i: (0, i))]
+        + weight_specs(stacks, rows, 4),
+        out_specs=[
+            whole,
+            whole,
+            whole,
+            whole_spec((tokens, 1)),
+            block,
+            block,
+            pl.BlockSpec((1, chips, rows, width), lambda i: (i, 0, 0, 0)),
+        ],
+        out_shape=[
+            jax.ShapeDtypeStruct((tokens, width), F32),
+            jax.ShapeDtypeStruct((tokens, width), BF),
+            jax.ShapeDtypeStruct((tokens, width), F32),
+            jax.ShapeDtypeStruct((tokens, 1), F32),
+            jax.ShapeDtypeStruct((tokens, hidden), BF),
+            jax.ShapeDtypeStruct((tokens, hidden), BF),
+            jax.ShapeDtypeStruct((hidden // width, chips, rows, width), BF),
+        ],
+        compiler_params=params_of(),
+        name="feed",
+        cost_estimate=cost(24),
+    )(where, inputs, own, other, vecs, bias, *stacks)
+
+
+def close_kernel(count, where_ref, active_ref, u_ref, cot_ref, keep_ref, vec_ref, *refs):
+    stacks = refs[:count]
+    out_ref, dy_ref, low_ref, sums_ref, wide_ref = refs[count:]
+    step = pl.program_id(0)
+
+    @pl.when(step == 0)
+    def _():
+        place(where_ref, stacks, wide_ref)
+
+    weight = wide_ref[...].reshape(-1, u_ref.shape[1])
+    rows = u_ref[...] + (dot(active_ref[...], weight) + vec_ref[6:7])
+    hat, scale = normalize(rows)
+    gain = vec_ref[4:5]
+    keep = keep_ref[...]
+    out_ref[...] = ((hat * gain + vec_ref[5:6]) * keep).astype(BF)
+    cot = cot_ref[...].astype(F32) * keep
+    dy = normalize_back(cot, hat, scale, gain)
+    low = dy.astype(BF)
+    dy_ref[...] = dy
+    low_ref[...] = low
+    add_sums(sums_ref, 0, cot * hat, step == 0)
+    add_sums(sums_ref, 1, cot, step == 0)
+    add_sums(sums_ref, 2, low.astype(F32), step == 0)
+
+
+def close_call(where, stacks, rows, active, u, cot, keep, vecs):
+    tokens, width = u.shape
+    hidden = active.shape[1]
+    nz = stacks[0].shape[0]
+    groups = 4
+    chips = len(stacks) * nz
+    steps = 4
+    block = pl.BlockSpec((tokens // steps, width), lambda i: (i, 0))
+    return pl.pallas_call(
+        functools.partial(close_kernel, len(stacks)),
+        grid=(steps,),
         in_specs=[
-            pl.BlockSpec((tokens, width), lambda i: (0, 0)),
-            pl.BlockSpec((width, block), lambda i: (0, i)),
-            pl.BlockSpec((1, block), lambda i: (0, i)),
-        ],
-        out_specs=[out, out],
-        out_shape=[jax.ShapeDtypeStruct((tokens, hidden), BF)] * 2,
-        compiler_params=pltpu.CompilerParams(vmem_limit_bytes=VMEM_LIMIT),
-        name="feed",
-    )(rows, first, bias)
-
-
-def store_slots(slots_ref, out_ref, total, half):
-    chips = out_ref.shape[1]
-    rows = total.shape[0] // chips
-    for chip in range(chips):
-        part = total[chip * rows : chip * rows + rows].astype(BF)
-        out_ref[0, slots_ref[0, chip]] = part[:, :half]
-        out_ref[1, slots_ref[1, chip]] = part[:, half:]
-
-
-def feed_back_kernel(slots_ref, rows_t_ref, low_ref, second_ref, first_ref, slope_ref, rest_ref, du_ref, dfirst_ref, dbias_ref):
+            smem(),
+            pl.BlockSpec((tokens // steps, hidden), lambda i: (i, 0)),
+            block,
+            block,
+            pl.BlockSpec((tokens // steps, 1), lambda i: (i, 0)),
+            whole_spec(vecs.shape),
+        ]
+        + [whole_spec((nz, groups * rows, width))] * len(stacks),
+        out_specs=[
+            block,
+            block,
+            block,
+            whole_spec((8, width)),
+            whole_spec((chips, groups * rows, width)),
+        ],
+        out_shape=[
+            jax.ShapeDtypeStruct((tokens, width), BF),
+            jax.ShapeDtypeStruct((tokens, width), F32),
+            jax.ShapeDtypeStruct((tokens, width), BF),
+            jax.ShapeDtypeStruct((8, width), F32),
+            jax.ShapeDtypeStruct((chips, groups * rows, width), BF),
+        ],
+        compiler_params=params_of(),
+        name="close",
+        cost_estimate=cost(13),
+    )(where, active, u, cot, keep, vecs, *stacks)
+
+
+def store_slots(slots_ref, out_ref, total, first=0):
+    rows = out_ref.shape[1]
+    for index in range(total.shape[0] // rows):
+        part = total[index * rows : index * rows + rows].astype(BF)
+        out_ref[slots_ref[first + index]] = part
+
+
+def second_kernel(slots_ref, active_ref, low_ref, out_ref):
+    total = dot(active_ref[...].T, low_ref[...])
+    count = total.shape[0] // out_ref.shape[1]
+    store_slots(slots_ref, out_ref, total, pl.program_id(0) * count)
+
+
+def second_call(slots, active, low, chips):
+    tokens, width = low.shape
+    hidden = active.shape[1]
+    return pl.pallas_call(
+        second_kernel,
+        grid=(hidden // width,),
+        in_specs=[
+            smem(),
+            pl.BlockSpec((tokens, width), lambda i: (0, i)),
+            whole_spec((tokens, width)),
+        ],
+        out_specs=whole_spec((chips, hidden // chips, width)),
+        out_shape=jax.ShapeDtypeStruct((chips, hidden // chips, width), BF),
+        compiler_params=params_of(),
+        name="second",
+        cost_estimate=cost(10),
+    )(slots, active, low)
+
+
+def feed_back_kernel(
+    slots_ref, rows_ref, low_ref, second_ref, first_ref, slope_ref, dy_ref, hat_ref, scale_ref, vec_ref,
+    dpre_ref, dlow_ref, dfirst_ref, dbias_ref, sums_ref, rows_t, total_ref,
+):
     step = pl.program_id(0)
+
+    @pl.when(step == 0)
+    def _():
+        rows_t[...] = rows_ref[...].T
+        total_ref[...] = dy_ref[...]
+
     d_active = dot_nt(low_ref[...], second_ref[...])
     d_before = (slope_ref[...].astype(F32) * d_active).astype(BF)
     dbias_ref[...] = jnp.sum(d_before.astype(F32), axis=0, keepdims=True)
-    part = dot_nt(d_before, first_ref[...])
-
-    @pl.when(step == 0)
+    total_ref[...] += dot_nt(d_before, first_ref[0])
+    store_slots(slots_ref, dfirst_ref, dot(rows_t[...], d_before))
+
+    @pl.when(step == pl.num_programs(0) - 1)
     def _():
-        du_ref[...] = rest_ref[...] + part
-
-    @pl.when(step > 0)
-    def _():
-        du_ref[...] += part
-
-    total = dot(rows_t_ref[...], d_before)
-    store_slots(slots_ref, dfirst_ref, total, total.shape[1] // 2)
-
-
-def feed_back_call(slots, rows, low, second, first, slope, rest, chips, block):
+        grad = total_ref[...]
+        hat = hat_ref[...]
+        d_pre = normalize_back(grad, hat, scale_ref[...], vec_ref[2:3])
+        dpre_ref[...] = d_pre
+        dlow_ref[...] = d_pre.astype(BF)
+        add_sums(sums_ref, 0, grad * hat, True)
+        add_sums(sums_ref, 1, grad, True)
+
+
+def feed_back_call(slots, rows, low, second, first, slope, dy, hat, scale, vecs, chips):
     tokens, width = rows.shape
     hidden = second.shape[0]
     piece = width // chips
-    whole = pl.BlockSpec((tokens, width), lambda i: (0, 0))
+    whole = whole_spec((tokens, width))
     return pl.pallas_call(
         feed_back_kernel,
-        grid=(hidden // block,),
+        grid=(hidden // width,),
         in_specs=[
-            pl.BlockSpec(memory_space=pltpu.SMEM),
-            pl.BlockSpec((width, tokens), lambda i: (0, 0)),
-            whole,
-            pl.BlockSpec((block, width), lambda i: (i, 0)),
-            pl.BlockSpec((width, block), lambda i: (0, i)),
-            pl.BlockSpec((tokens, block), lambda i: (0, i)),
-            whole,
+            smem(),
+            whole,
+            whole,
+            pl.BlockSpec((width, width), lambda i: (i, 0)),
+            pl.BlockSpec((1, width, width), lambda i: (i, 0, 0)),
+            pl.BlockSpec((tokens, width), lambda i: (0, i)),
+            whole,
+            whole,
+            whole_spec((tokens, 1)),
+            whole_spec(vecs.shape),
         ],
         out_specs=[
             whole,
-            pl.BlockSpec((2, chips, piece, block // 2), lambda i: (0, 0, 0, i)),
-            pl.BlockSpec((1, block), lambda i: (0, i)),
+            whole,
+            pl.BlockSpec((chips, piece, width), lambda i: (0, 0, i)),
+            pl.BlockSpec((1, width), lambda i: (0, i)),
+            whole_spec((8, width)),
         ],
         out_shape=[
             jax.ShapeDtypeStruct((tokens, width), F32),
-            jax.ShapeDtypeStruct((2, chips, piece, hidden // 2), BF),
+            jax.ShapeDtypeStruct((tokens, width), BF),
+            jax.ShapeDtypeStruct((chips, piece, hidden), BF),
             jax.ShapeDtypeStruct((1, hidden), F32),
-        ],
-        compiler_params=pltpu.CompilerParams(vmem_limit_bytes=VMEM_LIMIT),
+            jax.ShapeDtypeStruct((8, width), F32),
+        ],
+        scratch_shapes=[pltpu.VMEM((width, tokens), BF), pltpu.VMEM((tokens, width), F32)],
+        compiler_params=params_of(),
         name="feed_back",
-    )(slots, rows.T, low, second, first, slope, rest)
-
-
-def outer_kernel(slots_ref, left_ref, right_ref, out_ref):
-    chips = out_ref.shape[1]
+        cost_estimate=cost(26),
+    )(slots, rows, low, second, first, slope, dy, hat, scale, vecs)
+
+
+def middle_kernel(slots_ref, own_ref, other_ref, keep_ref, mixed_ref, weight_ref, dmixed_ref, dw_ref, low_ref):
+    half = own_ref.shape[0] // 2
+    for page in range(2):
+        here = pl.ds(half * page, half)
+        there = pl.ds(half * (1 - page), half)
+        merged = (own_ref[here, :] + other_ref[there, :].astype(F32)) * keep_ref[here, :]
+        low_ref[here, :] = merged.astype(BF)
+    low = low_ref[...]
+    dmixed_ref[...] = dot_nt(low, weight_ref[...]).astype(BF)
+    store_slots(slots_ref, dw_ref, dot(mixed_ref[...].T, low))
+
+
+def middle_call(slots, own, other, keep, mixed, weight, chips):
+    tokens, width = own.shape
+    whole = whole_spec((tokens, width))
+    piece = (chips, width // chips, width)
+    return pl.pallas_call(
+        middle_kernel,
+        grid=(1,),
+        in_specs=[smem(), whole, whole, whole_spec((tokens, 1)), whole, whole_spec((width, width))],
+        out_specs=[whole, whole_spec(piece)],
+        out_shape=[jax.ShapeDtypeStruct((tokens, width), BF), jax.ShapeDtypeStruct(piece, BF)],
+        scratch_shapes=[pltpu.VMEM((tokens, width), BF)],
+        compiler_params=params_of(),
+        name="middle",
+        cost_estimate=cost(8),
+    )(slots, own, other, keep, mixed, weight)
+
+
+def grads_kernel(
+    slots_ref, joint_ref, plain_ref, grad_ref, weight_ref, dpre_ref, normed_ref, both_ref, coef_ref,
+    dw_ref, rows_ref, sums_ref, left_t, total_ref,
+):
     step = pl.program_id(0)
-    total = dot(left_ref[...], right_ref[...])
-    rows = out_ref.shape[2]
-    count = total.shape[0] // rows
-    half = total.shape[1] // 2
-    for index in range(count):
-        part = total[index * rows : index * rows + rows].astype(BF)
-        chip = step * count + index
-        out_ref[0, slots_ref[0, chip]] = part[:, :half]
-        out_ref[1, slots_ref[1, chip]] = part[:, half:]
-
-
-def outer_call(slots, left_t, right, chips, steps):
-    height, tokens = left_t.shape
-    width = right.shape[1]
-    block = height // steps
+    space_size = both_ref.shape[1]
+
+    @pl.when(step == 0)
+    def _():
+        left_t[...] = joint_ref[...].T
+
+    @pl.when(step == 2)
+    def _():
+        left_t[...] = plain_ref[...].T
+
+    grad = grad_ref[0]
+    chips = dw_ref.shape[0]
+    piece = left_t.shape[0] // chips
+    near = space_size // (2 * chips)
+
+    total = dot(left_t[...], grad)
+
+    def store(index):
+        for chip in range(chips):
+            low = total[chip * piece : chip * piece + piece].astype(BF)
+            dw_ref[slots_ref[chip], index * piece : index * piece + piece] = low
+
+    for index in range(3):
+        pl.when(step == index)(functools.partial(store, index))
+    part = dot_nt(grad, weight_ref[0])
+
+    @pl.when(step == 0)
+    def _():
+        total_ref[...] = part
+
+    @pl.when(step == 1)
+    def _():
+        joint = total_ref[...] + part
+        total_ref[...] = joint + dpre_ref[...]
+        space = dot(both_ref[...].T, joint.astype(BF)).astype(BF)
+        for chip in range(chips):
+            for k in range(2):
+                begin = k * space_size // 2 + chip * near
+                start = 3 * piece + k * near
+                dw_ref[slots_ref[chip], start : start + near] = space[begin : begin + near]
+
+    @pl.when(step == 2)
+    def _():
+        dx = total_ref[...] + part
+        rows_ref[...] = dx * coef_ref[2:3] * coef_ref[1:2]
+        add_sums(sums_ref, 0, dx * normed_ref[...], True)
+        add_sums(sums_ref, 1, dx, True)
+
+
+def grads_call(slots, joint, plain, grad, weight, d_pre, normed, both, coefs, chips):
+    tokens, width = joint.shape
+    whole = whole_spec((tokens, width))
+    height = 3 * (width // chips) + both.shape[1] // chips
     return pl.pallas_call(
-        outer_kernel,
-        grid=(steps,),
+        grads_kernel,
+        grid=(3,),
         in_specs=[
-            pl.BlockSpec(memory_space=pltpu.SMEM),
-            pl.BlockSpec((block, tokens), lambda i: (i, 0)),
-            pl.BlockSpec((tokens, width), lambda i: (0, 0)),
-        ],
-        out_specs=pl.BlockSpec((2, chips, height // chips, width // 2), lambda i: (0, 0, 0, 0)),
-        out_shape=jax.ShapeDtypeStruct((2, chips, height // chips, width // 2), BF),
-        compiler_params=pltpu.CompilerParams(vmem_limit_bytes=VMEM_LIMIT),
-        name="outer",
-    )(slots, left_t, right)
-
-
-def layer_norm(rows, gain, shift_row):
-    center = rows - jnp.mean(rows, axis=-1, keepdims=True)
-    spread = jnp.mean(center * center, axis=-1, keepdims=True)
-    scale = lax.rsqrt(spread + EPSILON)
-    hat = center * scale
-    return hat * gain + shift_row, hat, scale
-
-
-def layer_norm_back(grad, hat, scale, gain):
-    scaled = grad * gain
-    first = jnp.mean(scaled, axis=-1, keepdims=True)
-    second = jnp.mean(scaled * hat, axis=-1, keepdims=True)
-    d_rows = scale * (scaled - first - hat * second)
-    return d_rows, jnp.sum(grad * hat, axis=0), jnp.sum(grad, axis=0)
+            smem(),
+            whole,
+            whole,
+            pl.BlockSpec((1, tokens, width), lambda i: (i, 0, 0)),
+            pl.BlockSpec((1, width, width), lambda i: (i, 0, 0)),
+            whole,
+            whole,
+            whole_spec(both.shape),
+            whole_spec(coefs.shape),
+        ],
+        out_specs=[
+            whole_spec((chips, height, width)),
+            whole,
+            whole_spec((8, width)),
+        ],
+        out_shape=[
+            jax.ShapeDtypeStruct((chips, height, width), BF),
+            jax.ShapeDtypeStruct((tokens, width), F32),
+            jax.ShapeDtypeStruct((8, width), F32),
+        ],
+        scratch_shapes=[pltpu.VMEM((width, tokens), BF), pltpu.VMEM((tokens, width), F32)],
+        compiler_params=params_of(),
+        name="grads",
+        cost_estimate=cost(12),
+    )(slots, joint, plain, grad, weight, d_pre, normed, both, coefs)
 
 
 def adam(weight, grad, first, second, rate, decay):
@@ -620,6 +994,8 @@
     )
     in_piece = by_core(in_own, in_other).reshape(2 * rows_a, hidden)
     out_piece = by_core(out_own, out_other).reshape(2 * rows_o, width)
+    in_cut = in_piece.reshape(2 * rows_a, -1, width).transpose(1, 0, 2)
+    out_cut = out_piece.reshape(-1, 2 * rows_a, width)
 
     raw_own = visual[0].astype(F32)
     sums = jnp.stack([jnp.sum(raw_own, axis=0), jnp.sum(raw_own * raw_own, axis=0)])
@@ -650,17 +1026,17 @@
     small = jnp.concatenate(
         [space_both, pack_both, jnp.concatenate(split_three(sums + sums_other), axis=0)], axis=0
     )
-    small = jnp.pad(small, ((0, -small.shape[0] % 8), (0, 0)))
-    column = jnp.stack([small] + [shift(small, "z", k) for k in range(1, nz)])
-    plane = [
-        (column if sy == 0 and sx == 0 else diagonal(column, sy, sx), sy, sx)
-        for sy in range(ny)
-        for sx in range(nx)
-    ]
-    nearby = jnp.concatenate([part for part, _, _ in plane], axis=0)
-    source = jnp.stack([chip_of(k, sy, sx) for _, sy, sx in plane for k in range(nz)])
-    place_of = jnp.zeros((chips,), jnp.int32).at[source].set(jnp.arange(chips, dtype=jnp.int32))
-    gathered = jnp.take(nearby, place_of, axis=0)
+    pad = -(small.shape[0] + 6 * rows_a) % 16
+    first = jnp.concatenate(
+        [attn_piece[:3].reshape(6 * rows_a, width), jnp.pad(small, ((0, pad), (0, 0)))], axis=0
+    )
+    rest = jnp.concatenate([out_cut, in_cut, attn_piece[3:]], axis=0).reshape(-1, width)
+    wide_rest = lax.all_gather(rest, CHIP)
+    halves, sources = relay(first)
+    weight_rows = 6 * rows_a
+    gathered = jnp.concatenate(
+        [in_order(halves[k], sources[k], weight_rows, first.shape[0]) for k in range(2)], axis=2
+    )
     wide_spatial = gathered[:, : 2 * space_rows].reshape(chips, 2, 2, -1, width)
     wide_spatial = wide_spatial.transpose(2, 0, 1, 3, 4).reshape(2 * NB, width)
     packs = gathered[:, 2 * space_rows : 2 * space_rows + 2 * small_rows]
@@ -691,9 +1067,9 @@
     stream_inverse = jnp.where(seen, inverse, 1.0)
     stream_gain = jnp.where(seen, wide_vec[0], 1.0)
     stream_shift = jnp.where(seen, wide_vec[1], 0.0)
-    raw = jnp.concatenate([data_own, data_other], axis=0).astype(F32)
-    normed = (raw - stream_mean) * stream_inverse
-    inputs = normed * stream_gain + stream_shift
+    raw = jnp.concatenate([data_own, data_other], axis=0)
+    coefs = jnp.stack([stream_mean, stream_inverse, stream_gain, stream_shift])
+    coefs = jnp.pad(coefs, ((0, 4), (0, 0)))
     position = jnp.arange(count, dtype=jnp.int32)
     lengths_both = jnp.concatenate([lengths, length_other])
     keep_pages = (position[None, :] < lengths_both[:, None]).astype(F32).reshape(tokens, 1)
@@ -710,75 +1086,64 @@
         ],
         axis=1,
     )
-    place = dot(both, wide_spatial)
-    joint = (inputs + place).astype(BF)
-    plain = inputs.astype(BF)
     base = base_rows(tables)
 
-    wide_attn = gather_matrix((attn_piece[:2], attn_piece[2:]), chips, True)
-    wide_attn = wide_attn.reshape(4, width, width)
-    half_in, half_out = hidden // 2, width // 2
-    wide_in = gather_matrix((in_piece[:, :half_in], in_piece[:, half_in:]), chips, False)
-    wide_in = wide_in.reshape(width, hidden)
-    wide_out = gather_matrix((out_piece[:, :half_out], out_piece[:, half_out:]), chips, False)
-    wide_out = wide_out.reshape(hidden, width)
-
-    scale = HD ** (-0.5)
-    queries = (dot(joint, wide_attn[0]).astype(BF) * scale).astype(BF)
-    keys = dot(joint, wide_attn[1]).astype(BF)
-    values = dot(plain, wide_attn[2]).astype(BF)
-    mixed, log_total = attend_call(valid, queries, keys, values, both, base, count)
-    att = dot(mixed, wide_attn[3])
-    own_att = att * keep_rows
-    other_att = swap(own_att)
-    other_att = jnp.concatenate([other_att[count:], other_att[:count]], axis=0)
-    merged = own_att + other_att
-
-    u, hat_one, scale_one = layer_norm(inputs + merged, wide_vec[2], wide_vec[3])
-    u_low = u.astype(BF)
-    active, slope = feed_call(u_low, wide_in, wide_bias, FEED_BLOCK)
-    ff = dot(active, wide_out) + wide_vec[6]
-    y, hat_two, scale_two = layer_norm(u + ff, wide_vec[4], wide_vec[5])
-    out = (y * keep_rows).astype(BF)
-
-    cot = jnp.concatenate([cot_own, cot_other], axis=0).astype(F32) * keep_rows
-    dy, gain_two, shift_two = layer_norm_back(cot, hat_two, scale_two, wide_vec[4])
-    dff = dy.astype(BF)
-    dff_sum = jnp.sum(dff.astype(F32), axis=0)
-    slots = jnp.stack([slot_table(0), slot_table(1)])
-    d_out = outer_call(slots, active.T, dff, chips, 4)
-    du, d_in, d_bias = feed_back_call(slots, u_low, dff, wide_out, wide_in, slope, dy, chips, FEED_BLOCK)
-    d_pre, gain_one, shift_one = layer_norm_back(du, hat_one, scale_one, wide_vec[2])
-
-    other_pre = swap(d_pre)
-    other_pre = jnp.concatenate([other_pre[count:], other_pre[:count]], axis=0)
-    d_merged = d_pre + other_pre
-    d_att = (d_merged * keep_rows).astype(BF)
-    d_w3 = outer_call(slots, mixed.T, d_att, chips, 1)
-    d_mixed = dot_nt(d_att, wide_attn[3]).astype(BF)
-    dq, dk, dv, table_parts = attend_back_call(
-        valid, queries, keys, values, d_mixed, mixed, log_total, both, base, count
-    )
-    joint_t = joint.T
-    d_w0 = outer_call(slots, joint_t, dq, chips, 1)
-    d_w1 = outer_call(slots, joint_t, dk, chips, 1)
-    d_w2 = outer_call(slots, plain.T, dv, chips, 1)
-    d_joint = dot_nt(dq, wide_attn[0]) + dot_nt(dk, wide_attn[1])
-    dx = d_joint + dot_nt(dv, wide_attn[2]) + d_pre
-    d_space = dot(both.T, d_joint.astype(BF))
-    d_tables = table_sums(table_parts)
-    norm_shift = jnp.sum(dx, axis=0)
-    norm_gain = jnp.sum(dx * normed, axis=0)
-    grad_rows = dx * stream_gain * stream_inverse
-
-    def reduced(halves, blocks=1):
-        sums = [scatter_line(scatter_plane(halves[k], k)) for k in range(2)]
-        cut = jnp.stack([part.reshape(part.shape[0], blocks, -1) for part in sums], axis=2)
-        return cut.reshape(cut.shape[0], -1)
-
-    sum_out = reduced(d_out)
-    sum_in = reduced(d_in, hidden // FEED_BLOCK)
-    sum_attn = jnp.stack([reduced(part) for part in (d_w0, d_w1, d_w2, d_w3)])
+    rows_one = rows_rest = 2 * rows_a
+    where_rest = jnp.arange(chips, dtype=jnp.int32)
+    if rows_one % 16:
+        whole_one = [in_order(halves[k], sources[k], 0, weight_rows) for k in range(2)]
+        whole_one, rows_one = grouped(jnp.concatenate(whole_one, axis=2), rows_one, 3)
+        wide_one, sources = [whole_one], [jnp.zeros((1,), jnp.int32)] * 2
+        wide_rest, rows_rest = grouped(wide_rest, rows_rest, 5, 2 * rows_o)
+        where_rest = jnp.zeros((1,), jnp.int32)
+    else:
+        wide_one = halves[0] + halves[1]
+    wide_rest = [wide_rest]
+    vecs = jnp.pad(wide_vec, ((0, 1), (0, 0)))
+
+    projected, weight_qkv, normed, inputs, joint, plain = project_call(
+        sources, wide_one, rows_one, raw, both, wide_spatial, coefs
+    )
+    mixed, log_total = attend_call(valid, projected, both, base, count)
+    att, att_low, weight_out = output_call(where_rest, wide_rest, rows_rest, mixed, keep_rows)
+    att_other = swap(att_low)
+
+    u, u_low, hat_one, scale_one, active, slope, weight_in = feed_call(
+        where_rest, wide_rest, rows_rest, inputs, att, att_other, vecs, wide_bias
+    )
+    cot = jnp.concatenate([cot_own, cot_other], axis=0)
+    out, dy, dff, close_sums, weight_second = close_call(
+        where_rest, wide_rest, rows_rest, active, u, cot, keep_rows, vecs
+    )
+
+    slots = slot_table()
+    d_out = second_call(jnp.arange(chips, dtype=jnp.int32), active, dff, chips)
+    d_pre, d_pre_low, d_in, d_bias, pre_sums = feed_back_call(
+        slots, u_low, after(dff, d_out), weight_second.reshape(hidden, width),
+        weight_in.reshape(-1, width, width), slope, dy, hat_one, scale_one, vecs, chips,
+    )
+    d_pre_other = swap(d_pre_low)
+
+    d_mixed, d_last = middle_call(
+        slots, d_pre, d_pre_other, keep_rows, mixed, weight_out.reshape(width, width), chips
+    )
+    d_projected, table_parts = attend_back_call(
+        valid, projected, d_mixed, mixed, log_total, both, base, count
+    )
+    column_in = scatter_plane(d_in, d_projected)
+    column_last = scatter_plane(d_last, d_projected)
+    d_first, grad_rows, norm_sums = grads_call(
+        slots, joint, plain, after(d_projected, (column_in, column_last)), weight_qkv.reshape(3, width, width), d_pre, normed,
+        both, coefs, chips,
+    )
+
+    sum_out = lax.psum_scatter(d_out, CHIP).astype(F32)
+    sum_in = scatter_line(column_in)
+    sum_last = scatter_line(column_last)
+    sum_first = scatter_line(scatter_plane(d_first))
+    sum_attn = jnp.concatenate(
+        [sum_first[: 6 * rows_a].reshape(3, 2 * rows_a, width), sum_last[None]], axis=0
+    )
 
     def own_rows(value, axis):
         first, second = jnp.split(value, 2, axis=axis)
@@ -787,65 +1152,40 @@
     def by_stream(own, other):
         return jnp.where(seen, jnp.stack([own, other]), jnp.stack([other, own]))
 
+    own_space, other_space = own_rows(sum_first[6 * rows_a :].reshape(2, 2, -1, width), 1)
+    grad_spatial = (own_space + other_space).reshape(spatial.shape)
     is_norm = jnp.where(seen, 1.0, 0.0)
-    vec_grad = jnp.stack(
-        [norm_gain * is_norm, norm_shift * is_norm, gain_one, shift_one, gain_two, shift_two, dff_sum]
-    )
-
-    def lines(values):
-        flat = values.reshape(chips, -1)
-        flat = jnp.pad(flat, ((0, 0), (0, -flat.shape[1] % width)))
-        return flat.reshape(chips, -1, width)
-
-    space_grad = d_space.reshape(2, chips, 2, -1, width).transpose(1, 2, 0, 3, 4)
-    pos_grad = d_tables.reshape(3, H, chips, 2, -1).transpose(2, 3, 0, 1, 4)
-    vecs = vec_grad.reshape(7, chips, 2, -1).transpose(1, 2, 0, 3)
-    pieces = [
-        space_grad.reshape(chips, -1, width),
-        lines(pos_grad),
-        lines(vecs),
-        lines(d_bias),
-    ]
-    bounds = np.cumsum([0] + [part.shape[1] for part in pieces])
-    small_grad = jnp.concatenate(pieces, axis=1)
-    small_grad = jnp.pad(small_grad, ((0, 0), (0, -small_grad.shape[1] % 8), (0, 0)))
-    order = jnp.zeros((chips,), jnp.int32).at[slots[0]].set(jnp.arange(chips, dtype=jnp.int32))
-    small_slots = jnp.take(small_grad.astype(BF), order, axis=0)
-    small_sum = scatter_line(scatter_plane(small_slots, 0))
-    own_space, other_space = own_rows(small_sum[: bounds[1]], 0)
-    grad_spatial = (own_space + other_space).reshape(spatial.shape)
-
-    def unline(index, shape):
-        size = int(np.prod(shape))
-        flat = small_sum[bounds[index] : bounds[index + 1]].reshape(-1)[: 2 * size]
-        return own_rows(flat.reshape((2,) + shape), 0)
-
-    own_pos, other_pos = unline(1, pos_tables.shape[1:])
-    grad_pos = by_stream(own_pos[0], other_pos[0])
-    own_vec, other_vec = unline(2, (7, vectors.shape[1]))
-    pair_vec = by_stream(own_vec[0], other_vec[0])
+    little = jnp.concatenate(
+        [
+            norm_sums[:2] * is_norm, pre_sums[:2], close_sums[:3], jnp.zeros((1, width), F32),
+            d_bias.reshape(-1, width), table_sums(table_parts).reshape(-1, width),
+        ],
+        axis=0,
+    ).astype(BF)
+    little = jnp.pad(little, ((0, -little.shape[0] % 8), (0, 0)))
+    little = functools.reduce(jnp.add, [part.astype(F32) for part in around(little)]).astype(BF)
+    little = functools.reduce(jnp.add, [part.astype(F32) for part in line_of(little)])
+    little = by_stream(little, swap(little))
+    member = 2 * chip_of(0, 0, 0) + core
+    vec_sum = lax.dynamic_slice_in_dim(little[:, :7], member * vectors.shape[1], vectors.shape[1], 2)
     grad_vec = jnp.stack(
-        [pair_vec[0, 0], pair_vec[0, 1]]
-        + [pair_vec[0, 2], pair_vec[0, 3], pair_vec[1, 2], pair_vec[1, 3]]
-        + [pair_vec[0, 4], pair_vec[0, 5], pair_vec[1, 4], pair_vec[1, 5]]
-        + [pair_vec[0, 6], pair_vec[1, 6]]
-    )
-    own_bias, other_bias = unline(3, bias_in.shape[1:])
-    grad_bias = by_stream(own_bias[0], other_bias[0])
+        [vec_sum[0, 0], vec_sum[0, 1]]
+        + [vec_sum[s, k + m] for k in (2, 4) for s in range(2) for m in range(2)]
+        + [vec_sum[0, 6], vec_sum[1, 6]]
+    )
+    bias_lines = hidden // width
+    bias_sum = little[:, 8 : 8 + bias_lines].reshape(2, hidden)
+    grad_bias = lax.dynamic_slice_in_dim(bias_sum, member * bias_in.shape[1], bias_in.shape[1], 1)
+    pos_sum = little[:, 8 + bias_lines : 8 + bias_lines + 3 * H * NR // width].reshape(2, 3, H, NR)
+    grad_pos = lax.dynamic_slice_in_dim(pos_sum, member * pos_tables.shape[3], pos_tables.shape[3], 3)
 
     squares = jnp.sum(sum_out * sum_out) + jnp.sum(sum_in * sum_in) + jnp.sum(sum_attn * sum_attn)
     for grad in (grad_spatial, grad_pos, grad_vec, grad_bias):
         squares = squares + jnp.sum(grad * grad)
     tile = jnp.full((8, 128), squares, F32)
     tile = tile + swap(tile)
-    around = tile
-    for sy in range(ny):
-        for sx in range(nx):
-            if sy or sx:
-                around = around + diagonal(tile, sy, sx)
-    norm = around
-    for k in range(1, nz):
-        norm = norm + shift(around, "z", k)
+    tile = functools.reduce(jnp.add, around(tile))
+    norm = functools.reduce(jnp.add, line_of(tile))
     grad_norm = jnp.sqrt(norm[0, 0])
     factor = CLIP / jnp.maximum(grad_norm, CLIP)
 

time: 746 us -> 530 us (0.71)
  starting transfers between devices: 186 us -> 56.5 us
  local copies, waits for them, and re-layouts: 92.6 us -> 52.6 us
  other arithmetic: 93.1 us -> 54.3 us
  matrix products: 38.7 us -> 0 us
  Pallas kernels: 156 us -> 191 us
  waiting for transfers between devices: 162 us -> 145 us
  between operations: 10.3 us -> 23.2 us
    ppermute x107 -> x22, starting transfers between devices: 175 us -> 33.7 us  [shift(): lax.ppermute(value, axis, [(i, (i + step) % size) for i in range(size)])]
    ppermute x107 -> x22, waiting for transfers between devices: 161 us -> 88.3 us  [shift(): lax.ppermute(value, axis, [(i, (i + step) % size) for i in range(size)])]
    dot_general x11 -> x0, matrix products: 38.7 us -> none  [the longest x7 25.9 us: dot(): return jnp.dot(left, right, preferred_element_type=F32)]
    pallas_call x10 -> x8, Pallas kernels: 87.1 us -> 121 us  [the longest x1 26.2 us: feed_back_call(): pl.pallas_call(feed_back_kernel, grid=(hidden // width,), in_specs=[smem(...]
    ppermute x6 -> x15, waiting for transfers between devices: 1.26 us -> 26.9 us  [diagonal(): return lax.ppermute(value, ('y', 'x'), pairs)]
    all_gather x0 -> x1, waiting for transfers between devices: none -> 25.2 us  [body(): wide_rest = lax.all_gather(rest, CHIP)]
    reduce_sum x6 -> x0, other arithmetic: 16.2 us -> none  [the longest x2 6.73 us: layer_norm_back(): return (d_rows, jnp.sum(grad * hat, axis=0), jnp.sum(grad, axis=0))]
    ppermute x6 -> x15, starting transfers between devices: 7.04 us -> 17.7 us  [diagonal(): return lax.ppermute(value, ('y', 'x'), pairs)]
  transfers between devices with their start and end apart: 135 -> 59, of which waited for: 40 -> 22; matrix products, arithmetic and copies ran while one was open for 21% -> 18% of each run, Pallas kernels for 12% -> 21%
where the time goes in v2:
time: 530 us; the launch traced here: 522 us
  Pallas kernels  191 us (36%)
  waiting for transfers between devices  145 us (27%)
  starting transfers between devices  56.5 us (11%)
  other arithmetic  54.3 us (10%)
  local copies, waits for them, and re-layouts  52.6 us (10%)
  between operations  23.2 us (4%)
    ppermute x22, waiting for transfers between devices, shift(): lax.ppermute(value, axis, [(i, (i + step) % size) for i in range(size)])  88.3 us
    pallas_call x1, Pallas kernels, attend_back_call(): pl.pallas_call(attend_back_kernel, grid=(pairs, pages), in_specs=[pl.Bloc...  41.9 us
    ppermute x22, starting transfers between devices, shift(): lax.ppermute(value, axis, [(i, (i + step) % size) for i in range(size)])  33.7 us
    pallas_call x1, Pallas kernels, attend_call(): pl.pallas_call(attend_kernel, grid=(pairs, pages), in_specs=[pl.BlockSpec...  28.1 us
    ppermute x15, waiting for transfers between devices, diagonal(): return lax.ppermute(value, ('y', 'x'), pairs)  26.9 us
    pallas_call x1, Pallas kernels, feed_back_call(): pl.pallas_call(feed_back_kernel, grid=(hidden // width,), in_specs=[smem(...  26.2 us
    all_gather x1, waiting for transfers between devices, body(): wide_rest = lax.all_gather(rest, CHIP)  25.2 us
    pallas_call x1, Pallas kernels, feed_call(): pl.pallas_call(functools.partial(feed_kernel, len(stacks)), grid=(hidden...  24.7 us
  transfers between devices with their start and end apart: 59, of which 22 were waited for; matrix products, arithmetic and copies ran while one was open for 18% of the time, Pallas kernels for 21%

profile of v2, /device:TPU:0, one launch (start us, length us, event | category | flops | bytes accessed | tf_op | source)
XLA Modules:
  0.0 522.1 jit_solution(3601054147070782258)
XLA Ops:
  18.8 3.0 collective-permute-start.6
  21.8 2.6 collective-permute-start.7
  28.9 4.1 collective-permute-done.6
  33.0 21.1 %collective-permute-done.7 = bf16[176,768]{1,0:T(8,128)(2,1)S(1)} collective-permute-done((bf16[176,768]{1,0:T(8,128)(2,1)S(1)}, bf16[176,768]{1,0:T(8,128)(2,1)S(1)}, u32[]{:S(2)}, u32[]{:S(2)}) %collective-permute-start.7) | collective-permute-done | bytes 270368 | tf_op jit(solution)/shard_map/ppermute | solution.py:63
  58.6 11.2 %collective-permute-done.11 = bf16[4,176,384]{2,1,0:T(8,128)(2,1)S(1)} collective-permute-done((bf16[4,176,384]{2,1,0:T(8,128)(2,1)S(1)}, bf16[4,176,384]{2,1,0:T(8,128)(2,1)S(1)}, u32[]{:S(2)}, u32[]{:S(2)}) %collective-permute-start.11) | collective-permute-done | bytes 540704 | tf_op jit(solution)/shard_map/ppermute | solution.py:63
  71.1 5.0 collective-permute-done.9
  78.6 2.4 pad_maximum_fusion.raw_ref
  81.1 31.9 %collective-permute-done.12.refs_3_ = bf16[8,176,384]{2,1,0:T(8,128)(2,1)S(1)} collective-permute-done((bf16[8,176,384]{2,1,0:T(8,128)(2,1)S(1)}, bf16[8,176,384]{2,1,0:T(8,128)(2,1)S(1)}, u32[]{:S(2)}, u32[]{:S(2)}) %collective-permute-start.12) | collective-permute-done | bytes 1081376 | tf_op jit(solution)/shard_map/ppermute | solution.py:63
  121.6 11.9 %project.1 = (bf16[3,1024,768]{2,1,0:T(8,128)(2,1)}, bf16[3,16,48,768]{3,2,1,0:T(8,128)(2,1)}, f32[1024,768]{1,0:T(8,128)}, f32[1024,768]{1,0:T(8,128)}, bf16[10...) custom-call(s32[16]{0:T(128)} %stack.295.one_ref, s32[16]{0:T(128)} %stack.296.two_ref, ...), custom_call_target="tpu_custom_call" | custom-call | flops 13200000000 | bytes 42000000 | tf_op jit(solution)/shard_map/project/pallas_call | solution.py:539
  133.5 28.1 %attend.1 = (bf16[1024,768]{1,0:T(8,128)(2,1)}, f32[2,6,8,512]{3,2,1,0:T(8,128)}) custom-call(s32[2]{0:T(128)} %get-tuple-element.200.valid_ref, bf16[3,1024,768]{2,1,0:T(8,128)(2,1)} %get-tuple-element.70.q_ref.k_ref.v_ref, bf16[3,1024,768]{2,1,0:T(8,128)(2,1)} %get-tuple-element.70.q_ref.k_ref.v_ref, ...), custom_call_target="tpu_custom_call" | custom-call | flops 30799998976 | bytes 98000000 | tf_op jit(solution)/shard_map/attend/pallas_call | solution.py:307
  161.6 25.2 %all-gather.2.cloned.1.call-done.refs_0_ = bf16[16,432,768]{2,1,0:T(8,128)(2,1)} async-done(((bf16[1,432,768]{2,1,0:T(8,128)(2,1)}), bf16[16,432,768]{2,1,0:T(8,128)(2,1)}) %all-gather.2.cloned.1.call-update) | async-done | bytes 10616848 | tf_op jit(solution)/shard_map/all_gather | solution.py:1034
  187.3 6.0 %output.1 = (f32[1024,768]{1,0:T(8,128)}, bf16[1024,768]{1,0:T(8,128)(2,1)}, bf16[16,48,768]{2,1,0:T(8,128)(2,1)}) custom-call(s32[16]{0:T(128)} %iota.46.where_ref, bf16[1024,768]{1,0:T(8,128)(2,1)} %get-tuple-element.71.mixed_ref, f32[1024,1]{1,0:T(8,128)} %bitcast.257, bf16[16,432,768]{2,1,0:T(8,128)(2,1)} %all-gather.2.cloned.1.call-done.refs_0_), custom_call_target="tpu_custom_call" | custom-call | flops 5500000256 | bytes 17500000 | tf_op jit(solution)/shard_map/output/pallas_call | solution.py:580
  194.5 3.3 collective-permute-done.17
  201.8 24.7 %feed.1 = (f32[1024,768]{1,0:T(8,128)}, bf16[1024,768]{1,0:T(8,128)(2,1)}, f32[1024,768]{1,0:T(8,128)}, f32[1024,1]{1,0:T(8,128)}, bf16[1024,3072]{1,0:T(8,128)(...) custom-call(s32[16]{0:T(128)} %iota.41.where_ref, f32[1024,768]{1,0:T(8,128)} %get-tuple-element.69.inputs_ref, ...), custom_call_target="tpu_custom_call" | custom-call | flops 26400000000 | bytes 84000000 | tf_op jit(solution)/shard_map/feed/pallas_call | solution.py:635
  227.0 13.1 %close.1 = (bf16[1024,768]{1,0:T(8,128)(2,1)}, f32[1024,768]{1,0:T(8,128)}, bf16[1024,768]{1,0:T(8,128)(2,1)}, f32[8,768]{1,0:T(8,128)}, bf16[16,192,768]{2,1,0:T(8,128)(2,1)}) custom-call(s32[16]{0:T(128)} %iota.40.where_ref, bf16[1024,3072]{1,0:T(8,128)(2,1)} %get-tuple-element.74.active_ref, f32[1024,768]{1,0:T(8,128)} %get-tuple-element.75.u_ref, ...), custom_call_target="tpu_custom_call" | custom-call | flops 14300000256 | bytes 45500000 | tf_op jit(solution)/shard_map/close/pallas_call | solution.py:698
  240.6 10.0 %second.1 = bf16[16,192,768]{2,1,0:T(8,128)(2,1)} custom-call(s32[16]{0:T(128)} %iota.49.slots_ref, bf16[1024,3072]{1,0:T(8,128)(2,1)} %get-tuple-element.74.active_ref, bf16[1024,768]{1,0:T(8,128)(2,1)} %get-tuple-element.81.low_ref), custom_call_target="tpu_custom_call" | custom-call | flops 11000000512 | bytes 35000000 | tf_op jit(solution)/shard_map/second/pallas_call | solution.py:746
  250.6 26.2 %feed_back.1 = (f32[1024,768]{1,0:T(8,128)}, bf16[1024,768]{1,0:T(8,128)(2,1)}, bf16[16,48,3072]{2,1,0:T(8,128)(2,1)}, f32[1,3072]{1,0:T(1,128)}, f32[8,768]{1,0:T(8,128)}) custom-call(s32[16]{0:T(128)} %fusion.49.slots_ref, bf16[1024,768]{1,0:T(8,128)(2,1)} %get-tuple-element.79.rows_ref, bf16[1024,768]{1,0:T(8,128)(2,1)} %get-tuple-element.81.low_ref, ...), custom_call_target="tpu_custom_call" | custom-call | flops 28600000512 | bytes 91000000 | tf_op jit(solution)/shard_map/feed_back/pallas_call | solution.py:795
  279.9 4.2 fusion.87
  289.7 2.4 select_bitcast_fusion.2
  292.1 7.5 %middle.1 = (bf16[1024,768]{1,0:T(8,128)(2,1)}, bf16[16,48,768]{2,1,0:T(8,128)(2,1)}) custom-call(s32[16]{0:T(128)} %fusion.49.slots_ref, f32[1024,768]{1,0:T(8,128)} %get-tuple-element.88.own_ref.dpre_ref, bf16[1024,768]{1,0:T(8,128)(2,1)} %collective-permute-done.19.other_ref, f32[1024,1]{1,0:T(8,128)} %bitcast.259, ...), custom_call_target="tpu_custom_call" | custom-call | flops 8800000000 | bytes 28000000 | tf_op jit(solution)/shard_map/middle/pallas_call | solution.py:847
  299.6 41.9 %attend_back.1 = (bf16[3,1024,768]{2,1,0:T(8,128)(2,1)}, f32[12,8,512]{2,1,0:T(8,128)}) custom-call(s32[2]{0:T(128)} %get-tuple-element.200.valid_ref, bf16[3,1024,768]{2,1,0:T(8,128)(2,1)} %get-tuple-element.70.q_ref.k_ref.v_ref, bf16[3,1024,768]{2,1,0:T(8,128)(2,1)} %get-tuple-element.70.q_ref.k_ref.v_ref, ...), custom_call_target="tpu_custom_call" | custom-call | flops 45099999232 | bytes 143500000 | tf_op jit(solution)/shard_map/attend_back/pallas_call | solution.py:424
  355.7 2.7 add_convert_fusion
  359.7 2.0 collective-permute-start.28
  361.7 2.5 collective-permute-done.23
  365.7 6.2 %collective-permute-done.25 = bf16[4,48,768]{2,1,0:T(8,128)(2,1)} collective-permute-done((bf16[4,48,768]{2,1,0:T(8,128)(2,1)S(1)}, bf16[4,48,768]{2,1,0:T(8,128)(2,1)}, u32[]{:S(2)}, u32[]{:S(2)}) %collective-permute-start.25) | collective-permute-done | bytes 294944 | tf_op jit(solution)/shard_map/ppermute | solution.py:73
  373.1 21.7 %grads.1 = (bf16[16,160,768]{2,1,0:T(8,128)(2,1)}, f32[1024,768]{1,0:T(8,128)}, f32[8,768]{1,0:T(8,128)}) custom-call(s32[16]{0:T(128)} %fusion.49.slots_ref, bf16[1024,768]{1,0:T(8,128)(2,1)} %get-tuple-element.77.joint_ref, bf16[1024,768]{1,0:T(8,128)(2,1)} %get-tuple-element.78.plain_ref, bf16[3,1024,768]{2,1,0:T(8,128)(2,1)} %get-tuple-element.98.grad_ref, ...), custom_call_target="tpu_custom_call" | custom-call | flops 13200000000 | bytes 42000000 | tf_op jit(solution)/shard_map/grads/pallas_call | solution.py:918
  396.3 1.9 collective-permute-start.41
  398.1 3.9 fusion.88
  403.2 1.8 multiply_reduce_fusion
  405.0 2.1 collective-permute-done.42
  409.1 1.7 collective-permute-start.31
  412.3 2.0 collective-permute-done.43
  415.2 3.1 collective-permute-start.45
  421.4 2.8 collective-permute-start.38
  424.2 1.9 collective-permute-done.37
  435.8 15.6 %collective-permute-done.31 = bf16[4,160,768]{2,1,0:T(8,128)(2,1)} collective-permute-done((bf16[4,160,768]{2,1,0:T(8,128)(2,1)}, bf16[4,160,768]{2,1,0:T(8,128)(2,1)}, u32[]{:S(2)}, u32[]{:S(2)}) %collective-permute-start.31) | collective-permute-done | bytes 983072 | tf_op jit(solution)/shard_map/ppermute | solution.py:73
  451.4 2.3 add_convert_fusion.1
  460.0 2.7 stack.351
  464.3 6.4 %collective-permute-done.34 = bf16[160,768]{1,0:T(8,128)(2,1)S(1)} collective-permute-done((bf16[160,768]{1,0:T(8,128)(2,1)S(1)}, bf16[160,768]{1,0:T(8,128)(2,1)S(1)}, u32[]{:S(2)}, u32[]{:S(2)}) %collective-permute-start.34) | collective-permute-done | bytes 245792 | tf_op jit(solution)/shard_map/ppermute | solution.py:63
  474.7 1.7 fusion.5
  477.6 1.7 multiply_reduce_fusion.1
  484.4 1.8 broadcast_select_fusion.2
  487.9 1.8 collective-permute-start.50
  489.8 3.8 select_bitcast_fusion
  493.7 2.8 collective-permute-start.51
  499.2 1.8 collective-permute-done.52
  504.3 2.8 fusion.82
  509.2 2.9 fusion.84
  (461 shorter events, 109.1 us)
Async XLA Ops:
  7.2 179.6 %all-gather.2.cloned.1.call-start = ((), (), s32[]{:S(2)}) async-start(), calls=%async_computation.1 | async-start | bytes 11280384 | tf_op jit(solution)/shard_map/all_gather | solution.py:1034
  12.9 464.7 %reduce-scatter.2.cloned.1.call-start = ((), (), s32[]{:S(2)}) async-start(), calls=%async_computation.2 | async-start | bytes 5013504 | tf_op jit(solution)/shard_map/reduce_scatter | solution.py:1140
  15.3 43.2 %collective-permute-start.1 = (s32[1,2,512]{2,1,0:T(2,128)S(1)}, s32[1,2,512]{2,1,0:T(2,128)S(1)}, u32[]{:S(2)}, u32[]{:S(2)}) collective-permute-start(s32[1,2,512]{2,1,0:T(2,128)S(1)} %copy-done.54), channel_id=1, source_target_pairs={{0,1},{1,0},{2,3},{3,2},{4,5},{5,4},{6,7},{7,6},{8,9},{9,8},{10,11... | collective-permute-start | bytes 12296 | tf_op jit(solution)/shard_map/ppermute | solution.py:58
  15.6 12.0 %collective-permute-start.13 = (s32[1]{0:T(128)}, s32[1]{0:T(128)}, u32[]{:S(2)}, u32[]{:S(2)}) collective-permute-start(s32[1]{0:T(128)} %param.31), channel_id=1, source_target_pairs={{0,1},{1,0},{2,3},{3,2},{4,5},{5,4},{6,7},{7,6},{8,9},{9,8},{10,11... | collective-permute-start | bytes 20 | tf_op jit(solution)/shard_map/ppermute | solution.py:58
  18.8 14.2 %collective-permute-start.6 = (bf16[176,768]{1,0:T(8,128)(2,1)S(1)}, bf16[176,768]{1,0:T(8,128)(2,1)S(1)}, u32[]{:S(2)}, u32[]{:S(2)}) collective-permute-start(bf16[176,768]{1,0:T(8,128)(2,1)S(1)} %get-tuple-element.246), channel_id=1, source_target_pairs={{0,8},{8,16},{16,24},{24,0},{1,9},{9,17},{17,25},{25,1},{2,10},{10... | collective-permute-start | bytes 811016 | tf_op jit(solution)/shard_map/ppermute | solution.py:63
  21.8 32.3 %collective-permute-start.7 = (bf16[176,768]{1,0:T(8,128)(2,1)S(1)}, bf16[176,768]{1,0:T(8,128)(2,1)S(1)}, u32[]{:S(2)}, u32[]{:S(2)}) collective-permute-start(bf16[176,768]{1,0:T(8,128)(2,1)S(1)} %get-tuple-element.246), channel_id=1, source_target_pairs={{0,16},{8,24},{16,0},{24,8},{1,17},{9,25},{17,1},{25,9},{2,18},{10... | collective-permute-start | bytes 811016 | tf_op jit(solution)/shard_map/ppermute | solution.py:63
  24.4 29.7 %collective-permute-start.8 = (bf16[176,768]{1,0:T(8,128)(2,1)S(1)}, bf16[176,768]{1,0:T(8,128)(2,1)S(1)}, u32[]{:S(2)}, u32[]{:S(2)}) collective-permute-start(bf16[176,768]{1,0:T(8,128)(2,1)S(1)} %get-tuple-element.246), channel_id=1, source_target_pairs={{0,24},{8,0},{16,8},{24,16},{1,25},{9,1},{17,9},{25,17},{2,26},{10... | collective-permute-start | bytes 811016 | tf_op jit(solution)/shard_map/ppermute | solution.py:63
  27.7 51.0 %collective-permute-start = (bf16[512,768]{1,0:T(8,128)(2,1)}, bf16[512,768]{1,0:T(8,128)(2,1)}, u32[]{:S(2)}, u32[]{:S(2)}) collective-permute-start(bf16[512,768]{1,0:T(8,128)(2,1)} %get-tuple-element.217), channel_id=1, source_target_pairs={{0,1},{1,0},{2,3},{3,2},{4,5},{5,4},{6,7},{7,6},{8,9},{9,8},{10,11... | collective-permute-start | bytes 2359304 | tf_op jit(solution)/shard_map/ppermute | solution.py:58
  54.3 15.4 %collective-permute-start.11 = (bf16[4,176,384]{2,1,0:T(8,128)(2,1)S(1)}, bf16[4,176,384]{2,1,0:T(8,128)(2,1)S(1)}, u32[]{:S(2)}, u32[]{:S(2)}) collective-permute-start(bf16[4,176,384]{2,1,0:T(8,128)(2,1)S(1)} %get-tuple-element.225), channel_id=1, source_target_pairs={{0,4},{4,0},{1,5},{5,1},{2,6},{6,2},{3,7},{7,3},{8,12},{12,8},{9,1... | collective-permute-start | bytes 1622024 | tf_op jit(solution)/shard_map/ppermute | solution.py:63
  57.0 19.1 %collective-permute-start.9 = (bf16[4,176,384]{2,1,0:T(8,128)(2,1)S(1)}, bf16[4,176,384]{2,1,0:T(8,128)(2,1)S(1)}, u32[]{:S(2)}, u32[]{:S(2)}) collective-permute-start(bf16[4,176,384]{2,1,0:T(8,128)(2,1)S(1)} %get-tuple-element.226), channel_id=1, source_target_pairs={{0,2},{2,0},{1,3},{3,1},{4,6},{6,4},{5,7},{7,5},{8,10},{10,8},{9,1... | collective-permute-start | bytes 1622024 | tf_op jit(solution)/shard_map/ppermute | solution.py:63
  69.9 43.0 %collective-permute-start.12 = (bf16[8,176,384]{2,1,0:T(8,128)(2,1)S(1)}, bf16[8,176,384]{2,1,0:T(8,128)(2,1)S(1)}, u32[]{:S(2)}, u32[]{:S(2)}) collective-permute-start(bf16[8,176,384]{2,1,0:T(8,128)(2,1)S(1)} %pad_maximum_fusion.3.refs_2_), channel_id=1, source_target_pairs={{0,2},{2,0},{1,3},{3,1},{4,6},{6,4},{5,7},{7,5},{8,10},{10,8},{9,1... | collective-permute-start | bytes 3244040 | tf_op jit(solution)/shard_map/ppermute | solution.py:63
  77.2 37.4 %collective-permute-start.10 = (bf16[8,176,384]{2,1,0:T(8,128)(2,1)}, bf16[8,176,384]{2,1,0:T(8,128)(2,1)}, u32[]{:S(2)}, u32[]{:S(2)}) collective-permute-start(bf16[8,176,384]{2,1,0:T(8,128)(2,1)} %pad_maximum_fusion.2.refs_0_), channel_id=1, source_target_pairs={{0,4},{4,0},{1,5},{5,1},{2,6},{6,2},{3,7},{7,3},{8,12},{12,8},{9,1... | collective-permute-start | bytes 3244040 | tf_op jit(solution)/shard_map/ppermute | solution.py:63
  193.3 7.3 %collective-permute-start.16 = (bf16[1024,768]{1,0:T(8,128)(2,1)}, bf16[1024,768]{1,0:T(8,128)(2,1)S(1)}, u32[]{:S(2)}, u32[]{:S(2)}) collective-permute-start(bf16[1024,768]{1,0:T(8,128)(2,1)} %get-tuple-element.73), channel_id=1, source_target_pairs={{0,1},{1,0},{2,3},{3,2},{4,5},{5,4},{6,7},{7,6},{8,9},{9,8},{10,11... | collective-permute-start | bytes 4718600 | tf_op jit(solution)/shard_map/ppermute | solution.py:58
  276.8 15.3 %collective-permute-start.19 = (bf16[1024,768]{1,0:T(8,128)(2,1)}, bf16[1024,768]{1,0:T(8,128)(2,1)}, u32[]{:S(2)}, u32[]{:S(2)}) collective-permute-start(bf16[1024,768]{1,0:T(8,128)(2,1)} %get-tuple-element.89), channel_id=1, source_target_pairs={{0,1},{1,0},{2,3},{3,2},{4,5},{5,4},{6,7},{7,6},{8,9},{9,8},{10,11... | collective-permute-start | bytes 4718600 | tf_op jit(solution)/shard_map/ppermute | solution.py:58
  279.5 10.3 %collective-permute-start.18 = (bf16[512,768]{1,0:T(8,128)(2,1)S(1)}, bf16[512,768]{1,0:T(8,128)(2,1)}, u32[]{:S(2)}, u32[]{:S(2)}) collective-permute-start(bf16[512,768]{1,0:T(8,128)(2,1)S(1)} %slice.474), channel_id=1, source_target_pairs={{0,1},{1,0},{2,3},{3,2},{4,5},{5,4},{6,7},{7,6},{8,9},{9,8},{10,11... | collective-permute-start | bytes 2359304 | tf_op jit(solution)/shard_map/ppermute | solution.py:58
  284.1 70.1 %collective-permute-start.20 = (bf16[4,48,3072]{2,1,0:T(8,128)(2,1)}, bf16[4,48,3072]{2,1,0:T(8,128)(2,1)}, u32[]{:S(2)}, u32[]{:S(2)}) collective-permute-start(bf16[4,48,3072]{2,1,0:T(8,128)(2,1)} %get-tuple-element.207), channel_id=1, source_target_pairs={{0,2},{2,0},{4,6},{6,4},{1,3},{3,1},{5,7},{7,5},{8,10},{10,8},{12,... | collective-permute-start | bytes 3538952 | tf_op jit(solution)/shard_map/ppermute | solution.py:73
  285.6 70.1 %collective-permute-start.21 = (bf16[4,48,3072]{2,1,0:T(8,128)(2,1)}, bf16[4,48,3072]{2,1,0:T(8,128)(2,1)}, u32[]{:S(2)}, u32[]{:S(2)}) collective-permute-start(bf16[4,48,3072]{2,1,0:T(8,128)(2,1)} %get-tuple-element.206), channel_id=1, source_target_pairs={{0,4},{2,6},{4,0},{6,2},{1,5},{3,7},{5,1},{7,3},{8,12},{10,14},{12... | collective-permute-start | bytes 3538952 | tf_op jit(solution)/shard_map/ppermute | solution.py:73
  286.2 69.5 %collective-permute-start.22 = (bf16[4,48,3072]{2,1,0:T(8,128)(2,1)}, bf16[4,48,3072]{2,1,0:T(8,128)(2,1)}, u32[]{:S(2)}, u32[]{:S(2)}) collective-permute-start(bf16[4,48,3072]{2,1,0:T(8,128)(2,1)} %get-tuple-element.205), channel_id=1, source_target_pairs={{0,6},{2,4},{4,2},{6,0},{1,7},{3,5},{5,3},{7,1},{8,14},{10,12},{12... | collective-permute-start | bytes 3538952 | tf_op jit(solution)/shard_map/ppermute | solution.py:73
  352.0 12.2 %collective-permute-start.23 = (bf16[4,48,768]{2,1,0:T(8,128)(2,1)S(1)}, bf16[4,48,768]{2,1,0:T(8,128)(2,1)}, u32[]{:S(2)}, u32[]{:S(2)}) collective-permute-start(bf16[4,48,768]{2,1,0:T(8,128)(2,1)S(1)} %get-tuple-element.224), channel_id=1, source_target_pairs={{0,2},{2,0},{4,6},{6,4},{1,3},{3,1},{5,7},{7,5},{8,10},{10,8},{12,... | collective-permute-start | bytes 884744 | tf_op jit(solution)/shard_map/ppermute | solution.py:73
  353.5 12.1 %collective-permute-start.24 = (bf16[4,48,768]{2,1,0:T(8,128)(2,1)S(1)}, bf16[4,48,768]{2,1,0:T(8,128)(2,1)}, u32[]{:S(2)}, u32[]{:S(2)}) collective-permute-start(bf16[4,48,768]{2,1,0:T(8,128)(2,1)S(1)} %get-tuple-element.223), channel_id=1, source_target_pairs={{0,4},{2,6},{4,0},{6,2},{1,5},{3,7},{5,1},{7,3},{8,12},{10,14},{12... | collective-permute-start | bytes 884744 | tf_op jit(solution)/shard_map/ppermute | solution.py:73
  354.2 17.6 %collective-permute-start.25 = (bf16[4,48,768]{2,1,0:T(8,128)(2,1)S(1)}, bf16[4,48,768]{2,1,0:T(8,128)(2,1)}, u32[]{:S(2)}, u32[]{:S(2)}) collective-permute-start(bf16[4,48,768]{2,1,0:T(8,128)(2,1)S(1)} %get-tuple-element.222), channel_id=1, source_target_pairs={{0,6},{2,4},{4,2},{6,0},{1,7},{3,5},{5,3},{7,1},{8,14},{10,12},{12... | collective-permute-start | bytes 884744 | tf_op jit(solution)/shard_map/ppermute | solution.py:73
  359.6 42.4 %collective-permute-start.27 = (bf16[48,3072]{1,0:T(8,128)(2,1)}, bf16[48,3072]{1,0:T(8,128)(2,1)}, u32[]{:S(2)}, u32[]{:S(2)}) collective-permute-start(bf16[48,3072]{1,0:T(8,128)(2,1)} %get-tuple-element.218), channel_id=1, source_target_pairs={{0,8},{8,16},{16,24},{24,0},{1,9},{9,17},{17,25},{25,1},{2,10},{10... | collective-permute-start | bytes 884744 | tf_op jit(solution)/shard_map/ppermute | solution.py:63
  359.7 43.5 %collective-permute-start.28 = (bf16[48,3072]{1,0:T(8,128)(2,1)}, bf16[48,3072]{1,0:T(8,128)(2,1)}, u32[]{:S(2)}, u32[]{:S(2)}) collective-permute-start(bf16[48,3072]{1,0:T(8,128)(2,1)} %get-tuple-element.220), channel_id=1, source_target_pairs={{0,16},{8,24},{16,0},{24,8},{1,17},{9,25},{17,1},{25,9},{2,18},{10... | collective-permute-start | bytes 884744 | tf_op jit(solution)/shard_map/ppermute | solution.py:63
  364.2 39.0 %collective-permute-start.29 = (bf16[48,3072]{1,0:T(8,128)(2,1)}, bf16[48,3072]{1,0:T(8,128)(2,1)S(1)}, u32[]{:S(2)}, u32[]{:S(2)}) collective-permute-start(bf16[48,3072]{1,0:T(8,128)(2,1)} %get-tuple-element.219), channel_id=1, source_target_pairs={{0,24},{8,0},{16,8},{24,16},{1,25},{9,1},{17,9},{25,17},{2,26},{10... | collective-permute-start | bytes 884744 | tf_op jit(solution)/shard_map/ppermute | solution.py:63
  395.8 9.3 %collective-permute-start.40 = (bf16[24,768]{1,0:T(8,128)(2,1)S(1)}, bf16[24,768]{1,0:T(8,128)(2,1)S(1)}, u32[]{:S(2)}, u32[]{:S(2)}) collective-permute-start(bf16[24,768]{1,0:T(8,128)(2,1)S(1)} %pad.42), channel_id=1, source_target_pairs={{0,2},{2,0},{4,6},{6,4},{1,3},{3,1},{5,7},{7,5},{8,10},{10,8},{12,... | collective-permute-start | bytes 110600 | tf_op jit(solution)/shard_map/ppermute | solution.py:73
  396.3 8.8 %collective-permute-start.41 = (bf16[24,768]{1,0:T(8,128)(2,1)S(1)}, bf16[24,768]{1,0:T(8,128)(2,1)S(1)}, u32[]{:S(2)}, u32[]{:S(2)}) collective-permute-start(bf16[24,768]{1,0:T(8,128)(2,1)S(1)} %pad.42), channel_id=1, source_target_pairs={{0,4},{2,6},{4,0},{6,2},{1,5},{3,7},{5,1},{7,3},{8,12},{10,14},{12... | collective-permute-start | bytes 110600 | tf_op jit(solution)/shard_map/ppermute | solution.py:73
  402.0 5.1 collective-permute-start.42
  407.2 7.1 %collective-permute-start.43 = (bf16[24,768]{1,0:T(8,128)(2,1)S(1)}, bf16[24,768]{1,0:T(8,128)(2,1)S(1)}, u32[]{:S(2)}, u32[]{:S(2)}) collective-permute-start(bf16[24,768]{1,0:T(8,128)(2,1)S(1)} %add_convert_fusion.4), channel_id=1, source_target_pairs={{0,8},{8,16},{16,24},{24,0},{1,9},{9,17},{17,25},{25,1},{2,10},{10... | collective-permute-start | bytes 110600 | tf_op jit(solution)/shard_map/ppermute | solution.py:63
  407.3 8.0 %collective-permute-start.44 = (bf16[24,768]{1,0:T(8,128)(2,1)S(1)}, bf16[24,768]{1,0:T(8,128)(2,1)S(1)}, u32[]{:S(2)}, u32[]{:S(2)}) collective-permute-start(bf16[24,768]{1,0:T(8,128)(2,1)S(1)} %add_convert_fusion.4), channel_id=1, source_target_pairs={{0,16},{8,24},{16,0},{24,8},{1,17},{9,25},{17,1},{25,9},{2,18},{10... | collective-permute-start | bytes 110600 | tf_op jit(solution)/shard_map/ppermute | solution.py:63
  408.7 27.1 %collective-permute-start.30 = (bf16[4,160,768]{2,1,0:T(8,128)(2,1)}, bf16[4,160,768]{2,1,0:T(8,128)(2,1)S(1)}, u32[]{:S(2)}, u32[]{:S(2)}) collective-permute-start(bf16[4,160,768]{2,1,0:T(8,128)(2,1)} %get-tuple-element.211), channel_id=1, source_target_pairs={{0,2},{2,0},{4,6},{6,4},{1,3},{3,1},{5,7},{7,5},{8,10},{10,8},{12,... | collective-permute-start | bytes 2949128 | tf_op jit(solution)/shard_map/ppermute | solution.py:73
  409.1 42.3 %collective-permute-start.31 = (bf16[4,160,768]{2,1,0:T(8,128)(2,1)}, bf16[4,160,768]{2,1,0:T(8,128)(2,1)}, u32[]{:S(2)}, u32[]{:S(2)}) collective-permute-start(bf16[4,160,768]{2,1,0:T(8,128)(2,1)} %get-tuple-element.210), channel_id=1, source_target_pairs={{0,4},{2,6},{4,0},{6,2},{1,5},{3,7},{5,1},{7,3},{8,12},{10,14},{12... | collective-permute-start | bytes 2949128 | tf_op jit(solution)/shard_map/ppermute | solution.py:73
  410.8 40.6 %collective-permute-start.32 = (bf16[4,160,768]{2,1,0:T(8,128)(2,1)}, bf16[4,160,768]{2,1,0:T(8,128)(2,1)}, u32[]{:S(2)}, u32[]{:S(2)}) collective-permute-start(bf16[4,160,768]{2,1,0:T(8,128)(2,1)} %get-tuple-element.209), channel_id=1, source_target_pairs={{0,6},{2,4},{4,2},{6,0},{1,7},{3,5},{5,3},{7,1},{8,14},{10,12},{12... | collective-permute-start | bytes 2949128 | tf_op jit(solution)/shard_map/ppermute | solution.py:73
  414.3 7.1 %collective-permute-start.36 = (bf16[48,768]{1,0:T(8,128)(2,1)S(1)}, bf16[48,768]{1,0:T(8,128)(2,1)S(1)}, u32[]{:S(2)}, u32[]{:S(2)}) collective-permute-start(bf16[48,768]{1,0:T(8,128)(2,1)S(1)} %get-tuple-element.236), channel_id=1, source_target_pairs={{0,8},{8,16},{16,24},{24,0},{1,9},{9,17},{17,25},{25,1},{2,10},{10... | collective-permute-start | bytes 221192 | tf_op jit(solution)/shard_map/ppermute | solution.py:63
  415.2 4.8 collective-permute-start.45
  420.0 6.1 %collective-permute-start.37 = (bf16[48,768]{1,0:T(8,128)(2,1)S(1)}, bf16[48,768]{1,0:T(8,128)(2,1)S(1)}, u32[]{:S(2)}, u32[]{:S(2)}) collective-permute-start(bf16[48,768]{1,0:T(8,128)(2,1)S(1)} %get-tuple-element.238), channel_id=1, source_target_pairs={{0,16},{8,24},{16,0},{24,8},{1,17},{9,25},{17,1},{25,9},{2,18},{10... | collective-permute-start | bytes 221192 | tf_op jit(solution)/shard_map/ppermute | solution.py:63
  421.4 6.0 %collective-permute-start.38 = (bf16[48,768]{1,0:T(8,128)(2,1)S(1)}, bf16[48,768]{1,0:T(8,128)(2,1)S(1)}, u32[]{:S(2)}, u32[]{:S(2)}) collective-permute-start(bf16[48,768]{1,0:T(8,128)(2,1)S(1)} %get-tuple-element.237), channel_id=1, source_target_pairs={{0,24},{8,0},{16,8},{24,16},{1,25},{9,1},{17,9},{25,17},{2,26},{10... | collective-permute-start | bytes 221192 | tf_op jit(solution)/shard_map/ppermute | solution.py:63
  426.1 78.1 %collective-permute-start.55 = (f32[24,3072]{1,0:T(8,128)}, f32[24,3072]{1,0:T(8,128)}, u32[]{:S(2)}, u32[]{:S(2)}) collective-permute-start(f32[24,3072]{1,0:T(8,128)} %get-tuple-element.232), channel_id=1, source_target_pairs={{0,1},{1,0},{2,3},{3,2},{4,5},{5,4},{6,7},{7,6},{8,9},{9,8},{10,11... | collective-permute-start | bytes 884744 | tf_op jit(solution)/shard_map/ppermute | solution.py:58
  429.0 58.9 %collective-permute-start.26 = (f32[512,768]{1,0:T(8,128)S(1)}, f32[512,768]{1,0:T(8,128)}, u32[]{:S(2)}, u32[]{:S(2)}) collective-permute-start(f32[512,768]{1,0:T(8,128)S(1)} %slice.484), channel_id=1, source_target_pairs={{0,1},{1,0},{2,3},{3,2},{4,5},{5,4},{6,7},{7,6},{8,9},{9,8},{10,11... | collective-permute-start | bytes 4718600 | tf_op jit(solution)/shard_map/ppermute | solution.py:58
  454.4 9.9 %collective-permute-start.33 = (bf16[160,768]{1,0:T(8,128)(2,1)}, bf16[160,768]{1,0:T(8,128)(2,1)S(1)}, u32[]{:S(2)}, u32[]{:S(2)}) collective-permute-start(bf16[160,768]{1,0:T(8,128)(2,1)} %get-tuple-element.227), channel_id=1, source_target_pairs={{0,8},{8,16},{16,24},{24,0},{1,9},{9,17},{17,25},{25,1},{2,10},{10... | collective-permute-start | bytes 737288 | tf_op jit(solution)/shard_map/ppermute | solution.py:63
  455.8 15.0 %collective-permute-start.34 = (bf16[160,768]{1,0:T(8,128)(2,1)S(1)}, bf16[160,768]{1,0:T(8,128)(2,1)S(1)}, u32[]{:S(2)}, u32[]{:S(2)}) collective-permute-start(bf16[160,768]{1,0:T(8,128)(2,1)S(1)} %get-tuple-element.229), channel_id=1, source_target_pairs={{0,16},{8,24},{16,0},{24,8},{1,17},{9,25},{17,1},{25,9},{2,18},{10... | collective-permute-start | bytes 737288 | tf_op jit(solution)/shard_map/ppermute | solution.py:63
  457.1 14.4 %collective-permute-start.35 = (bf16[160,768]{1,0:T(8,128)(2,1)S(1)}, bf16[160,768]{1,0:T(8,128)(2,1)}, u32[]{:S(2)}, u32[]{:S(2)}) collective-permute-start(bf16[160,768]{1,0:T(8,128)(2,1)S(1)} %get-tuple-element.228), channel_id=1, source_target_pairs={{0,24},{8,0},{16,8},{24,16},{1,25},{9,1},{17,9},{25,17},{2,26},{10... | collective-permute-start | bytes 737288 | tf_op jit(solution)/shard_map/ppermute | solution.py:63
  486.2 23.0 %collective-permute-start.54 = (f32[4,24,768]{2,1,0:T(8,128)}, f32[4,24,768]{2,1,0:T(8,128)}, u32[]{:S(2)}, u32[]{:S(2)}) collective-permute-start(f32[4,24,768]{2,1,0:T(8,128)} %get-tuple-element.234), channel_id=1, source_target_pairs={{0,1},{1,0},{2,3},{3,2},{4,5},{5,4},{6,7},{7,6},{8,9},{9,8},{10,11... | collective-permute-start | bytes 884744 | tf_op jit(solution)/shard_map/ppermute | solution.py:58
  486.2 7.5 %collective-permute-start.48 = (f32[8,128]{1,0:T(8,128)S(1)}, f32[8,128]{1,0:T(8,128)S(1)}, u32[]{:S(2)}, u32[]{:S(2)}) collective-permute-start(f32[8,128]{1,0:T(8,128)S(1)} %broadcast_add_fusion), channel_id=1, source_target_pairs={{0,2},{2,0},{4,6},{6,4},{1,3},{3,1},{5,7},{7,5},{8,10},{10,8},{12,... | collective-permute-start | bytes 12296 | tf_op jit(solution)/shard_map/ppermute | solution.py:73
  487.1 6.6 %collective-permute-start.49 = (f32[8,128]{1,0:T(8,128)S(1)}, f32[8,128]{1,0:T(8,128)S(1)}, u32[]{:S(2)}, u32[]{:S(2)}) collective-permute-start(f32[8,128]{1,0:T(8,128)S(1)} %broadcast_add_fusion), channel_id=1, source_target_pairs={{0,4},{2,6},{4,0},{6,2},{1,5},{3,7},{5,1},{7,3},{8,12},{10,14},{12... | collective-permute-start | bytes 12296 | tf_op jit(solution)/shard_map/ppermute | solution.py:73
  487.9 5.8 %collective-permute-start.50 = (f32[8,128]{1,0:T(8,128)S(1)}, f32[8,128]{1,0:T(8,128)S(1)}, u32[]{:S(2)}, u32[]{:S(2)}) collective-permute-start(f32[8,128]{1,0:T(8,128)S(1)} %broadcast_add_fusion), channel_id=1, source_target_pairs={{0,6},{2,4},{4,2},{6,0},{1,7},{3,5},{5,3},{7,1},{8,14},{10,12},{12... | collective-permute-start | bytes 12296 | tf_op jit(solution)/shard_map/ppermute | solution.py:73
  493.7 5.5 %collective-permute-start.51 = (f32[8,128]{1,0:T(8,128)S(1)}, f32[8,128]{1,0:T(8,128)S(1)}, u32[]{:S(2)}, u32[]{:S(2)}) collective-permute-start(f32[8,128]{1,0:T(8,128)S(1)} %add_add_fusion.3), channel_id=1, source_target_pairs={{0,8},{8,16},{16,24},{24,0},{1,9},{9,17},{17,25},{25,1},{2,10},{10... | collective-permute-start | bytes 12296 | tf_op jit(solution)/shard_map/ppermute | solution.py:63
  496.5 4.5 collective-permute-start.52
  499.2 12.9 %collective-permute-start.56 = (f32[96,768]{1,0:T(8,128)S(1)}, f32[96,768]{1,0:T(8,128)S(1)}, u32[]{:S(2)}, u32[]{:S(2)}) collective-permute-start(f32[96,768]{1,0:T(8,128)S(1)} %get-tuple-element.230), channel_id=1, source_target_pairs={{0,1},{1,0},{2,3},{3,2},{4,5},{5,4},{6,7},{7,6},{8,9},{9,8},{10,11... | collective-permute-start | bytes 884744 | tf_op jit(solution)/shard_map/ppermute | solution.py:58
  (72 other events, 424.0 us)
Sparse Core Ops, SparseCore 0:
  13.1 173.6 all-gather.1
  278.2 157.7 reduce-scatter.1

commit v3 on v2

--- a/solution.py
+++ b/solution.py
@@ -44,6 +44,17 @@
 
 def params_of():
     return pltpu.CompilerParams(vmem_limit_bytes=VMEM_LIMIT)
+
+
+def held(others):
+    return [pl.BlockSpec(memory_space=pl.ANY)] * len(others)
+
+
+def waiting(kernel, count, others):
+    def run(*refs):
+        kernel(*refs[:count], *refs[count + others :])
+
+    return run
 
 
 def dot(left, right):
@@ -149,26 +160,61 @@
             target[where_ref[index * count + k], :, begin : begin + width] = ref[k]
 
 
-def slot_table():
+def slot_table(turned=False):
     nz, ny, nx = (lax.axis_size(a) for a in CHIP)
     chips = jnp.arange(nz * ny * nx)
     zr = (chips // (ny * nx) - lax.axis_index("z")) % nz
     yr = (chips // nx % ny - lax.axis_index("y")) % ny
     xr = (chips % nx - lax.axis_index("x")) % nx
+    if turned:
+        return ((xr * ny + yr) * nz + zr).astype(jnp.int32)
     return ((yr * nx + xr) * nz + zr).astype(jnp.int32)
+
+
+def sum_kernel(count, *refs):
+    total = refs[0][...].astype(F32)
+    for ref in refs[1:count]:
+        total = total + ref[...].astype(F32)
+    refs[-1][...] = total.astype(refs[-1].dtype)
+
+
+def sum_call(own, moved, others, kind=BF):
+    shape = moved[0].shape
+    steps = 2 if shape[0] % 2 == 0 else 1
+    block = pl.BlockSpec((shape[0] // steps,) + shape[1:], lambda i: (i, 0, 0))
+    return pl.pallas_call(
+        functools.partial(sum_kernel, 1 + len(moved)),
+        grid=(steps,),
+        in_specs=[block] * (1 + len(moved)) + held(others),
+        out_specs=block,
+        out_shape=jax.ShapeDtypeStruct(shape, kind),
+        compiler_params=params_of(),
+        name="sum",
+        cost_estimate=cost(2),
+    )(own, *moved, *others)
 
 
 def scatter_plane(slots, others=()):
     nz = lax.axis_size("z")
-    total = after(slots[:nz], others).astype(F32)
-    for index, (sy, sx) in enumerate(plane_steps()):
-        if index:
-            part = diagonal(slots[nz * index : nz * index + nz], sy, sx)
-            total = total + part.astype(F32)
-    return total.astype(BF)
-
-
-def scatter_line(column):
+    moved = [
+        diagonal(slots[nz * index : nz * index + nz], sy, sx)
+        for index, (sy, sx) in enumerate(plane_steps())
+        if index
+    ]
+    return sum_call(slots, moved, others)
+
+
+def scatter_step(slots, axis, others=()):
+    size = lax.axis_size(axis)
+    count = slots.shape[0] // size
+    moved = [shift(slots[count * k : count * k + count], axis, k) for k in range(1, size)]
+    return sum_call(slots, moved, others)
+
+
+def scatter_line(column, others=None):
+    if others is not None:
+        moved = [shift(column[k : k + 1], "z", k) for k in range(1, lax.axis_size("z"))]
+        return sum_call(column, moved, others, F32)[0]
     total = column[0].astype(F32)
     for k in range(1, lax.axis_size("z")):
         total = total + shift(column[k], "z", k).astype(F32)
@@ -207,23 +253,24 @@
     return jnp.pad(rows, ((0, 0), (0, 6), (0, 0)))
 
 
+def sum_map():
+    half = NR // 2
+    found = np.zeros((3, 512, 3, NR), np.float32)
+
+    def entry(distance):
+        return min(max(distance, -half), half - 1) + half
+
+    for k in range(512):
+        found[0, k, 0, entry(128 - k if k < 384 else 640 - k)] = 1.0
+        lane = k % 256
+        found[1, k, 1 + k // 256, entry(-lane if lane < 128 else 256 - lane)] = 1.0
+        found[2, k, 0, NR - 1 if k < 256 else 0] = 1.0
+    return found.reshape(3 * 512, 3 * NR)
+
+
 def table_sums(sums):
-    half = NR // 2
-    line = jnp.concatenate([sums[:, 0, 384:], sums[:, 0, :384]], axis=1)[:, ::-1]
-    far = jnp.sum(sums[:, 2, 256:], axis=1) + jnp.sum(line[:, : 256 - half], axis=1)
-    near = jnp.sum(sums[:, 2, :256], axis=1) + jnp.sum(line[:, 254 + half :], axis=1)
-    middle = line[:, 256 - half : 254 + half]
-    first = jnp.concatenate([far[:, None], middle, near[:, None]], axis=1)
-
-    def plane(part):
-        ordered = jnp.concatenate([part[:, 128:], part[:, :128]], axis=1)[:, ::-1]
-        low = jnp.sum(ordered[:, : 128 - half], axis=1)
-        high = jnp.sum(ordered[:, 126 + half :], axis=1)
-        return jnp.concatenate(
-            [low[:, None], ordered[:, 128 - half : 126 + half], high[:, None]], axis=1
-        )
-
-    return jnp.stack([first, plane(sums[:, 1, :256]), plane(sums[:, 1, 256:])])
+    flat = sums[:, :3].reshape(sums.shape[0], -1)
+    return jnp.dot(flat, jnp.asarray(sum_map()), precision=lax.Precision.HIGHEST)
 
 
 def build_tables(base, strip, planes, head):
@@ -412,17 +459,15 @@
             sums_ref[head, 2:3, 256:] = jnp.sum(d_strip[head, :, 640:], axis=0, keepdims=True)
 
 
-def attend_back_call(valid, projected, d_mixed, mixed, log_total, both, base, count):
+def attend_back_call(valid, projected, d_mixed, mixed, log_total, both, both_t, base, count, first, pairs, others=()):
     pages = projected.shape[1] // count
-    pairs = H // 2
-    both_t = both.T
 
     def part(index):
-        return pl.BlockSpec((None, count, 128), lambda pair, page: (index, page, pair))
-
-    wide = pl.BlockSpec((count, 128), lambda pair, page: (page, pair))
+        return pl.BlockSpec((None, count, 128), lambda pair, page: (index, page, first + pair))
+
+    wide = pl.BlockSpec((count, 128), lambda pair, page: (page, first + pair))
     return pl.pallas_call(
-        attend_back_kernel,
+        waiting(attend_back_kernel, 10, len(others)),
         grid=(pairs, pages),
         in_specs=[
             pl.BlockSpec(memory_space=pltpu.SMEM),
@@ -431,18 +476,19 @@
             part(2),
             wide,
             wide,
-            pl.BlockSpec((1, 1, 8, count), lambda pair, page: (page, pair, 0, 0)),
+            pl.BlockSpec((1, 1, 8, count), lambda pair, page: (page, first + pair, 0, 0)),
             pl.BlockSpec((count, 2 * NB), lambda pair, page: (page, 0)),
             pl.BlockSpec((2 * NB, count), lambda pair, page: (0, page)),
-            pl.BlockSpec((2, 8, 512), lambda pair, page: (pair, 0, 0)),
-        ],
+            pl.BlockSpec((2, 8, 512), lambda pair, page: (first + pair, 0, 0)),
+        ]
+        + held(others),
         out_specs=[
             pl.BlockSpec((3, count, 128), lambda pair, page: (0, page, pair)),
             pl.BlockSpec((2, 8, 512), lambda pair, page: (pair, 0, 0)),
         ],
         out_shape=[
-            jax.ShapeDtypeStruct(projected.shape, BF),
-            jax.ShapeDtypeStruct((H, 8, 512), F32),
+            jax.ShapeDtypeStruct(projected.shape[:2] + (128 * pairs,), BF),
+            jax.ShapeDtypeStruct((2 * pairs, 8, 512), F32),
         ],
         scratch_shapes=[
             pltpu.VMEM((2, 128, count + 384), F32),
@@ -452,8 +498,8 @@
         ],
         compiler_params=params_of(),
         name="attend_back",
-        cost_estimate=cost(41),
-    )(valid, projected, projected, projected, d_mixed, mixed, log_total, both, both_t, base)
+        cost_estimate=cost(7 * pairs),
+    )(valid, projected, projected, projected, d_mixed, mixed, log_total, both, both_t, base, *others)
 
 
 def gelu_parts(before):
@@ -573,15 +619,16 @@
     low_ref[...] = att.astype(BF)
 
 
-def output_call(where, stacks, rows, mixed, keep):
+def output_call(where, stacks, rows, mixed, keep, others):
     tokens, width = mixed.shape
     nz = stacks[0].shape[0]
     chips = len(stacks) * nz
     return pl.pallas_call(
-        functools.partial(output_kernel, len(stacks)),
+        waiting(functools.partial(output_kernel, len(stacks)), 3 + len(stacks), len(others)),
         grid=(1,),
         in_specs=[smem(), whole_spec((tokens, width)), whole_spec((tokens, 1))]
-        + weight_specs(stacks, rows, 8),
+        + weight_specs(stacks, rows, 8)
+        + held(others),
         out_specs=[
             whole_spec((tokens, width)),
             whole_spec((tokens, width)),
@@ -595,7 +642,7 @@
         compiler_params=params_of(),
         name="output",
         cost_estimate=cost(5),
-    )(where, mixed, keep, *stacks)
+    )(where, mixed, keep, *stacks, *others)
 
 
 def feed_kernel(count, where_ref, inputs_ref, own_ref, other_ref, vec_ref, bias_ref, *refs):
@@ -772,9 +819,15 @@
 
     d_active = dot_nt(low_ref[...], second_ref[...])
     d_before = (slope_ref[...].astype(F32) * d_active).astype(BF)
-    dbias_ref[...] = jnp.sum(d_before.astype(F32), axis=0, keepdims=True)
+    dbias_ref[0] = jnp.sum(d_before.astype(F32), axis=0, keepdims=True)
     total_ref[...] += dot_nt(d_before, first_ref[0])
-    store_slots(slots_ref, dfirst_ref, dot(rows_t[...], d_before))
+    total = dot(rows_t[...], d_before)
+    chips, piece = dfirst_ref.shape[0], dfirst_ref.shape[1] // 2
+    half = dfirst_ref.shape[2]
+    for chip in range(chips):
+        part = total[chip * piece : chip * piece + piece].astype(BF)
+        dfirst_ref[slots_ref[chip], :piece] = part[:, :half]
+        dfirst_ref[slots_ref[chip], piece:] = part[:, half:]
 
     @pl.when(step == pl.num_programs(0) - 1)
     def _():
@@ -787,13 +840,13 @@
         add_sums(sums_ref, 1, grad, True)
 
 
-def feed_back_call(slots, rows, low, second, first, slope, dy, hat, scale, vecs, chips):
+def feed_back_call(slots, rows, low, second, first, slope, dy, hat, scale, vecs, chips, others):
     tokens, width = rows.shape
     hidden = second.shape[0]
     piece = width // chips
     whole = whole_spec((tokens, width))
     return pl.pallas_call(
-        feed_back_kernel,
+        waiting(feed_back_kernel, 10, len(others)),
         grid=(hidden // width,),
         in_specs=[
             smem(),
@@ -806,144 +859,207 @@
             whole,
             whole_spec((tokens, 1)),
             whole_spec(vecs.shape),
-        ],
+        ]
+        + held(others),
         out_specs=[
             whole,
             whole,
-            pl.BlockSpec((chips, piece, width), lambda i: (0, 0, i)),
-            pl.BlockSpec((1, width), lambda i: (0, i)),
+            pl.BlockSpec((chips, 2 * piece, width // 2), lambda i: (0, i, 0)),
+            pl.BlockSpec((1, 1, width), lambda i: (i, 0, 0)),
             whole_spec((8, width)),
         ],
         out_shape=[
             jax.ShapeDtypeStruct((tokens, width), F32),
             jax.ShapeDtypeStruct((tokens, width), BF),
-            jax.ShapeDtypeStruct((chips, piece, hidden), BF),
-            jax.ShapeDtypeStruct((1, hidden), F32),
+            jax.ShapeDtypeStruct((chips, 2 * piece * (hidden // width), width // 2), BF),
+            jax.ShapeDtypeStruct((hidden // width, 1, width), F32),
             jax.ShapeDtypeStruct((8, width), F32),
         ],
         scratch_shapes=[pltpu.VMEM((width, tokens), BF), pltpu.VMEM((tokens, width), F32)],
         compiler_params=params_of(),
         name="feed_back",
         cost_estimate=cost(26),
-    )(slots, rows, low, second, first, slope, dy, hat, scale, vecs)
-
-
-def middle_kernel(slots_ref, own_ref, other_ref, keep_ref, mixed_ref, weight_ref, dmixed_ref, dw_ref, low_ref):
+    )(slots, rows, low, second, first, slope, dy, hat, scale, vecs, *others)
+
+
+def middle_kernel(own_ref, other_ref, keep_ref, weight_ref, dmixed_ref, low_ref):
     half = own_ref.shape[0] // 2
     for page in range(2):
         here = pl.ds(half * page, half)
         there = pl.ds(half * (1 - page), half)
         merged = (own_ref[here, :] + other_ref[there, :].astype(F32)) * keep_ref[here, :]
         low_ref[here, :] = merged.astype(BF)
-    low = low_ref[...]
-    dmixed_ref[...] = dot_nt(low, weight_ref[...]).astype(BF)
-    store_slots(slots_ref, dw_ref, dot(mixed_ref[...].T, low))
-
-
-def middle_call(slots, own, other, keep, mixed, weight, chips):
+    dmixed_ref[...] = dot_nt(low_ref[...], weight_ref[...]).astype(BF)
+
+
+def middle_call(own, other, keep, weight):
     tokens, width = own.shape
     whole = whole_spec((tokens, width))
-    piece = (chips, width // chips, width)
     return pl.pallas_call(
         middle_kernel,
         grid=(1,),
-        in_specs=[smem(), whole, whole, whole_spec((tokens, 1)), whole, whole_spec((width, width))],
-        out_specs=[whole, whole_spec(piece)],
-        out_shape=[jax.ShapeDtypeStruct((tokens, width), BF), jax.ShapeDtypeStruct(piece, BF)],
-        scratch_shapes=[pltpu.VMEM((tokens, width), BF)],
+        in_specs=[whole, whole, whole_spec((tokens, 1)), whole_spec((width, width))],
+        out_specs=[whole, whole],
+        out_shape=[jax.ShapeDtypeStruct((tokens, width), BF)] * 2,
         compiler_params=params_of(),
         name="middle",
+        cost_estimate=cost(6),
+    )(own, other, keep, weight)
+
+
+def turn_kernel(joint_ref, plain_ref, mixed_ref, both_ref, lefts_ref, both_t_ref):
+    for index, ref in enumerate((joint_ref, plain_ref, mixed_ref)):
+        lefts_ref[index] = ref[...].T
+    both_t_ref[...] = both_ref[...].T
+
+
+def turn_call(joint, plain, mixed, both):
+    tokens, width = joint.shape
+    whole = whole_spec((tokens, width))
+    return pl.pallas_call(
+        turn_kernel,
+        grid=(1,),
+        in_specs=[whole, whole, whole, whole_spec(both.shape)],
+        out_specs=[whole_spec((3, width, tokens)), whole_spec(both.shape[::-1])],
+        out_shape=[
+            jax.ShapeDtypeStruct((3, width, tokens), BF),
+            jax.ShapeDtypeStruct(both.shape[::-1], BF),
+        ],
+        compiler_params=params_of(),
+        name="turn",
         cost_estimate=cost(8),
-    )(slots, own, other, keep, mixed, weight)
-
-
-def grads_kernel(
-    slots_ref, joint_ref, plain_ref, grad_ref, weight_ref, dpre_ref, normed_ref, both_ref, coef_ref,
-    dw_ref, rows_ref, sums_ref, left_t, total_ref,
+    )(joint, plain, mixed, both)
+
+
+def store_rows(slots_ref, out_ref, start, total):
+    chips = out_ref.shape[0]
+    piece = total.shape[0] // chips
+    for chip in range(chips):
+        low = total[chip * piece : chip * piece + piece].astype(BF)
+        out_ref[slots_ref[chip], start : start + piece] = low
+
+
+def grads_one_kernel(slots_ref, turned_ref, left_ref, grad_ref, datt_ref, dwa_ref, dwb_ref):
+    step = pl.program_id(0)
+    total = dot(left_ref[0], jnp.where(step < 3, grad_ref[0], datt_ref[...]))
+    pl.when(step < 2)(functools.partial(store_rows, turned_ref, dwa_ref, 0, total))
+    pl.when(step >= 2)(functools.partial(store_rows, slots_ref, dwb_ref, 0, total))
+
+
+def grads_one_call(slots, turned, lefts, grad, datt, chips):
+    _, width, tokens = lefts.shape
+    half = width // 2
+    piece = width // chips
+    return pl.pallas_call(
+        grads_one_kernel,
+        grid=(5,),
+        in_specs=[
+            smem(),
+            smem(),
+            pl.BlockSpec((1, width, tokens), lambda i: (jnp.where(i < 2, 0, jnp.minimum(i - 1, 2)), 0, 0)),
+            pl.BlockSpec((1, tokens, half), lambda i: (jnp.minimum(i, 2), 0, 0)),
+            pl.BlockSpec((tokens, half), lambda i: (0, jnp.maximum(i - 3, 0))),
+        ],
+        out_specs=[
+            pl.BlockSpec((chips, None, piece, half), lambda i: (0, jnp.minimum(i, 1), 0, 0)),
+            pl.BlockSpec((chips, None, piece, half), lambda i: (0, jnp.maximum(i - 2, 0), 0, 0)),
+        ],
+        out_shape=[
+            jax.ShapeDtypeStruct((chips, 2, piece, half), BF),
+            jax.ShapeDtypeStruct((chips, 3, piece, half), BF),
+        ],
+        compiler_params=params_of(),
+        name="grads_one",
+        cost_estimate=cost(9),
+    )(slots, turned, lefts, grad, datt)
+
+
+def grads_two_kernel(
+    slots_ref, turned_ref, left_ref, near_ref, grad_ref, weight_ref, dpre_ref, normed_ref, both_t_ref,
+    coef_ref, early_ref, dwa_ref, dwb_ref, rows_ref, total_ref,
 ):
     step = pl.program_id(0)
-    space_size = both_ref.shape[1]
+    chips, half = dwa_ref.shape[0], dwa_ref.shape[2]
+    piece = dwa_ref.shape[1] // 2
+    space_size = both_t_ref.shape[0]
+    near = space_size // (2 * chips)
+    grad = grad_ref[0]
+    total = dot(left_ref[0], grad)
+    part = dot_nt(jnp.concatenate([near_ref[0], grad], axis=1), weight_ref[0])
 
     @pl.when(step == 0)
     def _():
-        left_t[...] = joint_ref[...].T
-
-    @pl.when(step == 2)
-    def _():
-        left_t[...] = plain_ref[...].T
-
-    grad = grad_ref[0]
-    chips = dw_ref.shape[0]
-    piece = left_t.shape[0] // chips
-    near = space_size // (2 * chips)
-
-    total = dot(left_t[...], grad)
-
-    def store(index):
-        for chip in range(chips):
-            low = total[chip * piece : chip * piece + piece].astype(BF)
-            dw_ref[slots_ref[chip], index * piece : index * piece + piece] = low
-
-    for index in range(3):
-        pl.when(step == index)(functools.partial(store, index))
-    part = dot_nt(grad, weight_ref[0])
-
-    @pl.when(step == 0)
-    def _():
+        store_rows(turned_ref, dwa_ref, 0, total)
         total_ref[...] = part
 
     @pl.when(step == 1)
     def _():
+        store_rows(turned_ref, dwa_ref, piece, total)
         joint = total_ref[...] + part
         total_ref[...] = joint + dpre_ref[...]
-        space = dot(both_ref[...].T, joint.astype(BF)).astype(BF)
+        space = dot(both_t_ref[...], joint.astype(BF)).astype(BF)
         for chip in range(chips):
             for k in range(2):
                 begin = k * space_size // 2 + chip * near
-                start = 3 * piece + k * near
-                dw_ref[slots_ref[chip], start : start + near] = space[begin : begin + near]
+                for side in range(2):
+                    start = piece + (2 * side + k) * near
+                    dwb_ref[slots_ref[chip], start : start + near] = space[
+                        begin : begin + near, half * side : half * side + half
+                    ]
 
     @pl.when(step == 2)
     def _():
+        store_rows(slots_ref, dwb_ref, 0, total)
         dx = total_ref[...] + part
         rows_ref[...] = dx * coef_ref[2:3] * coef_ref[1:2]
-        add_sums(sums_ref, 0, dx * normed_ref[...], True)
-        add_sums(sums_ref, 1, dx, True)
-
-
-def grads_call(slots, joint, plain, grad, weight, d_pre, normed, both, coefs, chips):
-    tokens, width = joint.shape
+        gain = jnp.sum(dx * normed_ref[...], axis=0, keepdims=True) * coef_ref[4:5]
+        shift_row = jnp.sum(dx, axis=0, keepdims=True) * coef_ref[4:5]
+        early = early_ref[...]
+        place_row = lax.broadcasted_iota(jnp.int32, early.shape, 0)
+        early = jnp.where(place_row == 0, gain, jnp.where(place_row == 1, shift_row, early)).astype(BF)
+        start = piece + 4 * near
+        count = early.shape[0]
+        for chip in range(chips):
+            for side in range(2):
+                dwb_ref[chip, start + count * side : start + count * side + count] = early[
+                    :, half * side : half * side + half
+                ]
+
+
+def grads_two_call(slots, turned, lefts, near, grad, weight, d_pre, normed, both_t, coefs, early, chips, others):
+    _, width, tokens = lefts.shape
+    half = width // 2
     whole = whole_spec((tokens, width))
-    height = 3 * (width // chips) + both.shape[1] // chips
+    piece = width // chips
+    tall = piece + 2 * (both_t.shape[0] // chips) + 2 * early.shape[0]
     return pl.pallas_call(
-        grads_kernel,
+        waiting(grads_two_kernel, 11, len(others)),
         grid=(3,),
         in_specs=[
             smem(),
-            whole,
-            whole,
-            pl.BlockSpec((1, tokens, width), lambda i: (i, 0, 0)),
+            smem(),
+            pl.BlockSpec((1, width, tokens), lambda i: (i // 2, 0, 0)),
+            pl.BlockSpec((1, tokens, half), lambda i: (i, 0, 0)),
+            pl.BlockSpec((1, tokens, half), lambda i: (i, 0, 0)),
             pl.BlockSpec((1, width, width), lambda i: (i, 0, 0)),
             whole,
             whole,
-            whole_spec(both.shape),
+            whole_spec(both_t.shape),
             whole_spec(coefs.shape),
-        ],
-        out_specs=[
-            whole_spec((chips, height, width)),
-            whole,
-            whole_spec((8, width)),
-        ],
+            whole_spec(early.shape),
+        ]
+        + held(others),
+        out_specs=[whole_spec((chips, 2 * piece, half)), whole_spec((chips, tall, half)), whole],
         out_shape=[
-            jax.ShapeDtypeStruct((chips, height, width), BF),
+            jax.ShapeDtypeStruct((chips, 2 * piece, half), BF),
+            jax.ShapeDtypeStruct((chips, tall, half), BF),
             jax.ShapeDtypeStruct((tokens, width), F32),
-            jax.ShapeDtypeStruct((8, width), F32),
-        ],
-        scratch_shapes=[pltpu.VMEM((width, tokens), BF), pltpu.VMEM((tokens, width), F32)],
+        ],
+        scratch_shapes=[pltpu.VMEM((tokens, width), F32)],
         compiler_params=params_of(),
-        name="grads",
-        cost_estimate=cost(12),
-    )(slots, joint, plain, grad, weight, d_pre, normed, both, coefs)
+        name="grads_two",
+        cost_estimate=cost(10),
+    )(slots, turned, lefts, near, grad, weight, d_pre, normed, both_t, coefs, early, *others)
 
 
 def adam(weight, grad, first, second, rate, decay):
@@ -953,6 +1069,126 @@
         first_new / (1 - BETA_ONE**STEP) / (jnp.sqrt(second_new / (1 - BETA_TWO**STEP)) + ADAM_EPS)
     )
     return (first_new, second_new, weight - rate * (ratio + decay * weight))
+
+
+def late_kernel(chips, piece, near, squares_ref, *refs):
+    out_ref = refs[-1]
+    total = refs[0][0].astype(F32)
+    for ref in refs[1:-1]:
+        total = total + ref[0].astype(F32)
+    count = total.shape[0]
+    out_ref[:count] = total
+    weights = total[: 3 * piece]
+    little = total[3 * piece + 4 * near :]
+    squares = jnp.sum(weights * weights) + jnp.sum(little * little) / chips + squares_ref[0]
+    out_ref[count:] = jnp.full((8, total.shape[1]), squares)
+
+
+def late_call(column, squares, chips, piece, near):
+    nz, count, half = column.shape
+    moved = [shift(column[k : k + 1], "z", k) for k in range(1, nz)]
+    block = whole_spec((1, count, half))
+    return pl.pallas_call(
+        functools.partial(late_kernel, chips, piece, near),
+        grid=(1,),
+        in_specs=[smem()] + [block] * nz,
+        out_specs=whole_spec((count + 8, half)),
+        out_shape=jax.ShapeDtypeStruct((count + 8, half), F32),
+        compiler_params=params_of(),
+        name="late",
+        cost_estimate=cost(2),
+    )(squares.reshape(1), column, *moved)
+
+
+def chip_squares_kernel(begin, end, own_ref, other_ref, out_ref):
+    space = own_ref[begin:end] + other_ref[begin:end]
+    count = own_ref.shape[0] - 8
+    both = own_ref[count:, :128] + other_ref[count:, :128]
+    out_ref[...] = both + jnp.sum(space * space)
+
+
+def chip_squares_call(own, other, begin, end):
+    return pl.pallas_call(
+        functools.partial(chip_squares_kernel, begin, end),
+        grid=(1,),
+        in_specs=[whole_spec(own.shape)] * 2,
+        out_specs=whole_spec((8, 128)),
+        out_shape=jax.ShapeDtypeStruct((8, 128), F32),
+        compiler_params=params_of(),
+        name="chip_squares",
+        cost_estimate=cost(1),
+    )(own, other)
+
+
+def adam_kernel(piece, near, norm_ref, seen_ref, *refs):
+    seen = seen_ref[0] == 1
+    factor = CLIP / jnp.maximum(jnp.sqrt(norm_ref[0:1, 0:1]), CLIP)
+    own_one, other_one, own_late, other_late = refs[:4]
+    attn, feed_in, feed_out = refs[4:7], refs[7:12], refs[12:17]
+    small = (refs[17:21], refs[21:25], refs[25:29])
+    space, outs = refs[29:32], refs[32:]
+    mine = piece // 2
+
+    def pick(first, second):
+        return jnp.where(seen, first, second)
+
+    def step(weight, grad, first, second, rate, decay, targets, at):
+        new = adam(weight[at], grad * factor, first[at], second[at], rate, decay)
+        for target, value in zip(targets, new):
+            target[at] = value
+        if len(targets) == 4:
+            targets[3][at] = new[2].astype(BF)
+
+    def late_rows(ref, index):
+        top = ref[piece * index : piece * index + mine]
+        return pick(top, ref[piece * index + mine : piece * index + piece])
+
+    half = own_one.shape[2]
+    for stream in range(2):
+        first = (lambda a, b: pick(a, b)) if stream == 0 else (lambda a, b: pick(b, a))
+        for matrix in range(4):
+            left = first(own_one[matrix], other_one[matrix])
+            if matrix < 3:
+                right = first(late_rows(own_late, matrix), late_rows(other_late, matrix))
+            else:
+                right = first(own_one[4], other_one[4])
+            for side, grad in enumerate((left, right)):
+                at = (stream, matrix, slice(None), slice(half * side, half * side + half))
+                step(attn[0], grad, attn[1], attn[2], RATE_ATTN, DECAY, outs[:4], at)
+        for group, target in ((feed_in, outs[4:8]), (feed_out, outs[8:12])):
+            grad = first(group[3][...], group[4][...])
+            step(group[0], grad, group[1], group[2], RATE_FEED, DECAY, target, (stream,))
+    for index, group in enumerate(small):
+        targets = outs[12 + 3 * index : 15 + 3 * index]
+        step(group[0], group[3][...], group[1], group[2], RATE_OTHER, 0.0, targets, (slice(None),))
+    for k in range(2):
+        for side in range(2):
+            begin = 3 * piece + (2 * side + k) * near
+            total = own_late[begin : begin + near] + other_late[begin : begin + near]
+            grad = pick(total[: near // 2], total[near // 2 :])
+            at = (k, slice(None), slice(half * side, half * side + half))
+            step(space[0], grad, space[1], space[2], RATE_OTHER, DECAY, outs[21:24], at)
+
+
+def adam_call(norm, seen, piece, near, parts, groups):
+    inputs = list(parts)
+    shapes = []
+    for index, group in enumerate(groups):
+        inputs += group
+        shapes += [jax.ShapeDtypeStruct(group[0].shape, F32)] * 3
+        if index < 3:
+            shapes.append(jax.ShapeDtypeStruct(group[0].shape, BF))
+    return pl.pallas_call(
+        functools.partial(adam_kernel, piece, near),
+        grid=(1,),
+        in_specs=[whole_spec(norm.shape), smem()]
+        + [pl.BlockSpec(memory_space=pltpu.VMEM)] * len(inputs),
+        out_specs=[whole_spec(shape.shape) for shape in shapes],
+        out_shape=shapes,
+        compiler_params=params_of(),
+        name="adam",
+        cost_estimate=cost(9),
+    )(norm, seen, *inputs)
 
 
 def body(
@@ -1068,8 +1304,11 @@
     stream_gain = jnp.where(seen, wide_vec[0], 1.0)
     stream_shift = jnp.where(seen, wide_vec[1], 0.0)
     raw = jnp.concatenate([data_own, data_other], axis=0)
-    coefs = jnp.stack([stream_mean, stream_inverse, stream_gain, stream_shift])
-    coefs = jnp.pad(coefs, ((0, 4), (0, 0)))
+    coefs = jnp.stack(
+        [stream_mean, stream_inverse, stream_gain, stream_shift]
+        + [jnp.full((width,), jnp.where(seen, 1.0, 0.0))]
+    )
+    coefs = jnp.pad(coefs, ((0, 3), (0, 0)))
     position = jnp.arange(count, dtype=jnp.int32)
     lengths_both = jnp.concatenate([lengths, length_other])
     keep_pages = (position[None, :] < lengths_both[:, None]).astype(F32).reshape(tokens, 1)
@@ -1105,7 +1344,10 @@
         sources, wide_one, rows_one, raw, both, wide_spatial, coefs
     )
     mixed, log_total = attend_call(valid, projected, both, base, count)
-    att, att_low, weight_out = output_call(where_rest, wide_rest, rows_rest, mixed, keep_rows)
+    lefts, both_t = turn_call(joint, plain, mixed, both)
+    att, att_low, weight_out = output_call(
+        where_rest, wide_rest, rows_rest, mixed, keep_rows, (lefts,)
+    )
     att_other = swap(att_low)
 
     u, u_low, hat_one, scale_one, active, slope, weight_in = feed_call(
@@ -1119,31 +1361,58 @@
     slots = slot_table()
     d_out = second_call(jnp.arange(chips, dtype=jnp.int32), active, dff, chips)
     d_pre, d_pre_low, d_in, d_bias, pre_sums = feed_back_call(
-        slots, u_low, after(dff, d_out), weight_second.reshape(hidden, width),
+        slots, u_low, dff, weight_second.reshape(hidden, width),
         weight_in.reshape(-1, width, width), slope, dy, hat_one, scale_one, vecs, chips,
+        (d_out,),
     )
     d_pre_other = swap(d_pre_low)
 
-    d_mixed, d_last = middle_call(
-        slots, d_pre, d_pre_other, keep_rows, mixed, weight_out.reshape(width, width), chips
-    )
-    d_projected, table_parts = attend_back_call(
-        valid, projected, d_mixed, mixed, log_total, both, base, count
-    )
-    column_in = scatter_plane(d_in, d_projected)
-    column_last = scatter_plane(d_last, d_projected)
-    d_first, grad_rows, norm_sums = grads_call(
-        slots, joint, plain, after(d_projected, (column_in, column_last)), weight_qkv.reshape(3, width, width), d_pre, normed,
-        both, coefs, chips,
-    )
-
+    d_mixed, d_att = middle_call(d_pre, d_pre_other, keep_rows, weight_out.reshape(width, width))
+    weight_qkv = weight_qkv.reshape(3, width, width)
+    back = functools.partial(attend_back_call, valid)
+    shared = (both, both_t, base, count)
+    half_one, tables_one = back(projected, d_mixed, mixed, log_total, *shared, 0, H // 4)
+    turned = slot_table(True)
+    one_a, one_b = grads_one_call(slots, turned, lefts, half_one, d_att, chips)
+    one_a, one_b = one_a.reshape(chips, -1, width // 2), one_b.reshape(chips, -1, width // 2)
+    half_two, tables_two = back(
+        projected, d_mixed, mixed, log_total, *shared, H // 4, H // 4, (one_b,)
+    )
+    column_in = scatter_plane(d_in, (half_two,))
+    near_a = scatter_step(one_a, "x", (half_two,))
+    near_b = scatter_step(one_b, "y", (half_two,))
+    early = jnp.concatenate(
+        [
+            jnp.zeros((2, width), F32), pre_sums[:2], close_sums[:3], jnp.zeros((1, width), F32),
+            d_bias.reshape(-1, width),
+            table_sums(jnp.concatenate([tables_one, tables_two], axis=0)).reshape(-1, width),
+        ],
+        axis=0,
+    )
+    little_rows = early.shape[0]
+    early = jnp.pad(early, ((0, -little_rows % 8), (0, 0)))
+    d_two, d_three, grad_rows = grads_two_call(
+        slots, turned, lefts, half_one, half_two, weight_qkv, d_pre, normed,
+        both_t, coefs, early, chips, (column_in, near_a, near_b),
+    )
+
+    piece = 2 * rows_a
+    half = width // 2
     sum_out = lax.psum_scatter(d_out, CHIP).astype(F32)
-    sum_in = scatter_line(column_in)
-    sum_last = scatter_line(column_last)
-    sum_first = scatter_line(scatter_plane(d_first))
-    sum_attn = jnp.concatenate(
-        [sum_first[: 6 * rows_a].reshape(3, 2 * rows_a, width), sum_last[None]], axis=0
-    )
+    sum_in = scatter_line(column_in, (d_two,))
+    column_one = jnp.concatenate([scatter_step(near_a, "y", (d_two,)), scatter_step(near_b, "x", (d_two,))], axis=1)
+    near_two = scatter_step(d_two, "x", (sum_in, column_one))
+    near_three = scatter_step(d_three, "y", (sum_in, column_one))
+    sum_in = sum_in.reshape(-1, piece, half).transpose(1, 0, 2).reshape(piece, hidden)
+    sum_one = scatter_line(column_one)
+    column_late = jnp.concatenate(
+        [scatter_step(near_two, "y", (sum_one,)), scatter_step(near_three, "x", (sum_one,))], axis=1
+    )
+    sum_one = sum_one.reshape(5, piece, half)
+    near = both.shape[1] // chips
+    squares = jnp.sum(sum_out * sum_out) + jnp.sum(sum_in * sum_in) + jnp.sum(sum_one * sum_one)
+    own_late = late_call(column_late, squares, chips, piece, near // 2)
+    other_late = swap(own_late)
 
     def own_rows(value, axis):
         first, second = jnp.split(value, 2, axis=axis)
@@ -1152,20 +1421,11 @@
     def by_stream(own, other):
         return jnp.where(seen, jnp.stack([own, other]), jnp.stack([other, own]))
 
-    own_space, other_space = own_rows(sum_first[6 * rows_a :].reshape(2, 2, -1, width), 1)
-    grad_spatial = (own_space + other_space).reshape(spatial.shape)
-    is_norm = jnp.where(seen, 1.0, 0.0)
-    little = jnp.concatenate(
-        [
-            norm_sums[:2] * is_norm, pre_sums[:2], close_sums[:3], jnp.zeros((1, width), F32),
-            d_bias.reshape(-1, width), table_sums(table_parts).reshape(-1, width),
-        ],
-        axis=0,
-    ).astype(BF)
-    little = jnp.pad(little, ((0, -little.shape[0] % 8), (0, 0)))
-    little = functools.reduce(jnp.add, [part.astype(F32) for part in around(little)]).astype(BF)
-    little = functools.reduce(jnp.add, [part.astype(F32) for part in line_of(little)])
-    little = by_stream(little, swap(little))
+    def little_of(late):
+        rows = late[3 * piece + 2 * near : late.shape[0] - 8].reshape(2, -1, half)
+        return jnp.concatenate([rows[0], rows[1]], axis=-1)
+
+    little = by_stream(little_of(own_late), little_of(other_late))
     member = 2 * chip_of(0, 0, 0) + core
     vec_sum = lax.dynamic_slice_in_dim(little[:, :7], member * vectors.shape[1], vectors.shape[1], 2)
     grad_vec = jnp.stack(
@@ -1176,22 +1436,13 @@
     bias_lines = hidden // width
     bias_sum = little[:, 8 : 8 + bias_lines].reshape(2, hidden)
     grad_bias = lax.dynamic_slice_in_dim(bias_sum, member * bias_in.shape[1], bias_in.shape[1], 1)
-    pos_sum = little[:, 8 + bias_lines : 8 + bias_lines + 3 * H * NR // width].reshape(2, 3, H, NR)
+    pos_sum = little[:, 8 + bias_lines : little_rows].reshape(2, H, 3, NR).transpose(0, 2, 1, 3)
     grad_pos = lax.dynamic_slice_in_dim(pos_sum, member * pos_tables.shape[3], pos_tables.shape[3], 3)
 
-    squares = jnp.sum(sum_out * sum_out) + jnp.sum(sum_in * sum_in) + jnp.sum(sum_attn * sum_attn)
-    for grad in (grad_spatial, grad_pos, grad_vec, grad_bias):
-        squares = squares + jnp.sum(grad * grad)
-    tile = jnp.full((8, 128), squares, F32)
-    tile = tile + swap(tile)
+    tile = chip_squares_call(own_late, other_late, 3 * piece, 3 * piece + 2 * near)
     tile = functools.reduce(jnp.add, around(tile))
     norm = functools.reduce(jnp.add, line_of(tile))
     grad_norm = jnp.sqrt(norm[0, 0])
-    factor = CLIP / jnp.maximum(grad_norm, CLIP)
-
-    grad_attn = by_stream(*own_rows(sum_attn, 1))
-    grad_in = by_stream(*own_rows(sum_in, 0))
-    grad_out = by_stream(*own_rows(sum_out, 0))
 
     out_own, out_other = out[:count], swap(out[count:])
     grad_own, grad_other = grad_rows[:count], swap(grad_rows[count:])
@@ -1200,22 +1451,25 @@
     grad_visual = mine_of(grad_own, grad_other)[None]
     grad_text = mine_of(grad_other, grad_own)[None]
 
-    params = (attn_w, ffn_in, ffn_out, bias_in, vectors, pos_tables, spatial)
-    grads = (grad_attn, grad_in, grad_out, grad_bias, grad_vec, grad_pos, grad_spatial)
-    states = (
-        (attn_mom, attn_sec), (in_mom, in_sec), (out_mom, out_sec), (bias_mom, bias_sec),
-        (vec_mom, vec_sec), (pos_mom, pos_sec), (spatial_mom, spatial_sec),
-    )
-    rates = (RATE_ATTN, RATE_FEED, RATE_FEED, RATE_OTHER, RATE_OTHER, RATE_OTHER, RATE_OTHER)
-    decays = (DECAY, DECAY, DECAY, 0.0, 0.0, 0.0, DECAY)
-    results = [out_visual, out_text, grad_visual, grad_text, grad_norm]
-    for index, (weight, grad, state, rate, decay) in enumerate(
-        zip(params, grads, states, rates, decays)
-    ):
-        new = adam(weight, grad * factor, state[0], state[1], rate, decay)
-        results.extend(new)
-        if index < 3:
-            results.append(new[2].astype(BF))
+    def turned_pos(value):
+        return jnp.swapaxes(value, 2, 3)
+
+    groups = (
+        (attn_w, attn_mom, attn_sec),
+        (ffn_in, in_mom, in_sec) + tuple(own_rows(sum_in, 0)),
+        (ffn_out, out_mom, out_sec) + tuple(own_rows(sum_out, 0)),
+        (bias_in, bias_mom, bias_sec, grad_bias),
+        (vectors, vec_mom, vec_sec, grad_vec),
+        tuple(turned_pos(part) for part in (pos_tables, pos_mom, pos_sec, grad_pos)),
+        (spatial, spatial_mom, spatial_sec),
+    )
+    new = adam_call(
+        norm, seen.astype(jnp.int32).reshape(1), piece, near // 2,
+        (*own_rows(sum_one, 1), own_late, other_late), groups,
+    )
+    results = [out_visual, out_text, grad_visual, grad_text, grad_norm] + list(new)
+    for index in range(5 + 18, 5 + 21):
+        results[index] = turned_pos(results[index])
     return tuple(results)
 
 

time: 530 us -> 518 us (0.977)
  Pallas kernels: 191 us -> 234 us
  other arithmetic: 54.3 us -> 30 us
  waiting for transfers between devices: 145 us -> 129 us
  local copies, waits for them, and re-layouts: 52.6 us -> 45.5 us
    pallas_call x5 -> x21, Pallas kernels: 103 us -> 147 us  [the longest x2 44 us: attend_back_call(): pl.pallas_call(waiting(attend_back_kernel, 10, len(others)), grid=(pairs,...]
    ppermute x15 -> x6, waiting for transfers between devices: 26.9 us -> 3.46 us  [diagonal(): return lax.ppermute(value, ('y', 'x'), pairs)]
    convert_element_type x7 -> x0, other arithmetic: 13.6 us -> none  [the longest x3 7.31 us: body(): results.append(new[2].astype(BF))]
    ppermute x22 -> x27, waiting for transfers between devices: 88.3 us -> 102 us  [shift(): lax.ppermute(value, axis, [(i, (i + step) % size) for i in range(size)])]
    ppermute x15 -> x6, starting transfers between devices: 17.7 us -> 6.98 us  [diagonal(): return lax.ppermute(value, ('y', 'x'), pairs)]
    ppermute x22 -> x27, starting transfers between devices: 33.7 us -> 42 us  [shift(): lax.ppermute(value, axis, [(i, (i + step) % size) for i in range(size)])]
    concatenate x3 -> x5, other arithmetic: 0.17 us -> 5.97 us  [the longest x2 2.98 us: body(): jnp.concatenate([scatter_step(near_two, 'y', (sum_one,)), scatter_step(ne...]
    unnamed x134 -> x110, local copies, waits for them, and re-layouts: 8.49 us -> 11.6 us
  transfers between devices with their start and end apart: 59 -> 53, of which waited for: 22 -> 19; matrix products, arithmetic and copies ran while one was open for 18% -> 13% of each run, Pallas kernels for 21% -> 28%
where the time goes in v3:
time: 518 us; the launch traced here: 514 us
  Pallas kernels  234 us (45%)
  waiting for transfers between devices  129 us (25%)
  starting transfers between devices  53.4 us (10%)
  local copies, waits for them, and re-layouts  45.5 us (9%)
  other arithmetic  30 us (6%)
  between operations  20.2 us (4%)
    ppermute x27, waiting for transfers between devices, shift(): lax.ppermute(value, axis, [(i, (i + step) % size) for i in range(size)])  102 us
    pallas_call x2, Pallas kernels, attend_back_call(): pl.pallas_call(waiting(attend_back_kernel, 10, len(others)), grid=(pairs,...  44 us
    ppermute x27, starting transfers between devices, shift(): lax.ppermute(value, axis, [(i, (i + step) % size) for i in range(size)])  42 us
    pallas_call x1, Pallas kernels, attend_call(): pl.pallas_call(attend_kernel, grid=(pairs, pages), in_specs=[pl.BlockSpec...  28.1 us
    pallas_call x1, Pallas kernels, feed_back_call(): pl.pallas_call(waiting(feed_back_kernel, 10, len(others)), grid=(hidden /...  26.2 us
    pallas_call x1, Pallas kernels, feed_call(): pl.pallas_call(functools.partial(feed_kernel, len(stacks)), grid=(hidden...  25.3 us
    pallas_call x10, Pallas kernels, sum_call(): pl.pallas_call(functools.partial(sum_kernel, 1 + len(moved)), grid=(steps...  22.4 us
    all_gather x1, waiting for transfers between devices, body(): wide_rest = lax.all_gather(rest, CHIP)  20 us
  transfers between devices with their start and end apart: 53, of which 19 were waited for; matrix products, arithmetic and copies ran while one was open for 13% of the time, Pallas kernels for 28%

profile of v3, /device:TPU:0, one launch (start us, length us, event | category | flops | bytes accessed | tf_op | source)
XLA Modules:
  0.0 513.7 jit_solution(5208676987311295061)
XLA Ops:
  17.9 2.9 collective-permute-start.6
  20.9 2.6 collective-permute-start.7
  28.3 3.8 collective-permute-done.6
  32.0 21.1 %collective-permute-done.7 = bf16[176,768]{1,0:T(8,128)(2,1)S(1)} collective-permute-done((bf16[176,768]{1,0:T(8,128)(2,1)S(1)}, bf16[176,768]{1,0:T(8,128)(2,1)S(1)}, u32[]{:S(2)}, u32[]{:S(2)}) %collective-permute-start.7) | collective-permute-done | bytes 270368 | tf_op jit(solution)/shard_map/ppermute | solution.py:74
  57.6 11.2 %collective-permute-done.11 = bf16[4,176,384]{2,1,0:T(8,128)(2,1)S(1)} collective-permute-done((bf16[4,176,384]{2,1,0:T(8,128)(2,1)S(1)}, bf16[4,176,384]{2,1,0:T(8,128)(2,1)S(1)}, u32[]{:S(2)}, u32[]{:S(2)}) %collective-permute-start.11) | collective-permute-done | bytes 540704 | tf_op jit(solution)/shard_map/ppermute | solution.py:74
  70.2 5.0 collective-permute-done.9
  79.0 33.0 %collective-permute-done.12.refs_3_ = bf16[8,176,384]{2,1,0:T(8,128)(2,1)S(1)} collective-permute-done((bf16[8,176,384]{2,1,0:T(8,128)(2,1)S(1)}, bf16[8,176,384]{2,1,0:T(8,128)(2,1)S(1)}, u32[]{:S(2)}, u32[]{:S(2)}) %collective-permute-start.12) | collective-permute-done | bytes 1081376 | tf_op jit(solution)/shard_map/ppermute | solution.py:74
  120.7 10.9 %project.1 = (bf16[3,1024,768]{2,1,0:T(8,128)(2,1)}, bf16[3,16,48,768]{3,2,1,0:T(8,128)(2,1)}, f32[1024,768]{1,0:T(8,128)}, f32[1024,768]{1,0:T(8,128)}, bf16[10...) custom-call(s32[16]{0:T(128)} %stack.242.one_ref, s32[16]{0:T(128)} %stack.243.two_ref, ...), custom_call_target="tpu_custom_call" | custom-call | flops 13200000000 | bytes 42000000 | tf_op jit(solution)/shard_map/project/pallas_call | solution.py:585
  131.6 28.1 %attend.1 = (bf16[1024,768]{1,0:T(8,128)(2,1)}, f32[2,6,8,512]{3,2,1,0:T(8,128)}) custom-call(s32[2]{0:T(128)} %get-tuple-element.166.valid_ref.refs_0_, bf16[3,1024,768]{2,1,0:T(8,128)(2,1)} %get-tuple-element.96.q_ref.k_ref.v_ref.refs_1_.refs_2_.refs_3_, bf16[3,1024,768]{2,1,0:T(8,128)(2,1)} %get-tuple-element.96.q_ref.k_ref.v_ref.refs_1_.refs_2_.refs_3_, ...), custom_call_target="tpu_custom_call" | custom-call | flops 30799998976 | bytes 98000000 | tf_op jit(solution)/shard_map/attend/pallas_call | solution.py:354
  159.7 6.2 %turn.1 = (bf16[3,768,1024]{2,1,0:T(8,128)(2,1)}, bf16[256,1024]{1,0:T(8,128)(2,1)}) custom-call(bf16[1024,768]{1,0:T(8,128)(2,1)} %get-tuple-element.98.joint_ref, bf16[1024,768]{1,0:T(8,128)(2,1)} %get-tuple-element.99.plain_ref, bf16[1024,768]{1,0:T(8,128)(2,1)} %get-tuple-element.97.mixed_ref.refs_1_.refs_5_, ...), custom_call_target="tpu_custom_call" | custom-call | flops 8800000000 | bytes 28000000 | tf_op jit(solution)/shard_map/turn/pallas_call | solution.py:919
  165.9 20.0 %all-gather.2.cloned.1.call-done.refs_3_.refs_0_ = bf16[16,432,768]{2,1,0:T(8,128)(2,1)} async-done(((bf16[1,432,768]{2,1,0:T(8,128)(2,1)}), bf16[16,432,768]{2,1,0:T(8,128)(2,1)}) %all-gather.2.cloned.1.call-update) | async-done | bytes 10616848 | tf_op jit(solution)/shard_map/all_gather | solution.py:1270
  186.5 6.1 %output.1 = (f32[1024,768]{1,0:T(8,128)}, bf16[1024,768]{1,0:T(8,128)(2,1)}, bf16[16,48,768]{2,1,0:T(8,128)(2,1)}) custom-call(s32[16]{0:T(128)} %iota.47.refs_0_, bf16[1024,768]{1,0:T(8,128)(2,1)} %get-tuple-element.97.mixed_ref.refs_1_.refs_5_, f32[1024,1]{1,0:T(8,128)} %bitcast.217, bf16[16,432,768]{2,1,0:T(8,128)(2,1)} %all-gather.2.cloned.1.call-done.refs_3_.refs_0_, ...), custom_call_target="tpu_custom_call" | custom-call | flops 5500000256 | bytes 17500000 | tf_op jit(solution)/shard_map/output/pallas_call | solution.py:626
  193.8 3.3 collective-permute-done.17
  201.0 25.3 %feed.1 = (f32[1024,768]{1,0:T(8,128)}, bf16[1024,768]{1,0:T(8,128)(2,1)}, f32[1024,768]{1,0:T(8,128)}, f32[1024,1]{1,0:T(8,128)}, bf16[1024,3072]{1,0:T(8,128)(...) custom-call(s32[16]{0:T(128)} %iota.42.where_ref, f32[1024,768]{1,0:T(8,128)} %get-tuple-element.95.inputs_ref, ...), custom_call_target="tpu_custom_call" | custom-call | flops 26400000000 | bytes 84000000 | tf_op jit(solution)/shard_map/feed/pallas_call | solution.py:682
  226.8 12.8 %close.1 = (bf16[1024,768]{1,0:T(8,128)(2,1)}, f32[1024,768]{1,0:T(8,128)}, bf16[1024,768]{1,0:T(8,128)(2,1)}, f32[8,768]{1,0:T(8,128)}, bf16[16,192,768]{2,1,0:T(8,128)(2,1)}) custom-call(s32[16]{0:T(128)} %iota.41.where_ref, bf16[1024,3072]{1,0:T(8,128)(2,1)} %get-tuple-element.103.active_ref, f32[1024,768]{1,0:T(8,128)} %get-tuple-element.104.u_ref, ...), custom_call_target="tpu_custom_call" | custom-call | flops 14300000256 | bytes 45500000 | tf_op jit(solution)/shard_map/close/pallas_call | solution.py:745
  240.2 10.0 %second.1.refs_10_ = bf16[16,192,768]{2,1,0:T(8,128)(2,1)} custom-call(s32[16]{0:T(128)} %iota.50.slots_ref, bf16[1024,3072]{1,0:T(8,128)(2,1)} %get-tuple-element.103.active_ref, bf16[1024,768]{1,0:T(8,128)(2,1)} %get-tuple-element.107.low_ref.refs_2_), custom_call_target="tpu_custom_call" | custom-call | flops 11000000512 | bytes 35000000 | tf_op jit(solution)/shard_map/second/pallas_call | solution.py:793
  250.1 26.2 %feed_back.1 = (f32[1024,768]{1,0:T(8,128)}, bf16[1024,768]{1,0:T(8,128)(2,1)}, bf16[16,384,384]{2,1,0:T(8,128)(2,1)}, f32[4,1,768]{2,1,0:T(1,128)}, f32[8,768]{1,0:T(8,128)}) custom-call(s32[16]{0:T(128)} %multiply_add_fusion.1.refs_0_.slots_ref, bf16[1024,768]{1,0:T(8,128)(2,1)} %get-tuple-element.106.refs_1_, ...), custom_call_target="tpu_custom_call" | custom-call | flops 28600000512 | bytes 91000000 | tf_op jit(solution)/shard_map/feed_back/pallas_call | solution.py:848
  277.6 3.9 fusion.61
  286.9 2.4 select_bitcast_fusion.2
  289.3 5.6 %middle.1 = (bf16[1024,768]{1,0:T(8,128)(2,1)}, bf16[1024,768]{1,0:T(8,128)(2,1)}) custom-call(f32[1024,768]{1,0:T(8,128)} %get-tuple-element.114.own_ref.refs_6_, bf16[1024,768]{1,0:T(8,128)(2,1)} %collective-permute-done.19.other_ref, f32[1024,1]{1,0:T(8,128)} %bitcast.219, bf16[768,768]{1,0:T(8,128)(2,1)} %bitcast.253), custom_call_target="tpu_custom_call" | custom-call | flops 6600000000 | bytes 21000000 | tf_op jit(solution)/shard_map/middle/pallas_call | solution.py:898
  294.9 21.8 %attend_back.2 = (bf16[3,1024,384]{2,1,0:T(8,128)(2,1)}, f32[6,8,512]{2,1,0:T(8,128)}) custom-call(s32[2]{0:T(128)} %get-tuple-element.166.valid_ref.refs_0_, bf16[3,1024,768]{2,1,0:T(8,128)(2,1)} %get-tuple-element.96.q_ref.k_ref.v_ref.refs_1_.refs_2_.refs_3_, bf16[3,1024,768]{2,1,0:T(8,128)(2,1)} %get-tuple-element.96.q_ref.k_ref.v_ref.refs_1_.refs_2_.refs_3_, ...), custom_call_target="tpu_custom_call" | custom-call | flops 23100000256 | bytes 73500000 | tf_op jit(solution)/shard_map/attend_back/pallas_call | solution.py:469
  316.7 9.5 %grads_one.1 = (bf16[16,2,48,384]{3,2,1,0:T(8,128)(2,1)}, bf16[16,3,48,384]{3,2,1,0:T(8,128)(2,1)}) custom-call(s32[16]{0:T(128)} %multiply_add_fusion.1.refs_0_.slots_ref, s32[16]{0:T(128)} %multiply_add_fusion.turned_ref.refs_1_, bf16[3,768,1024]{2,1,0:T(8,128)(2,1)} %get-tuple-element.100.refs_4_.left_ref.refs_2_, ...), custom_call_target="tpu_custom_call" | custom-call | flops 9900000256 | bytes 31500000 | tf_op jit(solution)/shard_map/grads_one/pallas_call | solution.py:953
  326.2 22.2 %attend_back.3 = (bf16[3,1024,384]{2,1,0:T(8,128)(2,1)}, f32[6,8,512]{2,1,0:T(8,128)}) custom-call(s32[2]{0:T(128)} %get-tuple-element.166.valid_ref.refs_0_, bf16[3,1024,768]{2,1,0:T(8,128)(2,1)} %get-tuple-element.96.q_ref.k_ref.v_ref.refs_1_.refs_2_.refs_3_, bf16[3,1024,768]{2,1,0:T(8,128)(2,1)} %get-tuple-element.96.q_ref.k_ref.v_ref.refs_1_.refs_2_.refs_3_, ...), custom_call_target="tpu_custom_call" | custom-call | flops 23100000256 | bytes 73500000 | tf_op jit(solution)/shard_map/attend_back/pallas_call | solution.py:469
  354.0 3.5 sum.10.refs_11_.refs_0_
  360.7 2.4 collective-permute-start.28
  363.1 5.0 collective-permute-done.23.refs_1_
  369.0 2.0 sum.11.refs_12_.refs_0_
  373.8 2.3 sum.12.refs_13_.refs_0_
  377.2 3.5 collective-permute-start.30
  380.7 15.6 %grads_two.1 = (bf16[16,96,384]{2,1,0:T(8,128)(2,1)}, bf16[16,128,384]{2,1,0:T(8,128)(2,1)}, f32[1024,768]{1,0:T(8,128)}) custom-call(s32[16]{0:T(128)} %multiply_add_fusion.1.refs_0_.slots_ref, s32[16]{0:T(128)} %multiply_add_fusion.turned_ref.refs_1_, bf16[3,768,1024]{2,1,0:T(8,128)(2,1)} %get-tuple-element.100.refs_4_.left_ref.refs_2_, ...), custom_call_target="tpu_custom_call" | custom-call | flops 11000000512 | bytes 35000000 | tf_op jit(solution)/shard_map/grads_two/pallas_call | solution.py:1035
  401.1 2.2 sum.13
  409.2 2.0 sum.15
  411.3 2.0 pad_maximum_fusion.2.refs_3_
  416.0 2.2 collective-permute-start.33
  418.2 2.3 sum.16.refs_0_
  422.2 4.5 collective-permute-done.31
  426.7 8.3 %collective-permute-done.32 = bf16[240,384]{1,0:T(8,128)(2,1)S(1)} collective-permute-done((bf16[240,384]{1,0:T(8,128)(2,1)}, bf16[240,384]{1,0:T(8,128)(2,1)S(1)}, u32[]{:S(2)}, u32[]{:S(2)}) %collective-permute-start.32) | collective-permute-done | bytes 184352 | tf_op jit(solution)/shard_map/ppermute | solution.py:74
  438.1 2.3 sum.18.refs_0_
  445.6 6.2 %collective-permute-done.37.refs_1_ = bf16[4,128,384]{2,1,0:T(8,128)(2,1)S(1)} collective-permute-done((bf16[4,128,384]{2,1,0:T(8,128)(2,1)S(1)}, bf16[4,128,384]{2,1,0:T(8,128)(2,1)S(1)}, u32[]{:S(2)}, u32[]{:S(2)}) %collective-permute-start.37) | collective-permute-done | bytes 393248 | tf_op jit(solution)/shard_map/ppermute | solution.py:74
  452.6 1.9 sum.19
  455.6 3.7 collective-permute-start.38
  459.3 2.2 collective-permute-start.39
  461.7 1.9 pad_maximum_fusion.6.refs_0_
  469.2 2.2 collective-permute-done.39.refs_2_
  472.2 2.2 late.1.own_ref.refs_2_
  484.1 2.2 collective-permute-done.44
  486.9 4.1 collective-permute-start.45
  498.2 7.3 %adam.1 = (f32[2,4,24,768]{3,2,1,0:T(8,128)}, f32[2,4,24,768]{3,2,1,0:T(8,128)}, f32[2,4,24,768]{3,2,1,0:T(8,128)}, bf16[2,4,24,768]{3,2,1,0:T(8,128)(2,1)}, f32...) custom-call(f32[8,128]{1,0:T(8,128)} %copy-done.33, ...), custom_call_target="tpu_custom_call" | custom-call | flops 9900000256 | bytes 31500000 | tf_op jit(solution)/shard_map/adam/pallas_call | solution.py:1181
  (390 shorter events, 105.4 us)
Async XLA Ops:
  7.2 178.7 %all-gather.2.cloned.1.call-start = ((), (), s32[]{:S(2)}) async-start(), calls=%async_computation.1 | async-start | bytes 11280384 | tf_op jit(solution)/shard_map/all_gather | solution.py:1270
  12.0 453.5 %reduce-scatter.2.cloned.1.call-start = ((), (), s32[]{:S(2)}) async-start(), calls=%async_computation.2 | async-start | bytes 5013504 | tf_op jit(solution)/shard_map/reduce_scatter | solution.py:1401
  13.2 4.5 collective-permute-start.4
  13.5 4.3 collective-permute-start.3
  14.1 3.6 collective-permute-start.5
  14.4 43.2 %collective-permute-start.1 = (s32[1,2,512]{2,1,0:T(2,128)S(1)}, s32[1,2,512]{2,1,0:T(2,128)S(1)}, u32[]{:S(2)}, u32[]{:S(2)}) collective-permute-start(s32[1,2,512]{2,1,0:T(2,128)S(1)} %copy-done.34), channel_id=1, source_target_pairs={{0,1},{1,0},{2,3},{3,2},{4,5},{5,4},{6,7},{7,6},{8,9},{9,8},{10,11... | collective-permute-start | bytes 12296 | tf_op jit(solution)/shard_map/ppermute | solution.py:69
  14.7 12.3 %collective-permute-start.13 = (s32[1]{0:T(128)}, s32[1]{0:T(128)}, u32[]{:S(2)}, u32[]{:S(2)}) collective-permute-start(s32[1]{0:T(128)} %param.32), channel_id=1, source_target_pairs={{0,1},{1,0},{2,3},{3,2},{4,5},{5,4},{6,7},{7,6},{8,9},{9,8},{10,11... | collective-permute-start | bytes 20 | tf_op jit(solution)/shard_map/ppermute | solution.py:69
  17.9 14.1 %collective-permute-start.6 = (bf16[176,768]{1,0:T(8,128)(2,1)S(1)}, bf16[176,768]{1,0:T(8,128)(2,1)S(1)}, u32[]{:S(2)}, u32[]{:S(2)}) collective-permute-start(bf16[176,768]{1,0:T(8,128)(2,1)S(1)} %get-tuple-element.207), channel_id=1, source_target_pairs={{0,8},{8,16},{16,24},{24,0},{1,9},{9,17},{17,25},{25,1},{2,10},{10... | collective-permute-start | bytes 811016 | tf_op jit(solution)/shard_map/ppermute | solution.py:74
  20.9 32.3 %collective-permute-start.7 = (bf16[176,768]{1,0:T(8,128)(2,1)S(1)}, bf16[176,768]{1,0:T(8,128)(2,1)S(1)}, u32[]{:S(2)}, u32[]{:S(2)}) collective-permute-start(bf16[176,768]{1,0:T(8,128)(2,1)S(1)} %get-tuple-element.207), channel_id=1, source_target_pairs={{0,16},{8,24},{16,0},{24,8},{1,17},{9,25},{17,1},{25,9},{2,18},{10... | collective-permute-start | bytes 811016 | tf_op jit(solution)/shard_map/ppermute | solution.py:74
  23.4 29.7 %collective-permute-start.8 = (bf16[176,768]{1,0:T(8,128)(2,1)S(1)}, bf16[176,768]{1,0:T(8,128)(2,1)S(1)}, u32[]{:S(2)}, u32[]{:S(2)}) collective-permute-start(bf16[176,768]{1,0:T(8,128)(2,1)S(1)} %get-tuple-element.207), channel_id=1, source_target_pairs={{0,24},{8,0},{16,8},{24,16},{1,25},{9,1},{17,9},{25,17},{2,26},{10... | collective-permute-start | bytes 811016 | tf_op jit(solution)/shard_map/ppermute | solution.py:74
  27.0 50.7 %collective-permute-start = (bf16[512,768]{1,0:T(8,128)(2,1)}, bf16[512,768]{1,0:T(8,128)(2,1)S(1)}, u32[]{:S(2)}, u32[]{:S(2)}) collective-permute-start(bf16[512,768]{1,0:T(8,128)(2,1)} %get-tuple-element.178), channel_id=1, source_target_pairs={{0,1},{1,0},{2,3},{3,2},{4,5},{5,4},{6,7},{7,6},{8,9},{9,8},{10,11... | collective-permute-start | bytes 2359304 | tf_op jit(solution)/shard_map/ppermute | solution.py:69
  53.4 15.4 %collective-permute-start.11 = (bf16[4,176,384]{2,1,0:T(8,128)(2,1)S(1)}, bf16[4,176,384]{2,1,0:T(8,128)(2,1)S(1)}, u32[]{:S(2)}, u32[]{:S(2)}) collective-permute-start(bf16[4,176,384]{2,1,0:T(8,128)(2,1)S(1)} %get-tuple-element.182), channel_id=1, source_target_pairs={{0,4},{4,0},{1,5},{5,1},{2,6},{6,2},{3,7},{7,3},{8,12},{12,8},{9,1... | collective-permute-start | bytes 1622024 | tf_op jit(solution)/shard_map/ppermute | solution.py:74
  56.1 19.1 %collective-permute-start.9 = (bf16[4,176,384]{2,1,0:T(8,128)(2,1)S(1)}, bf16[4,176,384]{2,1,0:T(8,128)(2,1)S(1)}, u32[]{:S(2)}, u32[]{:S(2)}) collective-permute-start(bf16[4,176,384]{2,1,0:T(8,128)(2,1)S(1)} %get-tuple-element.183), channel_id=1, source_target_pairs={{0,2},{2,0},{1,3},{3,1},{4,6},{6,4},{5,7},{7,5},{8,10},{10,8},{9,1... | collective-permute-start | bytes 1622024 | tf_op jit(solution)/shard_map/ppermute | solution.py:74
  68.9 43.0 %collective-permute-start.12 = (bf16[8,176,384]{2,1,0:T(8,128)(2,1)S(1)}, bf16[8,176,384]{2,1,0:T(8,128)(2,1)S(1)}, u32[]{:S(2)}, u32[]{:S(2)}) collective-permute-start(bf16[8,176,384]{2,1,0:T(8,128)(2,1)S(1)} %pad_maximum_fusion.4.refs_2_), channel_id=1, source_target_pairs={{0,2},{2,0},{1,3},{3,1},{4,6},{6,4},{5,7},{7,5},{8,10},{10,8},{9,1... | collective-permute-start | bytes 3244040 | tf_op jit(solution)/shard_map/ppermute | solution.py:74
  76.3 37.3 %collective-permute-start.10 = (bf16[8,176,384]{2,1,0:T(8,128)(2,1)}, bf16[8,176,384]{2,1,0:T(8,128)(2,1)}, u32[]{:S(2)}, u32[]{:S(2)}) collective-permute-start(bf16[8,176,384]{2,1,0:T(8,128)(2,1)} %pad_maximum_fusion.3.refs_0_), channel_id=1, source_target_pairs={{0,4},{4,0},{1,5},{5,1},{2,6},{6,2},{3,7},{7,3},{8,12},{12,8},{9,1... | collective-permute-start | bytes 3244040 | tf_op jit(solution)/shard_map/ppermute | solution.py:74
  192.6 7.3 %collective-permute-start.16 = (bf16[1024,768]{1,0:T(8,128)(2,1)}, bf16[1024,768]{1,0:T(8,128)(2,1)S(1)}, u32[]{:S(2)}, u32[]{:S(2)}) collective-permute-start(bf16[1024,768]{1,0:T(8,128)(2,1)} %get-tuple-element.102), channel_id=1, source_target_pairs={{0,1},{1,0},{2,3},{3,2},{4,5},{5,4},{6,7},{7,6},{8,9},{9,8},{10,11... | collective-permute-start | bytes 4718600 | tf_op jit(solution)/shard_map/ppermute | solution.py:69
  192.7 4.4 collective-permute-start.17
  276.3 13.0 %collective-permute-start.19 = (bf16[1024,768]{1,0:T(8,128)(2,1)}, bf16[1024,768]{1,0:T(8,128)(2,1)}, u32[]{:S(2)}, u32[]{:S(2)}) collective-permute-start(bf16[1024,768]{1,0:T(8,128)(2,1)} %get-tuple-element.115), channel_id=1, source_target_pairs={{0,1},{1,0},{2,3},{3,2},{4,5},{5,4},{6,7},{7,6},{8,9},{9,8},{10,11... | collective-permute-start | bytes 4718600 | tf_op jit(solution)/shard_map/ppermute | solution.py:69
  276.5 10.4 %collective-permute-start.18 = (bf16[512,768]{1,0:T(8,128)(2,1)S(1)}, bf16[512,768]{1,0:T(8,128)(2,1)}, u32[]{:S(2)}, u32[]{:S(2)}) collective-permute-start(bf16[512,768]{1,0:T(8,128)(2,1)S(1)} %slice.393), channel_id=1, source_target_pairs={{0,1},{1,0},{2,3},{3,2},{4,5},{5,4},{6,7},{7,6},{8,9},{9,8},{10,11... | collective-permute-start | bytes 2359304 | tf_op jit(solution)/shard_map/ppermute | solution.py:69
  281.5 71.5 %collective-permute-start.20 = (bf16[4,384,384]{2,1,0:T(8,128)(2,1)}, bf16[4,384,384]{2,1,0:T(8,128)(2,1)S(1)}, u32[]{:S(2)}, u32[]{:S(2)}) collective-permute-start(bf16[4,384,384]{2,1,0:T(8,128)(2,1)} %get-tuple-element.172), channel_id=1, source_target_pairs={{0,2},{2,0},{4,6},{6,4},{1,3},{3,1},{5,7},{7,5},{8,10},{10,8},{12,... | collective-permute-start | bytes 3538952 | tf_op jit(solution)/shard_map/ppermute | solution.py:84
  283.0 70.0 %collective-permute-start.21 = (bf16[4,384,384]{2,1,0:T(8,128)(2,1)}, bf16[4,384,384]{2,1,0:T(8,128)(2,1)}, u32[]{:S(2)}, u32[]{:S(2)}) collective-permute-start(bf16[4,384,384]{2,1,0:T(8,128)(2,1)} %get-tuple-element.171), channel_id=1, source_target_pairs={{0,4},{2,6},{4,0},{6,2},{1,5},{3,7},{5,1},{7,3},{8,12},{10,14},{12... | collective-permute-start | bytes 3538952 | tf_op jit(solution)/shard_map/ppermute | solution.py:84
  283.4 69.5 %collective-permute-start.22 = (bf16[4,384,384]{2,1,0:T(8,128)(2,1)}, bf16[4,384,384]{2,1,0:T(8,128)(2,1)}, u32[]{:S(2)}, u32[]{:S(2)}) collective-permute-start(bf16[4,384,384]{2,1,0:T(8,128)(2,1)} %get-tuple-element.170), channel_id=1, source_target_pairs={{0,6},{2,4},{4,2},{6,0},{1,7},{3,5},{5,3},{7,1},{8,14},{10,12},{12... | collective-permute-start | bytes 3538952 | tf_op jit(solution)/shard_map/ppermute | solution.py:84
  348.6 25.2 %collective-permute-start.24 = (bf16[8,144,384]{2,1,0:T(8,128)(2,1)S(1)}, bf16[8,144,384]{2,1,0:T(8,128)(2,1)}, u32[]{:S(2)}, u32[]{:S(2)}) collective-permute-start(bf16[8,144,384]{2,1,0:T(8,128)(2,1)S(1)} %bitcast.211), channel_id=1, source_target_pairs={{0,4},{4,0},{1,5},{5,1},{2,6},{6,2},{3,7},{7,3},{8,12},{12,8},{9,1... | collective-permute-start | bytes 2654216 | tf_op jit(solution)/shard_map/ppermute | solution.py:74
  350.1 18.0 %collective-permute-start.23 = (bf16[8,96,384]{2,1,0:T(8,128)(2,1)S(1)}, bf16[8,96,384]{2,1,0:T(8,128)(2,1)S(1)}, u32[]{:S(2)}, u32[]{:S(2)}) collective-permute-start(bf16[8,96,384]{2,1,0:T(8,128)(2,1)S(1)} %bitcast.215), channel_id=1, source_target_pairs={{0,2},{2,0},{1,3},{3,1},{4,6},{6,4},{5,7},{7,5},{8,10},{10,8},{9,1... | collective-permute-start | bytes 1769480 | tf_op jit(solution)/shard_map/ppermute | solution.py:74
  358.7 40.0 %collective-permute-start.26 = (bf16[1,384,384]{2,1,0:T(8,128)(2,1)S(1)}, bf16[1,384,384]{2,1,0:T(8,128)(2,1)S(1)}, u32[]{:S(2)}, u32[]{:S(2)}) collective-permute-start(bf16[1,384,384]{2,1,0:T(8,128)(2,1)S(1)} %get-tuple-element.181), channel_id=1, source_target_pairs={{0,8},{8,16},{16,24},{24,0},{1,9},{9,17},{17,25},{25,1},{2,10},{10... | collective-permute-start | bytes 884744 | tf_op jit(solution)/shard_map/ppermute | solution.py:74
  358.8 40.9 %collective-permute-start.27 = (bf16[1,384,384]{2,1,0:T(8,128)(2,1)S(1)}, bf16[1,384,384]{2,1,0:T(8,128)(2,1)S(1)}, u32[]{:S(2)}, u32[]{:S(2)}) collective-permute-start(bf16[1,384,384]{2,1,0:T(8,128)(2,1)S(1)} %get-tuple-element.180), channel_id=1, source_target_pairs={{0,16},{8,24},{16,0},{24,8},{1,17},{9,25},{17,1},{25,9},{2,18},{10... | collective-permute-start | bytes 884744 | tf_op jit(solution)/shard_map/ppermute | solution.py:74
  360.7 39.1 %collective-permute-start.28 = (bf16[1,384,384]{2,1,0:T(8,128)(2,1)S(1)}, bf16[1,384,384]{2,1,0:T(8,128)(2,1)S(1)}, u32[]{:S(2)}, u32[]{:S(2)}) collective-permute-start(bf16[1,384,384]{2,1,0:T(8,128)(2,1)S(1)} %get-tuple-element.179), channel_id=1, source_target_pairs={{0,24},{8,0},{16,8},{24,16},{1,25},{9,1},{17,9},{25,17},{2,26},{10... | collective-permute-start | bytes 884744 | tf_op jit(solution)/shard_map/ppermute | solution.py:74
  372.7 33.9 %collective-permute-start.29 = (bf16[4,96,384]{2,1,0:T(8,128)(2,1)}, bf16[4,96,384]{2,1,0:T(8,128)(2,1)}, u32[]{:S(2)}, u32[]{:S(2)}) collective-permute-start(bf16[4,96,384]{2,1,0:T(8,128)(2,1)} %slice.494), channel_id=1, source_target_pairs={{0,4},{4,0},{1,5},{5,1},{2,6},{6,2},{3,7},{7,3},{8,12},{12,8},{9,1... | collective-permute-start | bytes 884744 | tf_op jit(solution)/shard_map/ppermute | solution.py:74
  377.2 32.0 %collective-permute-start.30 = (bf16[4,144,384]{2,1,0:T(8,128)(2,1)S(1)}, bf16[4,144,384]{2,1,0:T(8,128)(2,1)}, u32[]{:S(2)}, u32[]{:S(2)}) collective-permute-start(bf16[4,144,384]{2,1,0:T(8,128)(2,1)S(1)} %slice.495), channel_id=1, source_target_pairs={{0,2},{2,0},{1,3},{3,1},{4,6},{6,4},{5,7},{7,5},{8,10},{10,8},{9,1... | collective-permute-start | bytes 1327112 | tf_op jit(solution)/shard_map/ppermute | solution.py:74
  398.7 39.4 %collective-permute-start.36 = (bf16[8,128,384]{2,1,0:T(8,128)(2,1)S(1)}, bf16[8,128,384]{2,1,0:T(8,128)(2,1)}, u32[]{:S(2)}, u32[]{:S(2)}) collective-permute-start(bf16[8,128,384]{2,1,0:T(8,128)(2,1)S(1)} %slice.417), channel_id=1, source_target_pairs={{0,4},{4,0},{1,5},{5,1},{2,6},{6,2},{3,7},{7,3},{8,12},{12,8},{9,1... | collective-permute-start | bytes 2359304 | tf_op jit(solution)/shard_map/ppermute | solution.py:74
  399.7 16.3 %collective-permute-start.34 = (bf16[8,96,384]{2,1,0:T(8,128)(2,1)}, bf16[8,96,384]{2,1,0:T(8,128)(2,1)}, u32[]{:S(2)}, u32[]{:S(2)}) collective-permute-start(bf16[8,96,384]{2,1,0:T(8,128)(2,1)} %slice.415), channel_id=1, source_target_pairs={{0,2},{2,0},{1,3},{3,1},{4,6},{6,4},{5,7},{7,5},{8,10},{10,8},{9,1... | collective-permute-start | bytes 1769480 | tf_op jit(solution)/shard_map/ppermute | solution.py:74
  406.5 57.2 %collective-permute-start.25 = (f32[512,768]{1,0:T(8,128)S(1)}, f32[512,768]{1,0:T(8,128)S(1)}, u32[]{:S(2)}, u32[]{:S(2)}) collective-permute-start(f32[512,768]{1,0:T(8,128)S(1)} %slice.405), channel_id=1, source_target_pairs={{0,1},{1,0},{2,3},{3,2},{4,5},{5,4},{6,7},{7,6},{8,9},{9,8},{10,11... | collective-permute-start | bytes 4718600 | tf_op jit(solution)/shard_map/ppermute | solution.py:69
  414.1 12.5 %collective-permute-start.31 = (bf16[240,384]{1,0:T(8,128)(2,1)}, bf16[240,384]{1,0:T(8,128)(2,1)S(1)}, u32[]{:S(2)}, u32[]{:S(2)}) collective-permute-start(bf16[240,384]{1,0:T(8,128)(2,1)} %get-tuple-element.184), channel_id=1, source_target_pairs={{0,8},{8,16},{16,24},{24,0},{1,9},{9,17},{17,25},{25,1},{2,10},{10... | collective-permute-start | bytes 552968 | tf_op jit(solution)/shard_map/ppermute | solution.py:74
  414.1 20.9 %collective-permute-start.32 = (bf16[240,384]{1,0:T(8,128)(2,1)}, bf16[240,384]{1,0:T(8,128)(2,1)S(1)}, u32[]{:S(2)}, u32[]{:S(2)}) collective-permute-start(bf16[240,384]{1,0:T(8,128)(2,1)} %get-tuple-element.185), channel_id=1, source_target_pairs={{0,16},{8,24},{16,0},{24,8},{1,17},{9,25},{17,1},{25,9},{2,18},{10... | collective-permute-start | bytes 552968 | tf_op jit(solution)/shard_map/ppermute | solution.py:74
  416.0 20.3 %collective-permute-start.33 = (bf16[240,384]{1,0:T(8,128)(2,1)}, bf16[240,384]{1,0:T(8,128)(2,1)}, u32[]{:S(2)}, u32[]{:S(2)}) collective-permute-start(bf16[240,384]{1,0:T(8,128)(2,1)} %get-tuple-element.186), channel_id=1, source_target_pairs={{0,24},{8,0},{16,8},{24,16},{1,25},{9,1},{17,9},{25,17},{2,26},{10... | collective-permute-start | bytes 552968 | tf_op jit(solution)/shard_map/ppermute | solution.py:74
  426.7 70.5 %collective-permute-start.49 = (f32[24,3072]{1,0:T(8,128)}, f32[24,3072]{1,0:T(8,128)}, u32[]{:S(2)}, u32[]{:S(2)}) collective-permute-start(f32[24,3072]{1,0:T(8,128)} %bitcast.131), channel_id=1, source_target_pairs={{0,1},{1,0},{2,3},{3,2},{4,5},{5,4},{6,7},{7,6},{8,9},{9,8},{10,11... | collective-permute-start | bytes 884744 | tf_op jit(solution)/shard_map/ppermute | solution.py:69
  435.0 8.8 %collective-permute-start.35 = (bf16[4,96,384]{2,1,0:T(8,128)(2,1)}, bf16[4,96,384]{2,1,0:T(8,128)(2,1)}, u32[]{:S(2)}, u32[]{:S(2)}) collective-permute-start(bf16[4,96,384]{2,1,0:T(8,128)(2,1)} %slice.504), channel_id=1, source_target_pairs={{0,4},{4,0},{1,5},{5,1},{2,6},{6,2},{3,7},{7,3},{8,12},{12,8},{9,1... | collective-permute-start | bytes 884744 | tf_op jit(solution)/shard_map/ppermute | solution.py:74
  441.5 10.4 %collective-permute-start.37 = (bf16[4,128,384]{2,1,0:T(8,128)(2,1)S(1)}, bf16[4,128,384]{2,1,0:T(8,128)(2,1)S(1)}, u32[]{:S(2)}, u32[]{:S(2)}) collective-permute-start(bf16[4,128,384]{2,1,0:T(8,128)(2,1)S(1)} %slice.505), channel_id=1, source_target_pairs={{0,2},{2,0},{1,3},{3,1},{4,6},{6,4},{5,7},{7,5},{8,10},{10,8},{9,1... | collective-permute-start | bytes 1179656 | tf_op jit(solution)/shard_map/ppermute | solution.py:74
  455.6 13.6 %collective-permute-start.38 = (bf16[1,224,384]{2,1,0:T(8,128)(2,1)S(1)}, bf16[1,224,384]{2,1,0:T(8,128)(2,1)S(1)}, u32[]{:S(2)}, u32[]{:S(2)}) collective-permute-start(bf16[1,224,384]{2,1,0:T(8,128)(2,1)S(1)} %get-tuple-element.188), channel_id=1, source_target_pairs={{0,8},{8,16},{16,24},{24,0},{1,9},{9,17},{17,25},{25,1},{2,10},{10... | collective-permute-start | bytes 516104 | tf_op jit(solution)/shard_map/ppermute | solution.py:74
  459.3 12.2 %collective-permute-start.39 = (bf16[1,224,384]{2,1,0:T(8,128)(2,1)S(1)}, bf16[1,224,384]{2,1,0:T(8,128)(2,1)S(1)}, u32[]{:S(2)}, u32[]{:S(2)}) collective-permute-start(bf16[1,224,384]{2,1,0:T(8,128)(2,1)S(1)} %get-tuple-element.189), channel_id=1, source_target_pairs={{0,16},{8,24},{16,0},{24,8},{1,17},{9,25},{17,1},{25,9},{2,18},{10... | collective-permute-start | bytes 516104 | tf_op jit(solution)/shard_map/ppermute | solution.py:74
  461.4 10.0 %collective-permute-start.40 = (bf16[1,224,384]{2,1,0:T(8,128)(2,1)S(1)}, bf16[1,224,384]{2,1,0:T(8,128)(2,1)S(1)}, u32[]{:S(2)}, u32[]{:S(2)}) collective-permute-start(bf16[1,224,384]{2,1,0:T(8,128)(2,1)S(1)} %get-tuple-element.187), channel_id=1, source_target_pairs={{0,24},{8,0},{16,8},{24,16},{1,25},{9,1},{17,9},{25,17},{2,26},{10... | collective-permute-start | bytes 516104 | tf_op jit(solution)/shard_map/ppermute | solution.py:74
  475.2 22.2 %collective-permute-start.50 = (f32[96,768]{1,0:T(8,128)S(1)}, f32[96,768]{1,0:T(8,128)S(1)}, u32[]{:S(2)}, u32[]{:S(2)}) collective-permute-start(f32[96,768]{1,0:T(8,128)S(1)} %get-tuple-element.190), channel_id=1, source_target_pairs={{0,1},{1,0},{2,3},{3,2},{4,5},{5,4},{6,7},{7,6},{8,9},{9,8},{10,11... | collective-permute-start | bytes 884744 | tf_op jit(solution)/shard_map/ppermute | solution.py:69
  479.1 3.8 collective-permute-start.42
  480.3 3.8 collective-permute-start.43
  481.5 4.7 collective-permute-start.44
  486.9 9.0 %collective-permute-start.45 = (f32[8,128]{1,0:T(8,128)S(1)}, f32[8,128]{1,0:T(8,128)S(1)}, u32[]{:S(2)}, u32[]{:S(2)}) collective-permute-start(f32[8,128]{1,0:T(8,128)S(1)} %add_add_fusion.3), channel_id=1, source_target_pairs={{0,8},{8,16},{16,24},{24,0},{1,9},{9,17},{17,25},{25,1},{2,10},{10... | collective-permute-start | bytes 12296 | tf_op jit(solution)/shard_map/ppermute | solution.py:74
  491.0 4.9 collective-permute-start.46
  492.3 3.6 collective-permute-start.47
  (53 other events, 203.6 us)
Sparse Core Ops, SparseCore 0:
  12.1 173.7 all-gather.1
  277.7 157.1 reduce-scatter.1

commit v4 on v3

--- a/solution.py
+++ b/solution.py
@@ -32,13 +32,14 @@
 F32 = jnp.float32
 AXES = ("z", "y", "x", "c")
 CHIP = ("z", "y", "x")
+BLOCK = 64
 VMEM_LIMIT = 56 * 1024 * 1024
 NT = (((1,), (1,)), ((), ()))
 
 
 def cost(microseconds):
     return pl.CostEstimate(
-        flops=int(microseconds * 1.1e9), bytes_accessed=int(microseconds * 3.5e6), transcendentals=0
+        flops=int(microseconds * 0.1e9), bytes_accessed=int(microseconds * 3.2 * 0.1e6), transcendentals=0
     )
 
 
@@ -138,7 +139,8 @@
 
 
 def inverse_of(where):
-    return jnp.zeros_like(where).at[where].set(jnp.arange(where.shape[0], dtype=jnp.int32))
+    spots = jnp.arange(where.shape[0], dtype=jnp.int32)
+    return jnp.sum(jnp.where(where[None, :] == spots[:, None], spots[None, :], 0), axis=1)
 
 
 def in_order(stacks, where, begin, end):
@@ -300,14 +302,14 @@
     return jnp.where((lanes >= HD) == (head == 1), value, jnp.zeros_like(value))
 
 
-def scores_t(key_side, query_side, strip, head, valid):
-    count = key_side.shape[0]
-    raw = dot_nt(key_side, query_side)
+def scores_t(raw, strip, head, valid):
+    count = raw.shape[0]
     blocks = []
-    for block in range(count // 128):
+    for begin in range(0, count, BLOCK):
+        block, row = divmod(begin, 128)
         start = 384 - 128 * block
-        part = raw[128 * block : 128 * block + 128] + strip[head, :, start : start + count]
-        rows = lax.broadcasted_iota(jnp.int32, (128, count), 0) + 128 * block
+        part = raw[begin : begin + BLOCK] + strip[head, row : row + BLOCK, start : start + count]
+        rows = lax.broadcasted_iota(jnp.int32, (BLOCK, count), 0) + begin
         blocks.append(jnp.where(rows < valid, part, NEGATIVE))
     return blocks
 
@@ -325,21 +327,23 @@
     key_side = jnp.concatenate([both, k_ref[...]], axis=1)
     values_t = v_ref[...].T
     mixed = []
+    raws = []
     for head in range(2):
         query_side = jnp.concatenate(
             [left_side(both, planes, head), head_lanes(q_ref[...], head)], axis=1
         )
-        blocks = scores_t(key_side, query_side, strip, head, valid)
-        highest = functools.reduce(
-            jnp.maximum, [jnp.max(block, axis=0, keepdims=True) for block in blocks]
-        )
-        raised = [jnp.exp(block - highest) for block in blocks]
-        total = functools.reduce(
-            jnp.add, [jnp.sum(part, axis=0, keepdims=True) for part in raised]
-        )
-        inverse = 1.0 / total
-        probs = jnp.concatenate([(part * inverse).astype(BF) for part in raised], axis=0)
-        mixed.append(dot(values_t[HD * head : HD * head + HD], probs))
+        raws.append(dot_nt(key_side, query_side))
+    for head in range(2):
+        blocks = scores_t(raws[head], strip, head, valid)
+        highest = jnp.max(functools.reduce(jnp.maximum, blocks), axis=0, keepdims=True)
+        total, raised = None, []
+        for block in blocks:
+            part = jnp.exp(block - highest)
+            total = part if total is None else total + part
+            raised.append(part.astype(BF))
+        total = jnp.sum(total, axis=0, keepdims=True)
+        product = dot(values_t[HD * head : HD * head + HD], jnp.concatenate(raised, axis=0))
+        mixed.append(product * (1.0 / total))
         log_ref[0, 0, head : head + 1, :] = highest + jnp.log(total)
     mixed_ref[...] = jnp.concatenate(mixed, axis=0).T.astype(BF)
 
@@ -412,23 +416,28 @@
     weighted = d_mixed_t.astype(F32) * mixed_ref[...].T.astype(F32)
     rows = lax.broadcasted_iota(jnp.int32, d_mixed_t.shape, 0)
     d_keys = d_values = None
-    d_queries = []
+    d_queries, masked, raws, d_all = [], [], [], []
     for head in range(2):
-        masked_q = head_lanes(q_ref[...], head)
-        query_side = jnp.concatenate([left_side(both, planes, head), masked_q], axis=1)
-        blocks = scores_t(key_side, query_side, strip, head, valid)
-        log_total = log_ref[0, 0, head : head + 1, :]
-        inner = jnp.sum(weighted[HD * head : HD * head + HD], axis=0, keepdims=True)
+        masked.append(head_lanes(q_ref[...], head))
+        query_side = jnp.concatenate([left_side(both, planes, head), masked[head]], axis=1)
+        raws.append(dot_nt(key_side, query_side))
         d_mixed_head = jnp.where(
             (rows >= HD) == (head == 1), d_mixed_t, jnp.zeros_like(d_mixed_t)
         )
-        d_probs = dot(values, d_mixed_head)
+        d_all.append(dot(values, d_mixed_head))
+    for head in range(2):
+        masked_q, d_probs = masked[head], d_all[head]
+        blocks = scores_t(raws[head], strip, head, valid)
+        log_total = log_ref[0, 0, head : head + 1, :]
+        inner = jnp.sum(weighted[HD * head : HD * head + HD], axis=0, keepdims=True)
         probs_low, scores_low = [], []
         for index, block in enumerate(blocks):
+            begin = BLOCK * index
+            row = begin % 128
             probs = jnp.exp(block - log_total)
-            d_scores = probs * (d_probs[128 * index : 128 * index + 128] - inner)
-            start = 384 - 128 * index
-            d_strip[head, :, start : start + count] += d_scores
+            d_scores = probs * (d_probs[begin : begin + BLOCK] - inner)
+            start = 384 - begin // 128 * 128
+            d_strip[head, row : row + BLOCK, start : start + count] += d_scores
             probs_low.append(probs.astype(BF))
             scores_low.append(d_scores.astype(BF))
         probs_low = jnp.concatenate(probs_low, axis=0)
@@ -503,21 +512,8 @@
 
 
 def gelu_parts(before):
-    size = jnp.abs(before) * (0.5**0.5)
-    denominator = 1.0 + 0.3275911 * size
-    t = pl.reciprocal(denominator, approx=True)
-    t = t * (2.0 - denominator * t)
     bell = jnp.exp(-0.5 * before * before)
-    tail = t * (
-        0.5 * 0.254829592
-        + t
-        * (
-            0.5 * -0.284496736
-            + t * (0.5 * 1.421413741 + t * (0.5 * -1.453152027 + t * (0.5 * 1.061405429)))
-        )
-    )
-    tail = tail * bell
-    below = jnp.where(before >= 0.0, 1.0 - tail, tail)
+    below = 0.5 + 0.5 * lax.erf(before * (0.5**0.5))
     return before * below, below + before * (bell * 0.3989422804014327)
 
 
@@ -666,10 +662,13 @@
     place(where_ref, stacks, wide_ref.at[0])
     width = inputs_ref.shape[1]
     weight = wide_ref[0].reshape(width, width)
-    before = dot(low_ref[...], weight) + bias_ref[...]
-    active, slope = gelu_parts(before)
-    active_ref[...] = active.astype(BF)
-    slope_ref[...] = slope.astype(BF)
+    count = low_ref.shape[0] // 4
+    for part in range(4):
+        here = pl.ds(count * part, count)
+        before = dot(low_ref[here, :], weight) + bias_ref[...]
+        active, slope = gelu_parts(before)
+        active_ref[here, :] = active.astype(BF)
+        slope_ref[here, :] = slope.astype(BF)
 
 
 def feed_call(where, stacks, rows, inputs, own, other, vecs, bias):

time: 518 us -> 501 us (0.967)
  Pallas kernels: 234 us -> 221 us
  waiting for transfers between devices: 129 us -> 122 us
    ppermute x27, waiting for transfers between devices: 102 us -> 90.4 us  [shift(): lax.ppermute(value, axis, [(i, (i + step) % size) for i in range(size)])]
    pallas_call x1, Pallas kernels: 25.3 us -> 17.2 us  [feed_call(): pl.pallas_call(functools.partial(feed_kernel, len(stacks)), grid=(hidden...]
    unnamed x110 -> x112, local copies, waits for them, and re-layouts: 11.6 us -> 10.2 us
  transfers between devices with their start and end apart: 53 -> 53, of which waited for: 19 -> 19; matrix products, arithmetic and copies ran while one was open for 13% -> 13% of each run, Pallas kernels for 28% -> 34%
where the time goes in v4:
time: 501 us; the launch traced here: 495 us
  Pallas kernels  221 us (44%)
  waiting for transfers between devices  122 us (24%)
  starting transfers between devices  53.9 us (11%)
  local copies, waits for them, and re-layouts  45.4 us (9%)
  other arithmetic  29.8 us (6%)
  between operations  20.5 us (4%)
    ppermute x27, waiting for transfers between devices, shift(): lax.ppermute(value, axis, [(i, (i + step) % size) for i in range(size)])  90.4 us
    ppermute x27, starting transfers between devices, shift(): lax.ppermute(value, axis, [(i, (i + step) % size) for i in range(size)])  42.7 us
    pallas_call x2, Pallas kernels, attend_back_call(): pl.pallas_call(waiting(attend_back_kernel, 10, len(others)), grid=(pairs,...  42.5 us
    pallas_call x1, Pallas kernels, feed_back_call(): pl.pallas_call(waiting(feed_back_kernel, 10, len(others)), grid=(hidden /...  25.9 us
    pallas_call x1, Pallas kernels, attend_call(): pl.pallas_call(attend_kernel, grid=(pairs, pages), in_specs=[pl.BlockSpec...  24.9 us
    all_gather x1, waiting for transfers between devices, body(): wide_rest = lax.all_gather(rest, CHIP)  23.5 us
    pallas_call x10, Pallas kernels, sum_call(): pl.pallas_call(functools.partial(sum_kernel, 1 + len(moved)), grid=(steps...  22.1 us
    pallas_call x1, Pallas kernels, feed_call(): pl.pallas_call(functools.partial(feed_kernel, len(stacks)), grid=(hidden...  17.2 us
  transfers between devices with their start and end apart: 53, of which 19 were waited for; matrix products, arithmetic and copies ran while one was open for 13% of the time, Pallas kernels for 34%

profile of v4, /device:TPU:0, one launch (start us, length us, event | category | flops | bytes accessed | tf_op | source)
XLA Modules:
  0.0 494.6 jit_solution(18424554016033218380)
XLA Ops:
  17.1 2.9 collective-permute-start.6
  20.1 2.6 collective-permute-start.7
  26.0 4.6 collective-permute-done.6
  30.5 21.3 %collective-permute-done.7 = bf16[176,768]{1,0:T(8,128)(2,1)S(1)} collective-permute-done((bf16[176,768]{1,0:T(8,128)(2,1)S(1)}, bf16[176,768]{1,0:T(8,128)(2,1)S(1)}, u32[]{:S(2)}, u32[]{:S(2)}) %collective-permute-start.7) | collective-permute-done | bytes 270368 | tf_op jit(solution)/shard_map/ppermute | solution.py:75
  56.6 10.0 %collective-permute-done.11 = bf16[4,176,384]{2,1,0:T(8,128)(2,1)S(1)} collective-permute-done((bf16[4,176,384]{2,1,0:T(8,128)(2,1)S(1)}, bf16[4,176,384]{2,1,0:T(8,128)(2,1)S(1)}, u32[]{:S(2)}, u32[]{:S(2)}) %collective-permute-start.11) | collective-permute-done | bytes 540704 | tf_op jit(solution)/shard_map/ppermute | solution.py:75
  68.2 5.1 %collective-permute-done.9 = bf16[4,176,384]{2,1,0:T(8,128)(2,1)S(1)} collective-permute-done((bf16[4,176,384]{2,1,0:T(8,128)(2,1)S(1)}, bf16[4,176,384]{2,1,0:T(8,128)(2,1)S(1)}, u32[]{:S(2)}, u32[]{:S(2)}) %collective-permute-start.9) | collective-permute-done | bytes 540704 | tf_op jit(solution)/shard_map/ppermute | solution.py:75
  74.9 2.4 pad_maximum_fusion.raw_ref
  77.4 33.5 %collective-permute-done.12.refs_3_ = bf16[8,176,384]{2,1,0:T(8,128)(2,1)S(1)} collective-permute-done((bf16[8,176,384]{2,1,0:T(8,128)(2,1)S(1)}, bf16[8,176,384]{2,1,0:T(8,128)(2,1)S(1)}, u32[]{:S(2)}, u32[]{:S(2)}) %collective-permute-start.12) | collective-permute-done | bytes 1081376 | tf_op jit(solution)/shard_map/ppermute | solution.py:75
  118.5 11.4 %project.1 = (bf16[3,1024,768]{2,1,0:T(8,128)(2,1)}, bf16[3,16,48,768]{3,2,1,0:T(8,128)(2,1)}, f32[1024,768]{1,0:T(8,128)}, f32[1024,768]{1,0:T(8,128)}, bf16[10...) custom-call(s32[16]{0:T(128)} %copy-done.47, s32[16]{0:T(128)} %copy-done.46, bf16[1024,768]{1,0:T(8,128)(2,1)} %pad_maximum_fusion.raw_ref, ...), custom_call_target="tpu_custom_call" | custom-call | flops 1200000000 | bytes 3840000 | tf_op jit(solution)/shard_map/project/pallas_call | solution.py:581
  131.1 24.9 %attend.1 = (bf16[1024,768]{1,0:T(8,128)(2,1)}, f32[2,6,8,512]{3,2,1,0:T(8,128)}) custom-call(s32[2]{0:T(128)} %get-tuple-element.166.valid_ref.refs_0_, bf16[3,1024,768]{2,1,0:T(8,128)(2,1)} %get-tuple-element.96.q_ref.k_ref.v_ref.refs_1_.refs_2_.refs_3_, bf16[3,1024,768]{2,1,0:T(8,128)(2,1)} %get-tuple-element.96.q_ref.k_ref.v_ref.refs_1_.refs_2_.refs_3_, ...), custom_call_target="tpu_custom_call" | custom-call | flops 2800000000 | bytes 8960000 | tf_op jit(solution)/shard_map/attend/pallas_call | solution.py:358
  156.0 6.2 %turn.1 = (bf16[3,768,1024]{2,1,0:T(8,128)(2,1)}, bf16[256,1024]{1,0:T(8,128)(2,1)}) custom-call(bf16[1024,768]{1,0:T(8,128)(2,1)} %get-tuple-element.98.joint_ref, bf16[1024,768]{1,0:T(8,128)(2,1)} %get-tuple-element.99.plain_ref, bf16[1024,768]{1,0:T(8,128)(2,1)} %get-tuple-element.97.mixed_ref.refs_1_.refs_5_, ...), custom_call_target="tpu_custom_call" | custom-call | flops 800000000 | bytes 2560000 | tf_op jit(solution)/shard_map/turn/pallas_call | solution.py:918
  162.2 23.5 %all-gather.2.cloned.1.call-done.refs_3_.refs_0_ = bf16[16,432,768]{2,1,0:T(8,128)(2,1)} async-done(((bf16[1,432,768]{2,1,0:T(8,128)(2,1)}), bf16[16,432,768]{2,1,0:T(8,128)(2,1)}) %all-gather.2.cloned.1.call-update) | async-done | bytes 10616848 | tf_op jit(solution)/shard_map/all_gather | solution.py:1269
  186.2 6.1 %output.1 = (f32[1024,768]{1,0:T(8,128)}, bf16[1024,768]{1,0:T(8,128)(2,1)}, bf16[16,48,768]{2,1,0:T(8,128)(2,1)}) custom-call(s32[16]{0:T(128)} %iota.47.refs_0_, bf16[1024,768]{1,0:T(8,128)(2,1)} %get-tuple-element.97.mixed_ref.refs_1_.refs_5_, f32[1024,1]{1,0:T(8,128)} %bitcast.182, bf16[16,432,768]{2,1,0:T(8,128)(2,1)} %all-gather.2.cloned.1.call-done.refs_3_.refs_0_, ...), custom_call_target="tpu_custom_call" | custom-call | flops 500000000 | bytes 1600000 | tf_op jit(solution)/shard_map/output/pallas_call | solution.py:622
  193.0 3.8 collective-permute-done.17
  200.8 17.2 %feed.1 = (f32[1024,768]{1,0:T(8,128)}, bf16[1024,768]{1,0:T(8,128)(2,1)}, f32[1024,768]{1,0:T(8,128)}, f32[1024,1]{1,0:T(8,128)}, bf16[1024,3072]{1,0:T(8,128)(...) custom-call(s32[16]{0:T(128)} %iota.44.where_ref, f32[1024,768]{1,0:T(8,128)} %get-tuple-element.95.inputs_ref, ...), custom_call_target="tpu_custom_call" | custom-call | flops 2400000000 | bytes 7680000 | tf_op jit(solution)/shard_map/feed/pallas_call | solution.py:681
  218.5 13.0 %close.1 = (bf16[1024,768]{1,0:T(8,128)(2,1)}, f32[1024,768]{1,0:T(8,128)}, bf16[1024,768]{1,0:T(8,128)(2,1)}, f32[8,768]{1,0:T(8,128)}, bf16[16,192,768]{2,1,0:T(8,128)(2,1)}) custom-call(s32[16]{0:T(128)} %iota.43.where_ref, bf16[1024,3072]{1,0:T(8,128)(2,1)} %get-tuple-element.103.active_ref, f32[1024,768]{1,0:T(8,128)} %get-tuple-element.104.u_ref, ...), custom_call_target="tpu_custom_call" | custom-call | flops 1300000000 | bytes 4160000 | tf_op jit(solution)/shard_map/close/pallas_call | solution.py:744
  232.1 9.9 %second.1.refs_10_ = bf16[16,192,768]{2,1,0:T(8,128)(2,1)} custom-call(s32[16]{0:T(128)} %iota.50.slots_ref, bf16[1024,3072]{1,0:T(8,128)(2,1)} %get-tuple-element.103.active_ref, bf16[1024,768]{1,0:T(8,128)(2,1)} %get-tuple-element.107.low_ref.refs_2_), custom_call_target="tpu_custom_call" | custom-call | flops 1000000000 | bytes 3200000 | tf_op jit(solution)/shard_map/second/pallas_call | solution.py:792
  242.5 25.9 %feed_back.1 = (f32[1024,768]{1,0:T(8,128)}, bf16[1024,768]{1,0:T(8,128)(2,1)}, bf16[16,384,384]{2,1,0:T(8,128)(2,1)}, f32[4,1,768]{2,1,0:T(1,128)}, f32[8,768]{1,0:T(8,128)}) custom-call(s32[16]{0:T(128)} %multiply_add_fusion.1.refs_0_.slots_ref, bf16[1024,768]{1,0:T(8,128)(2,1)} %get-tuple-element.106.refs_1_, ...), custom_call_target="tpu_custom_call" | custom-call | flops 2600000000 | bytes 8320000 | tf_op jit(solution)/shard_map/feed_back/pallas_call | solution.py:847
  268.6 3.9 fusion.55
  277.8 5.7 %middle.1 = (bf16[1024,768]{1,0:T(8,128)(2,1)}, bf16[1024,768]{1,0:T(8,128)(2,1)}) custom-call(f32[1024,768]{1,0:T(8,128)} %get-tuple-element.114.own_ref.refs_6_, bf16[1024,768]{1,0:T(8,128)(2,1)} %copy-done.19, f32[1024,1]{1,0:T(8,128)} %bitcast.184, bf16[768,768]{1,0:T(8,128)(2,1)} %bitcast.201), custom_call_target="tpu_custom_call" | custom-call | flops 600000000 | bytes 1920000 | tf_op jit(solution)/shard_map/middle/pallas_call | solution.py:897
  283.5 21.3 %attend_back.2 = (bf16[3,1024,384]{2,1,0:T(8,128)(2,1)}, f32[6,8,512]{2,1,0:T(8,128)}) custom-call(s32[2]{0:T(128)} %get-tuple-element.166.valid_ref.refs_0_, bf16[3,1024,768]{2,1,0:T(8,128)(2,1)} %get-tuple-element.96.q_ref.k_ref.v_ref.refs_1_.refs_2_.refs_3_, bf16[3,1024,768]{2,1,0:T(8,128)(2,1)} %get-tuple-element.96.q_ref.k_ref.v_ref.refs_1_.refs_2_.refs_3_, ...), custom_call_target="tpu_custom_call" | custom-call | flops 2100000000 | bytes 6720000 | tf_op jit(solution)/shard_map/attend_back/pallas_call | solution.py:478
  304.9 9.5 %grads_one.1 = (bf16[16,2,48,384]{3,2,1,0:T(8,128)(2,1)}, bf16[16,3,48,384]{3,2,1,0:T(8,128)(2,1)}) custom-call(s32[16]{0:T(128)} %multiply_add_fusion.1.refs_0_.slots_ref, s32[16]{0:T(128)} %multiply_add_fusion.turned_ref.refs_1_, bf16[3,768,1024]{2,1,0:T(8,128)(2,1)} %get-tuple-element.100.refs_4_.left_ref.refs_2_, ...), custom_call_target="tpu_custom_call" | custom-call | flops 900000000 | bytes 2880000 | tf_op jit(solution)/shard_map/grads_one/pallas_call | solution.py:952
  314.4 2.1 slice.400
  321.3 21.2 %attend_back.3 = (bf16[3,1024,384]{2,1,0:T(8,128)(2,1)}, f32[6,8,512]{2,1,0:T(8,128)}) custom-call(s32[2]{0:T(128)} %get-tuple-element.166.valid_ref.refs_0_, bf16[3,1024,768]{2,1,0:T(8,128)(2,1)} %get-tuple-element.96.q_ref.k_ref.v_ref.refs_1_.refs_2_.refs_3_, bf16[3,1024,768]{2,1,0:T(8,128)(2,1)} %get-tuple-element.96.q_ref.k_ref.v_ref.refs_1_.refs_2_.refs_3_, ...), custom_call_target="tpu_custom_call" | custom-call | flops 2100000000 | bytes 6720000 | tf_op jit(solution)/shard_map/attend_back/pallas_call | solution.py:478
  343.6 3.6 sum.10.refs_11_.refs_0_
  347.2 2.1 fusion.56
  351.2 2.4 collective-permute-start.28
  356.0 2.0 sum.11.refs_12_.refs_0_
  360.5 2.3 sum.12.refs_13_.refs_0_
  363.9 15.7 %grads_two.1 = (bf16[16,96,384]{2,1,0:T(8,128)(2,1)}, bf16[16,128,384]{2,1,0:T(8,128)(2,1)}, f32[1024,768]{1,0:T(8,128)}) custom-call(s32[16]{0:T(128)} %multiply_add_fusion.1.refs_0_.slots_ref, s32[16]{0:T(128)} %multiply_add_fusion.turned_ref.refs_1_, bf16[3,768,1024]{2,1,0:T(8,128)(2,1)} %get-tuple-element.100.refs_4_.left_ref.refs_2_, ...), custom_call_target="tpu_custom_call" | custom-call | flops 1000000000 | bytes 3200000 | tf_op jit(solution)/shard_map/grads_two/pallas_call | solution.py:1034
  386.5 2.4 select_bitcast_fusion.2
  388.9 2.2 sum.13
  396.8 2.0 sum.15
  399.9 3.9 collective-permute-start.31
  403.8 3.0 collective-permute-start.32
  406.8 2.9 collective-permute-done.34.refs_1_
  412.6 2.0 sum.16.refs_0_
  415.7 2.2 sum.18.refs_0_
  424.0 4.4 collective-permute-done.35.refs_1_
  433.6 2.1 sum.19
  438.3 3.4 collective-permute-start.39
  441.6 1.9 pad_maximum_fusion.6.refs_0_
  449.2 2.9 collective-permute-done.39.refs_2_
  452.8 2.2 late.1.own_ref.refs_2_
  464.9 2.2 collective-permute-done.44
  467.8 3.6 collective-permute-start.45
  471.5 2.5 collective-permute-start.47
  478.8 7.3 %adam.1 = (f32[2,4,24,768]{3,2,1,0:T(8,128)}, f32[2,4,24,768]{3,2,1,0:T(8,128)}, f32[2,4,24,768]{3,2,1,0:T(8,128)}, bf16[2,4,24,768]{3,2,1,0:T(8,128)(2,1)}, f32...) custom-call(f32[8,128]{1,0:T(8,128)} %copy-done.41, ...), custom_call_target="tpu_custom_call" | custom-call | flops 900000000 | bytes 2880000 | tf_op jit(solution)/shard_map/adam/pallas_call | solution.py:1180
  (386 shorter events, 104.7 us)
Async XLA Ops:
  7.2 178.5 %all-gather.2.cloned.1.call-start = ((), (), s32[]{:S(2)}) async-start(), calls=%async_computation.1 | async-start | bytes 11280384 | tf_op jit(solution)/shard_map/all_gather | solution.py:1269
  12.0 433.5 %reduce-scatter.2.cloned.1.call-start = ((), (), s32[]{:S(2)}) async-start(), calls=%async_computation.2 | async-start | bytes 5013504 | tf_op jit(solution)/shard_map/reduce_scatter | solution.py:1400
  13.2 3.7 collective-permute-start.4
  13.5 3.5 collective-permute-start.3
  14.1 2.8 collective-permute-start.5
  14.4 42.2 %collective-permute-start.1 = (s32[1,2,512]{2,1,0:T(2,128)S(1)}, s32[1,2,512]{2,1,0:T(2,128)S(1)}, u32[]{:S(2)}, u32[]{:S(2)}) collective-permute-start(s32[1,2,512]{2,1,0:T(2,128)S(1)} %copy-done.44), channel_id=1, source_target_pairs={{0,1},{1,0},{2,3},{3,2},{4,5},{5,4},{6,7},{7,6},{8,9},{9,8},{10,11... | collective-permute-start | bytes 12296 | tf_op jit(solution)/shard_map/ppermute | solution.py:70
  14.7 10.0 %collective-permute-start.13 = (s32[1]{0:T(128)}, s32[1]{0:T(128)}, u32[]{:S(2)}, u32[]{:S(2)}) collective-permute-start(s32[1]{0:T(128)} %param.32), channel_id=1, source_target_pairs={{0,1},{1,0},{2,3},{3,2},{4,5},{5,4},{6,7},{7,6},{8,9},{9,8},{10,11... | collective-permute-start | bytes 20 | tf_op jit(solution)/shard_map/ppermute | solution.py:70
  17.1 13.4 %collective-permute-start.6 = (bf16[176,768]{1,0:T(8,128)(2,1)S(1)}, bf16[176,768]{1,0:T(8,128)(2,1)S(1)}, u32[]{:S(2)}, u32[]{:S(2)}) collective-permute-start(bf16[176,768]{1,0:T(8,128)(2,1)S(1)} %get-tuple-element.207), channel_id=1, source_target_pairs={{0,8},{8,16},{16,24},{24,0},{1,9},{9,17},{17,25},{25,1},{2,10},{10... | collective-permute-start | bytes 811016 | tf_op jit(solution)/shard_map/ppermute | solution.py:75
  20.1 31.7 %collective-permute-start.7 = (bf16[176,768]{1,0:T(8,128)(2,1)S(1)}, bf16[176,768]{1,0:T(8,128)(2,1)S(1)}, u32[]{:S(2)}, u32[]{:S(2)}) collective-permute-start(bf16[176,768]{1,0:T(8,128)(2,1)S(1)} %get-tuple-element.207), channel_id=1, source_target_pairs={{0,16},{8,24},{16,0},{24,8},{1,17},{9,25},{17,1},{25,9},{2,18},{10... | collective-permute-start | bytes 811016 | tf_op jit(solution)/shard_map/ppermute | solution.py:75
  22.7 29.5 %collective-permute-start.8 = (bf16[176,768]{1,0:T(8,128)(2,1)S(1)}, bf16[176,768]{1,0:T(8,128)(2,1)S(1)}, u32[]{:S(2)}, u32[]{:S(2)}) collective-permute-start(bf16[176,768]{1,0:T(8,128)(2,1)S(1)} %get-tuple-element.207), channel_id=1, source_target_pairs={{0,24},{8,0},{16,8},{24,16},{1,25},{9,1},{17,9},{25,17},{2,26},{10... | collective-permute-start | bytes 811016 | tf_op jit(solution)/shard_map/ppermute | solution.py:75
  24.7 50.2 %collective-permute-start = (bf16[512,768]{1,0:T(8,128)(2,1)}, bf16[512,768]{1,0:T(8,128)(2,1)}, u32[]{:S(2)}, u32[]{:S(2)}) collective-permute-start(bf16[512,768]{1,0:T(8,128)(2,1)} %get-tuple-element.178), channel_id=1, source_target_pairs={{0,1},{1,0},{2,3},{3,2},{4,5},{5,4},{6,7},{7,6},{8,9},{9,8},{10,11... | collective-permute-start | bytes 2359304 | tf_op jit(solution)/shard_map/ppermute | solution.py:70
  52.4 14.1 %collective-permute-start.11 = (bf16[4,176,384]{2,1,0:T(8,128)(2,1)S(1)}, bf16[4,176,384]{2,1,0:T(8,128)(2,1)S(1)}, u32[]{:S(2)}, u32[]{:S(2)}) collective-permute-start(bf16[4,176,384]{2,1,0:T(8,128)(2,1)S(1)} %get-tuple-element.182), channel_id=1, source_target_pairs={{0,4},{4,0},{1,5},{5,1},{2,6},{6,2},{3,7},{7,3},{8,12},{12,8},{9,1... | collective-permute-start | bytes 1622024 | tf_op jit(solution)/shard_map/ppermute | solution.py:75
  55.1 18.2 %collective-permute-start.9 = (bf16[4,176,384]{2,1,0:T(8,128)(2,1)S(1)}, bf16[4,176,384]{2,1,0:T(8,128)(2,1)S(1)}, u32[]{:S(2)}, u32[]{:S(2)}) collective-permute-start(bf16[4,176,384]{2,1,0:T(8,128)(2,1)S(1)} %get-tuple-element.183), channel_id=1, source_target_pairs={{0,2},{2,0},{1,3},{3,1},{4,6},{6,4},{5,7},{7,5},{8,10},{10,8},{9,1... | collective-permute-start | bytes 1622024 | tf_op jit(solution)/shard_map/ppermute | solution.py:75
  66.7 44.2 %collective-permute-start.12 = (bf16[8,176,384]{2,1,0:T(8,128)(2,1)S(1)}, bf16[8,176,384]{2,1,0:T(8,128)(2,1)S(1)}, u32[]{:S(2)}, u32[]{:S(2)}) collective-permute-start(bf16[8,176,384]{2,1,0:T(8,128)(2,1)S(1)} %pad_maximum_fusion.4.refs_2_), channel_id=1, source_target_pairs={{0,2},{2,0},{1,3},{3,1},{4,6},{6,4},{5,7},{7,5},{8,10},{10,8},{9,1... | collective-permute-start | bytes 3244040 | tf_op jit(solution)/shard_map/ppermute | solution.py:75
  73.5 39.2 %collective-permute-start.10 = (bf16[8,176,384]{2,1,0:T(8,128)(2,1)S(1)}, bf16[8,176,384]{2,1,0:T(8,128)(2,1)}, u32[]{:S(2)}, u32[]{:S(2)}) collective-permute-start(bf16[8,176,384]{2,1,0:T(8,128)(2,1)S(1)} %pad_maximum_fusion.3.refs_0_), channel_id=1, source_target_pairs={{0,4},{4,0},{1,5},{5,1},{2,6},{6,2},{3,7},{7,3},{8,12},{12,8},{9,1... | collective-permute-start | bytes 3244040 | tf_op jit(solution)/shard_map/ppermute | solution.py:75
  192.3 7.3 %collective-permute-start.16 = (bf16[1024,768]{1,0:T(8,128)(2,1)}, bf16[1024,768]{1,0:T(8,128)(2,1)S(1)}, u32[]{:S(2)}, u32[]{:S(2)}) collective-permute-start(bf16[1024,768]{1,0:T(8,128)(2,1)} %get-tuple-element.102), channel_id=1, source_target_pairs={{0,1},{1,0},{2,3},{3,2},{4,5},{5,4},{6,7},{7,6},{8,9},{9,8},{10,11... | collective-permute-start | bytes 4718600 | tf_op jit(solution)/shard_map/ppermute | solution.py:70
  192.4 4.4 collective-permute-start.17
  268.4 8.2 %collective-permute-start.19 = (bf16[1024,768]{1,0:T(8,128)(2,1)}, bf16[1024,768]{1,0:T(8,128)(2,1)S(1)}, u32[]{:S(2)}, u32[]{:S(2)}) collective-permute-start(bf16[1024,768]{1,0:T(8,128)(2,1)} %get-tuple-element.115), channel_id=1, source_target_pairs={{0,1},{1,0},{2,3},{3,2},{4,5},{5,4},{6,7},{7,6},{8,9},{9,8},{10,11... | collective-permute-start | bytes 4718600 | tf_op jit(solution)/shard_map/ppermute | solution.py:70
  272.6 69.9 %collective-permute-start.20 = (bf16[4,384,384]{2,1,0:T(8,128)(2,1)}, bf16[4,384,384]{2,1,0:T(8,128)(2,1)}, u32[]{:S(2)}, u32[]{:S(2)}) collective-permute-start(bf16[4,384,384]{2,1,0:T(8,128)(2,1)} %get-tuple-element.172), channel_id=1, source_target_pairs={{0,2},{2,0},{4,6},{6,4},{1,3},{3,1},{5,7},{7,5},{8,10},{10,8},{12,... | collective-permute-start | bytes 3538952 | tf_op jit(solution)/shard_map/ppermute | solution.py:85
  274.1 69.5 %collective-permute-start.21 = (bf16[4,384,384]{2,1,0:T(8,128)(2,1)}, bf16[4,384,384]{2,1,0:T(8,128)(2,1)}, u32[]{:S(2)}, u32[]{:S(2)}) collective-permute-start(bf16[4,384,384]{2,1,0:T(8,128)(2,1)} %get-tuple-element.171), channel_id=1, source_target_pairs={{0,4},{2,6},{4,0},{6,2},{1,5},{3,7},{5,1},{7,3},{8,12},{10,14},{12... | collective-permute-start | bytes 3538952 | tf_op jit(solution)/shard_map/ppermute | solution.py:85
  274.6 68.9 %collective-permute-start.22 = (bf16[4,384,384]{2,1,0:T(8,128)(2,1)}, bf16[4,384,384]{2,1,0:T(8,128)(2,1)}, u32[]{:S(2)}, u32[]{:S(2)}) collective-permute-start(bf16[4,384,384]{2,1,0:T(8,128)(2,1)} %get-tuple-element.170), channel_id=1, source_target_pairs={{0,6},{2,4},{4,2},{6,0},{1,7},{3,5},{5,3},{7,1},{8,14},{10,12},{12... | collective-permute-start | bytes 3538952 | tf_op jit(solution)/shard_map/ppermute | solution.py:85
  316.5 34.7 %collective-permute-start.23 = (bf16[8,96,384]{2,1,0:T(8,128)(2,1)}, bf16[8,96,384]{2,1,0:T(8,128)(2,1)}, u32[]{:S(2)}, u32[]{:S(2)}) collective-permute-start(bf16[8,96,384]{2,1,0:T(8,128)(2,1)} %bitcast.57), channel_id=1, source_target_pairs={{0,2},{2,0},{1,3},{3,1},{4,6},{6,4},{5,7},{7,5},{8,10},{10,8},{9,1... | collective-permute-start | bytes 1769480 | tf_op jit(solution)/shard_map/ppermute | solution.py:75
  320.7 38.4 %collective-permute-start.24 = (bf16[8,144,384]{2,1,0:T(8,128)(2,1)}, bf16[8,144,384]{2,1,0:T(8,128)(2,1)S(1)}, u32[]{:S(2)}, u32[]{:S(2)}) collective-permute-start(bf16[8,144,384]{2,1,0:T(8,128)(2,1)} %bitcast.58), channel_id=1, source_target_pairs={{0,4},{4,0},{1,5},{5,1},{2,6},{6,2},{3,7},{7,3},{8,12},{12,8},{9,1... | collective-permute-start | bytes 2654216 | tf_op jit(solution)/shard_map/ppermute | solution.py:75
  342.5 41.0 %collective-permute-start.18 = (bf16[512,768]{1,0:T(8,128)(2,1)}, bf16[512,768]{1,0:T(8,128)(2,1)S(1)}, u32[]{:S(2)}, u32[]{:S(2)}) collective-permute-start(bf16[512,768]{1,0:T(8,128)(2,1)} %slice.393), channel_id=1, source_target_pairs={{0,1},{1,0},{2,3},{3,2},{4,5},{5,4},{6,7},{7,6},{8,9},{9,8},{10,11... | collective-permute-start | bytes 2359304 | tf_op jit(solution)/shard_map/ppermute | solution.py:70
  349.3 35.3 %collective-permute-start.26 = (bf16[1,384,384]{2,1,0:T(8,128)(2,1)}, bf16[1,384,384]{2,1,0:T(8,128)(2,1)}, u32[]{:S(2)}, u32[]{:S(2)}) collective-permute-start(bf16[1,384,384]{2,1,0:T(8,128)(2,1)} %get-tuple-element.181), channel_id=1, source_target_pairs={{0,8},{8,16},{16,24},{24,0},{1,9},{9,17},{17,25},{25,1},{2,10},{10... | collective-permute-start | bytes 884744 | tf_op jit(solution)/shard_map/ppermute | solution.py:75
  349.3 36.4 %collective-permute-start.27 = (bf16[1,384,384]{2,1,0:T(8,128)(2,1)}, bf16[1,384,384]{2,1,0:T(8,128)(2,1)}, u32[]{:S(2)}, u32[]{:S(2)}) collective-permute-start(bf16[1,384,384]{2,1,0:T(8,128)(2,1)} %get-tuple-element.180), channel_id=1, source_target_pairs={{0,16},{8,24},{16,0},{24,8},{1,17},{9,25},{17,1},{25,9},{2,18},{10... | collective-permute-start | bytes 884744 | tf_op jit(solution)/shard_map/ppermute | solution.py:75
  351.2 35.3 %collective-permute-start.28 = (bf16[1,384,384]{2,1,0:T(8,128)(2,1)}, bf16[1,384,384]{2,1,0:T(8,128)(2,1)}, u32[]{:S(2)}, u32[]{:S(2)}) collective-permute-start(bf16[1,384,384]{2,1,0:T(8,128)(2,1)} %get-tuple-element.179), channel_id=1, source_target_pairs={{0,24},{8,0},{16,8},{24,16},{1,25},{9,1},{17,9},{25,17},{2,26},{10... | collective-permute-start | bytes 884744 | tf_op jit(solution)/shard_map/ppermute | solution.py:75
  359.1 33.2 %collective-permute-start.29 = (bf16[4,96,384]{2,1,0:T(8,128)(2,1)S(1)}, bf16[4,96,384]{2,1,0:T(8,128)(2,1)S(1)}, u32[]{:S(2)}, u32[]{:S(2)}) collective-permute-start(bf16[4,96,384]{2,1,0:T(8,128)(2,1)S(1)} %slice.494), channel_id=1, source_target_pairs={{0,4},{4,0},{1,5},{5,1},{2,6},{6,2},{3,7},{7,3},{8,12},{12,8},{9,1... | collective-permute-start | bytes 884744 | tf_op jit(solution)/shard_map/ppermute | solution.py:75
  383.5 13.3 %collective-permute-start.30 = (bf16[4,144,384]{2,1,0:T(8,128)(2,1)S(1)}, bf16[4,144,384]{2,1,0:T(8,128)(2,1)}, u32[]{:S(2)}, u32[]{:S(2)}) collective-permute-start(bf16[4,144,384]{2,1,0:T(8,128)(2,1)S(1)} %slice.495), channel_id=1, source_target_pairs={{0,2},{2,0},{1,3},{3,1},{4,6},{6,4},{5,7},{7,5},{8,10},{10,8},{9,1... | collective-permute-start | bytes 1327112 | tf_op jit(solution)/shard_map/ppermute | solution.py:75
  384.5 31.1 %collective-permute-start.36 = (bf16[8,128,384]{2,1,0:T(8,128)(2,1)S(1)}, bf16[8,128,384]{2,1,0:T(8,128)(2,1)}, u32[]{:S(2)}, u32[]{:S(2)}) collective-permute-start(bf16[8,128,384]{2,1,0:T(8,128)(2,1)S(1)} %slice.417), channel_id=1, source_target_pairs={{0,4},{4,0},{1,5},{5,1},{2,6},{6,2},{3,7},{7,3},{8,12},{12,8},{9,1... | collective-permute-start | bytes 2359304 | tf_op jit(solution)/shard_map/ppermute | solution.py:75
  385.7 24.0 %collective-permute-start.34 = (bf16[8,96,384]{2,1,0:T(8,128)(2,1)}, bf16[8,96,384]{2,1,0:T(8,128)(2,1)S(1)}, u32[]{:S(2)}, u32[]{:S(2)}) collective-permute-start(bf16[8,96,384]{2,1,0:T(8,128)(2,1)} %slice.415), channel_id=1, source_target_pairs={{0,2},{2,0},{1,3},{3,1},{4,6},{6,4},{5,7},{7,5},{8,10},{10,8},{9,1... | collective-permute-start | bytes 1769480 | tf_op jit(solution)/shard_map/ppermute | solution.py:75
  386.5 57.1 %collective-permute-start.25 = (f32[512,768]{1,0:T(8,128)S(1)}, f32[512,768]{1,0:T(8,128)S(1)}, u32[]{:S(2)}, u32[]{:S(2)}) collective-permute-start(f32[512,768]{1,0:T(8,128)S(1)} %slice.405), channel_id=1, source_target_pairs={{0,1},{1,0},{2,3},{3,2},{4,5},{5,4},{6,7},{7,6},{8,9},{9,8},{10,11... | collective-permute-start | bytes 4718600 | tf_op jit(solution)/shard_map/ppermute | solution.py:70
  399.9 19.0 %collective-permute-start.31 = (bf16[240,384]{1,0:T(8,128)(2,1)S(1)}, bf16[240,384]{1,0:T(8,128)(2,1)S(1)}, u32[]{:S(2)}, u32[]{:S(2)}) collective-permute-start(bf16[240,384]{1,0:T(8,128)(2,1)S(1)} %get-tuple-element.184), channel_id=1, source_target_pairs={{0,8},{8,16},{16,24},{24,0},{1,9},{9,17},{17,25},{25,1},{2,10},{10... | collective-permute-start | bytes 552968 | tf_op jit(solution)/shard_map/ppermute | solution.py:75
  403.8 18.0 %collective-permute-start.32 = (bf16[240,384]{1,0:T(8,128)(2,1)S(1)}, bf16[240,384]{1,0:T(8,128)(2,1)S(1)}, u32[]{:S(2)}, u32[]{:S(2)}) collective-permute-start(bf16[240,384]{1,0:T(8,128)(2,1)S(1)} %get-tuple-element.185), channel_id=1, source_target_pairs={{0,16},{8,24},{16,0},{24,8},{1,17},{9,25},{17,1},{25,9},{2,18},{10... | collective-permute-start | bytes 552968 | tf_op jit(solution)/shard_map/ppermute | solution.py:75
  409.7 12.8 %collective-permute-start.33 = (bf16[240,384]{1,0:T(8,128)(2,1)S(1)}, bf16[240,384]{1,0:T(8,128)(2,1)S(1)}, u32[]{:S(2)}, u32[]{:S(2)}) collective-permute-start(bf16[240,384]{1,0:T(8,128)(2,1)S(1)} %get-tuple-element.186), channel_id=1, source_target_pairs={{0,24},{8,0},{16,8},{24,16},{1,25},{9,1},{17,9},{25,17},{2,26},{10... | collective-permute-start | bytes 552968 | tf_op jit(solution)/shard_map/ppermute | solution.py:75
  415.6 62.3 %collective-permute-start.49 = (f32[24,3072]{1,0:T(8,128)S(1)}, f32[24,3072]{1,0:T(8,128)S(1)}, u32[]{:S(2)}, u32[]{:S(2)}) collective-permute-start(f32[24,3072]{1,0:T(8,128)S(1)} %bitcast.210), channel_id=1, source_target_pairs={{0,1},{1,0},{2,3},{3,2},{4,5},{5,4},{6,7},{7,6},{8,9},{9,8},{10,11... | collective-permute-start | bytes 884744 | tf_op jit(solution)/shard_map/ppermute | solution.py:70
  419.0 9.5 %collective-permute-start.35 = (bf16[4,96,384]{2,1,0:T(8,128)(2,1)S(1)}, bf16[4,96,384]{2,1,0:T(8,128)(2,1)S(1)}, u32[]{:S(2)}, u32[]{:S(2)}) collective-permute-start(bf16[4,96,384]{2,1,0:T(8,128)(2,1)S(1)} %slice.504), channel_id=1, source_target_pairs={{0,4},{4,0},{1,5},{5,1},{2,6},{6,2},{3,7},{7,3},{8,12},{12,8},{9,1... | collective-permute-start | bytes 884744 | tf_op jit(solution)/shard_map/ppermute | solution.py:75
  421.7 11.1 %collective-permute-start.37 = (bf16[4,128,384]{2,1,0:T(8,128)(2,1)S(1)}, bf16[4,128,384]{2,1,0:T(8,128)(2,1)S(1)}, u32[]{:S(2)}, u32[]{:S(2)}) collective-permute-start(bf16[4,128,384]{2,1,0:T(8,128)(2,1)S(1)} %slice.505), channel_id=1, source_target_pairs={{0,2},{2,0},{1,3},{3,1},{4,6},{6,4},{5,7},{7,5},{8,10},{10,8},{9,1... | collective-permute-start | bytes 1179656 | tf_op jit(solution)/shard_map/ppermute | solution.py:75
  436.7 12.5 %collective-permute-start.38 = (bf16[1,224,384]{2,1,0:T(8,128)(2,1)S(1)}, bf16[1,224,384]{2,1,0:T(8,128)(2,1)S(1)}, u32[]{:S(2)}, u32[]{:S(2)}) collective-permute-start(bf16[1,224,384]{2,1,0:T(8,128)(2,1)S(1)} %get-tuple-element.188), channel_id=1, source_target_pairs={{0,8},{8,16},{16,24},{24,0},{1,9},{9,17},{17,25},{25,1},{2,10},{10... | collective-permute-start | bytes 516104 | tf_op jit(solution)/shard_map/ppermute | solution.py:75
  438.3 13.9 %collective-permute-start.39 = (bf16[1,224,384]{2,1,0:T(8,128)(2,1)S(1)}, bf16[1,224,384]{2,1,0:T(8,128)(2,1)S(1)}, u32[]{:S(2)}, u32[]{:S(2)}) collective-permute-start(bf16[1,224,384]{2,1,0:T(8,128)(2,1)S(1)} %get-tuple-element.189), channel_id=1, source_target_pairs={{0,16},{8,24},{16,0},{24,8},{1,17},{9,25},{17,1},{25,9},{2,18},{10... | collective-permute-start | bytes 516104 | tf_op jit(solution)/shard_map/ppermute | solution.py:75
  441.6 10.5 %collective-permute-start.40 = (bf16[1,224,384]{2,1,0:T(8,128)(2,1)S(1)}, bf16[1,224,384]{2,1,0:T(8,128)(2,1)}, u32[]{:S(2)}, u32[]{:S(2)}) collective-permute-start(bf16[1,224,384]{2,1,0:T(8,128)(2,1)S(1)} %get-tuple-element.187), channel_id=1, source_target_pairs={{0,24},{8,0},{16,8},{24,16},{1,25},{9,1},{17,9},{25,17},{2,26},{10... | collective-permute-start | bytes 516104 | tf_op jit(solution)/shard_map/ppermute | solution.py:75
  455.8 22.3 %collective-permute-start.50 = (f32[96,768]{1,0:T(8,128)S(1)}, f32[96,768]{1,0:T(8,128)S(1)}, u32[]{:S(2)}, u32[]{:S(2)}) collective-permute-start(f32[96,768]{1,0:T(8,128)S(1)} %get-tuple-element.190), channel_id=1, source_target_pairs={{0,1},{1,0},{2,3},{3,2},{4,5},{5,4},{6,7},{7,6},{8,9},{9,8},{10,11... | collective-permute-start | bytes 884744 | tf_op jit(solution)/shard_map/ppermute | solution.py:70
  459.7 3.8 collective-permute-start.42
  461.1 3.8 collective-permute-start.43
  462.4 4.7 collective-permute-start.44
  467.8 8.8 %collective-permute-start.45 = (f32[8,128]{1,0:T(8,128)S(1)}, f32[8,128]{1,0:T(8,128)S(1)}, u32[]{:S(2)}, u32[]{:S(2)}) collective-permute-start(f32[8,128]{1,0:T(8,128)S(1)} %add_add_fusion.3), channel_id=1, source_target_pairs={{0,8},{8,16},{16,24},{24,0},{1,9},{9,17},{17,25},{25,1},{2,10},{10... | collective-permute-start | bytes 12296 | tf_op jit(solution)/shard_map/ppermute | solution.py:75
  471.4 5.2 %collective-permute-start.46 = (f32[8,128]{1,0:T(8,128)S(1)}, f32[8,128]{1,0:T(8,128)S(1)}, u32[]{:S(2)}, u32[]{:S(2)}) collective-permute-start(f32[8,128]{1,0:T(8,128)S(1)} %add_add_fusion.3), channel_id=1, source_target_pairs={{0,16},{8,24},{16,0},{24,8},{1,17},{9,25},{17,1},{25,9},{2,18},{10... | collective-permute-start | bytes 12296 | tf_op jit(solution)/shard_map/ppermute | solution.py:75
  471.5 5.1 %collective-permute-start.47 = (f32[8,128]{1,0:T(8,128)S(1)}, f32[8,128]{1,0:T(8,128)S(1)}, u32[]{:S(2)}, u32[]{:S(2)}) collective-permute-start(f32[8,128]{1,0:T(8,128)S(1)} %add_add_fusion.3), channel_id=1, source_target_pairs={{0,24},{8,0},{16,8},{24,16},{1,25},{9,1},{17,9},{25,17},{2,26},{10... | collective-permute-start | bytes 12296 | tf_op jit(solution)/shard_map/ppermute | solution.py:75
  (54 other events, 232.0 us)
Sparse Core Ops, SparseCore 0:
  12.1 173.5 all-gather.1
  242.1 177.9 reduce-scatter.1
